TPU v7x, 128 devices: a whole 4x4x4 slice. The times are simulated.
128 devices in a mesh: dp: 16 (over y, z), expert: 8 (over x, core).
Axes of the slice: x: 4, y: 4, z: 4, core: 2. Of those that a mesh axis runs over, the one named last changes fastest.
Arguments:
- tokens: bfloat16 [32768, 1536], P(('dp', 'expert')), may hold values from -6 to 6
- d_out: bfloat16 [32768, 1536], P(('dp', 'expert')), may hold values from -6 to 6
- gain_in: bfloat16 [1536], P('dp'), may hold values from 0.099609375 to 1.8984375
- w_query: bfloat16 [1536, 1536], P('dp'), may hold values from -0.15625 to 0.15625
- key_projection_weight: bfloat16 [1536, 256], P('dp'), may hold values from -0.15625 to 0.15625
- value_projection_weight: bfloat16 [1536, 256], P('dp'), may hold values from -0.15625 to 0.15625
- w_out: bfloat16 [1536, 1536], P('dp'), may hold values from -3.5 to 3.5
- gain_mid: bfloat16 [1536], P('dp'), may hold values from 0.099609375 to 1.8984375
- w_router: bfloat16 [1536, 8], P('dp'), may hold values from -0.078125 to 0.078125
- w_gate: bfloat16 [8, 1536, 768], P('expert'), may hold values from -0.15625 to 0.15625
- w_up: bfloat16 [8, 1536, 768], P('expert'), may hold values from -0.15625 to 0.15625
- w_down: bfloat16 [8, 768, 1536], P('expert'), may hold values from -0.4375 to 0.4375
- routes: int32 [32768, 4], P(('dp', 'expert')), may hold values from 0 to 7, all different within a row; in each aligned block of 256 rows (0 to 255, 256 to 511, ...) at most 144 rows name the same one
- segments: int32 [16, 2048], P('dp'), may hold values from 0 to 3, never falling along the last dimension, each value on 1 to 1794 neighbouring positions
Outputs:
- mixed: bfloat16 [32768, 1536], P(('dp', 'expert'))
- grad_tokens: float32 [32768, 1536], P(('dp', 'expert'))
- grad_gain_in: float32 [1536], P('dp')
- grad_w_query: float32 [1536, 1536], P('dp')
- grad_w_key: float32 [1536, 256], P('dp')
- grad_w_value: float32 [1536, 256], P('dp')
- grad_w_out: float32 [1536, 1536], P('dp')
- grad_gain_mid: float32 [1536], P('dp')
- grad_w_router: float32 [1536, 8], P('dp')
- grad_w_gate: float32 [8, 1536, 768], P('expert')
- grad_w_up: float32 [8, 1536, 768], P('expert')
- grad_w_down: float32 [8, 768, 1536], P('expert')
Inputs may be any that keep to these rules, and one draw needn't show every extreme that they name: `routes`: each row names 4 different experts. The 256 rows of one device name no expert more than 144 times, and on some devices one expert exactly 144 times. `segments`: each row numbers its 4 documents in order without falling, every number used; one document of each row has exactly 1794 tokens.
All inputs are finite; a program needn't handle non-finite values.
Results may differ from a plain program's by a relative error of at most 0.025.
Values may be sent and summed in bfloat16 or wider, within the bound.
A program may use at most 256 MiB of HBM per device.

v0:
```python
import math

import jax
import jax.numpy as jnp
from jax import lax
from jax.sharding import PartitionSpec as P

QUERY_HEADS = 12
KEY_VALUE_HEADS = 2
HEAD_SIZE = 128
TOPK = 4
EXPERTS = 8
DOCS = 4


EPSILON = 1e-06
ROPE_BASE = 1000000.0
MASK_FILL = -1e30


def sent_together(arrays, axis, dim, along):
    columns = [a.reshape(*a.shape[:along], -1) for a in arrays]
    both = jnp.concatenate(columns, axis=along)
    whole, at, gathered = (lax.all_gather(both, axis, axis=dim, tiled=True), 0, [])
    for a, column in zip(arrays, columns):
        share = whole[..., at : at + column.shape[along]]
        gathered.append(share.reshape(*share.shape[:along], *a.shape[along:]))
        at += column.shape[along]
    return tuple(gathered)


def sent_together_2(arrays, axis, dim, along):
    both = jnp.concatenate(arrays, axis=along)
    whole, at, gathered = (lax.all_gather(both, axis, axis=dim, tiled=True), 0, [])
    for a in arrays:
        gathered.append(lax.slice_in_dim(whole, at, at + a.shape[along], axis=along))
        at += a.shape[along]
    return tuple(gathered)


def in_one_piece(arrays, axis, dim, along):
    ends, at = ([], 0)
    for a in arrays[:-1]:
        at += a.shape[along]
        ends.append(at)
    both = jnp.concatenate(arrays, axis=along)
    return tuple(
        jnp.split(lax.psum_scatter(both, axis, scatter_dimension=dim, tiled=True), ends, axis=along)
    )


def sent_together_3(arrays, axis, dim, along):
    widths = [math.prod(a.shape[along:]) for a in arrays]
    both = jnp.concatenate(
        [a.reshape(*a.shape[:along], w) for a, w in zip(arrays, widths)], axis=along
    )
    whole = lax.psum_scatter(both, axis, scatter_dimension=dim, tiled=True)
    parts = jnp.split(whole, [sum(widths[:k]) for k in range(1, len(widths))], axis=along)
    return tuple((b.reshape(*whole.shape[:along], *a.shape[along:]) for a, b in zip(arrays, parts)))


def together(arrays, axis):
    ends = [0]
    for a in arrays:
        ends.append(ends[-1] + a.size)
    subtotal = lax.psum(jnp.concatenate([a.ravel() for a in arrays]), axis)
    return tuple((subtotal[b:e].reshape(a.shape) for a, b, e in zip(arrays, ends, ends[1:])))


def rms_scale(value_rows, gain):
    inverse = lax.rsqrt(jnp.mean(value_rows * value_rows, axis=-1, keepdims=True) + EPSILON)
    return value_rows * inverse * gain


def doc_positions(seg_row):
    labels = jnp.arange(DOCS, dtype=jnp.int32)
    member = (seg_row[:, None] == labels[None, :]).astype(jnp.int32)
    counts = jnp.sum(member, axis=0)
    starts = jnp.cumsum(counts) - counts
    leading = jnp.sum(member * starts[None, :], axis=1)
    return jnp.arange(seg_row.shape[0], dtype=jnp.int32) - leading


def angles_for(positions):
    half_width = HEAD_SIZE // 2
    freqs = ROPE_BASE ** (-2.0 * jnp.arange(half_width, dtype=jnp.float32) / HEAD_SIZE)
    return positions.astype(jnp.float32)[:, None] * freqs[None, :]


def apply_rotary(heads, rotary_angles):
    half_width = heads.shape[-1] // 2
    cosine = jnp.cos(rotary_angles)[:, None, :]
    sine_part = jnp.sin(rotary_angles)[:, None, :]
    leading = heads[..., :half_width]
    trailing = heads[..., half_width:]
    return jnp.concatenate(
        [leading * cosine - trailing * sine_part, trailing * cosine + leading * sine_part], axis=-1
    )


def glu_act(gate_pre, up_pre):
    return jax.nn.gelu(gate_pre, approximate=True) * up_pre


def on_device(
    tokens,
    d_out,
    gain_in,
    w_query,
    key_projection_weight,
    value_projection_weight,
    w_out,
    gain_mid,
    w_router,
    w_gate,
    w_up,
    w_down,
    routes,
    segments,
):
    single_float_type = jnp.float32
    brain_half_type = jnp.bfloat16
    tokens_per_device = tokens.shape[0]
    width = tokens.shape[1]
    sequence_length = segments.shape[1]
    query_groups = QUERY_HEADS // KEY_VALUE_HEADS
    scaling = HEAD_SIZE ** (-0.5)
    part_index = lax.axis_index("expert")
    part_count = lax.axis_size("expert")
    exp_local = w_gate.shape[0]
    capacity = tokens_per_device * 9 // 16
    seg_row = segments[0]
    offset = part_index * tokens_per_device
    angles_all = angles_for(doc_positions(seg_row))
    local_angles = lax.dynamic_slice_in_dim(angles_all, offset, tokens_per_device, 0)
    my_seg = lax.dynamic_slice_in_dim(seg_row, offset, tokens_per_device, 0)
    my_rows = offset + jnp.arange(tokens_per_device, dtype=jnp.int32)
    key_places = jnp.arange(sequence_length, dtype=jnp.int32)
    allowed = (my_seg[:, None] == seg_row[None, :]) & (my_rows[:, None] >= key_places[None, :])
    gathered = sent_together(
        (
            gain_in,
            w_query,
            key_projection_weight,
            value_projection_weight,
            w_out,
            gain_mid,
            w_router,
        ),
        "dp",
        0,
        1,
    )
    full_gin, full_wq, complete_key_weight, full_wv, full_wo, full_gmid, full_wr = gathered
    inputs = tokens.astype(single_float_type)
    normed = rms_scale(inputs, full_gin.astype(single_float_type))
    normalized_block = normed.astype(brain_half_type)
    query_linear = jnp.dot(
        normalized_block, full_wq, preferred_element_type=single_float_type
    ).reshape(tokens_per_device, QUERY_HEADS, HEAD_SIZE)
    key_linear = jnp.dot(
        normalized_block, complete_key_weight, preferred_element_type=single_float_type
    ).reshape(tokens_per_device, KEY_VALUE_HEADS, HEAD_SIZE)
    value_b = jnp.dot(normalized_block, full_wv, preferred_element_type=single_float_type).astype(
        brain_half_type
    )
    query_block = (
        apply_rotary(query_linear, local_angles)
        .astype(brain_half_type)
        .reshape(tokens_per_device, KEY_VALUE_HEADS, query_groups, HEAD_SIZE)
    )
    key_block = (
        apply_rotary(key_linear, local_angles)
        .astype(brain_half_type)
        .reshape(tokens_per_device, KEY_VALUE_HEADS * HEAD_SIZE)
    )
    gathered_keys, gathered_values = sent_together_2((key_block, value_b), "expert", 0, 1)
    gathered_keys = gathered_keys.reshape(sequence_length, KEY_VALUE_HEADS, HEAD_SIZE)
    gathered_values = gathered_values.reshape(sequence_length, KEY_VALUE_HEADS, HEAD_SIZE)

    def scores_for(key_value_head):
        raw = (
            jnp.einsum(
                "tgd,sd->gts",
                query_block[:, key_value_head],
                gathered_keys[:, key_value_head],
                preferred_element_type=single_float_type,
            )
            * scaling
        )
        return jnp.where(allowed[None], raw, MASK_FILL)

    contexts = []
    log_sums = []
    for key_value_head in range(KEY_VALUE_HEADS):
        scores = scores_for(key_value_head)
        row_max = jnp.max(scores, axis=-1, keepdims=True)
        shifted = jnp.exp(scores - row_max)
        row_sum = jnp.sum(shifted, axis=-1, keepdims=True)
        probs_b = (shifted / row_sum).astype(brain_half_type)
        contexts.append(
            jnp.einsum(
                "gts,sd->tgd",
                probs_b,
                gathered_values[:, key_value_head],
                preferred_element_type=single_float_type,
            )
        )
        log_sums.append(row_max + jnp.log(row_sum))
    context_b = (
        jnp.stack(contexts, axis=1)
        .reshape(tokens_per_device, QUERY_HEADS * HEAD_SIZE)
        .astype(brain_half_type)
    )
    middle = inputs + jnp.dot(context_b, full_wo, preferred_element_type=single_float_type)
    normed_mid = rms_scale(middle, full_gmid.astype(single_float_type))
    normed_mid_b = normed_mid.astype(brain_half_type)
    logits = jnp.dot(normed_mid_b, full_wr, preferred_element_type=single_float_type)
    chosen = jnp.take_along_axis(logits, routes, axis=1)
    gates = jax.nn.softmax(chosen, axis=-1)
    pair_count = tokens_per_device * TOPK
    flat_expert = routes.reshape(pair_count)
    member = (flat_expert[:, None] == jnp.arange(EXPERTS, dtype=jnp.int32)[None, :]).astype(
        jnp.int32
    )
    ranks = jnp.sum((jnp.cumsum(member, axis=0) - member) * member, axis=1)
    target = flat_expert // exp_local
    within = flat_expert % exp_local
    slot_index = (within * part_count + target) * capacity + ranks
    slot_total = exp_local * part_count * capacity
    source_pair = (
        jnp.zeros((slot_total,), jnp.int32)
        .at[slot_index]
        .set(jnp.arange(pair_count, dtype=jnp.int32))
    )
    occupied = (
        jnp.zeros((slot_total,), brain_half_type)
        .at[slot_index]
        .set(jnp.ones((pair_count,), brain_half_type))
    )
    source_token = source_pair // TOPK
    outgoing = (normed_mid_b[source_token] * occupied[:, None]).reshape(
        exp_local, part_count, capacity, width
    )
    arrived = lax.all_to_all(outgoing, "expert", split_axis=1, concat_axis=1, tiled=True).reshape(
        exp_local, part_count * capacity, width
    )
    gate_pre = jnp.einsum("erd,edf->erf", arrived, w_gate, preferred_element_type=single_float_type)
    up_pre = jnp.einsum("erd,edf->erf", arrived, w_up, preferred_element_type=single_float_type)
    hidden_b = glu_act(gate_pre, up_pre).astype(brain_half_type)
    expert_out = jnp.einsum(
        "erf,efd->erd", hidden_b, w_down, preferred_element_type=single_float_type
    ).astype(brain_half_type)
    expert_out = expert_out.reshape(exp_local, part_count, capacity, width)
    returned = lax.all_to_all(
        expert_out, "expert", split_axis=1, concat_axis=1, tiled=True
    ).reshape(slot_total, width)
    picked = returned[slot_index].reshape(tokens_per_device, TOPK, width).astype(single_float_type)
    combined = jnp.einsum("tk,tkd->td", gates, picked)
    mixed = (middle + combined).astype(brain_half_type)
    upstream = d_out.astype(single_float_type)
    grad_gates = jnp.einsum("td,tkd->tk", upstream, picked)
    pair_grads = (
        (gates[:, :, None] * upstream[:, None, :])
        .astype(brain_half_type)
        .reshape(pair_count, width)
    )
    outgoing_grads = (pair_grads[source_pair] * occupied[:, None]).reshape(
        exp_local, part_count, capacity, width
    )
    grad_arrived = lax.all_to_all(
        outgoing_grads, "expert", split_axis=1, concat_axis=1, tiled=True
    ).reshape(exp_local, part_count * capacity, width)
    grad_hidden = jnp.einsum(
        "erd,efd->erf", grad_arrived, w_down, preferred_element_type=single_float_type
    )
    grad_wdown = jnp.einsum(
        "erf,erd->efd", hidden_b, grad_arrived, preferred_element_type=single_float_type
    )
    _, pull_act = jax.vjp(glu_act, gate_pre, up_pre)
    grad_gate_pre, grad_up_pre = pull_act(grad_hidden)
    grad_gate_b = grad_gate_pre.astype(brain_half_type)
    grad_up_b = grad_up_pre.astype(brain_half_type)
    grad_wgate = jnp.einsum(
        "erd,erf->edf", arrived, grad_gate_b, preferred_element_type=single_float_type
    )
    grad_wup = jnp.einsum(
        "erd,erf->edf", arrived, grad_up_b, preferred_element_type=single_float_type
    )
    grad_rows = jnp.einsum(
        "erf,edf->erd", grad_gate_b, w_gate, preferred_element_type=single_float_type
    )
    grad_rows = grad_rows + jnp.einsum(
        "erf,edf->erd", grad_up_b, w_up, preferred_element_type=single_float_type
    )
    grad_rows = grad_rows.astype(brain_half_type).reshape(exp_local, part_count, capacity, width)
    grad_back = lax.all_to_all(
        grad_rows, "expert", split_axis=1, concat_axis=1, tiled=True
    ).reshape(slot_total, width)
    grad_normed_mid = jnp.sum(
        grad_back[slot_index].reshape(tokens_per_device, TOPK, width).astype(single_float_type),
        axis=1,
    )
    again = sent_together(
        (
            gain_in,
            w_query,
            key_projection_weight,
            value_projection_weight,
            w_out,
            gain_mid,
            w_router,
        ),
        "dp",
        0,
        1,
    )
    back_gin, back_wq, back_wk, back_wv, back_wo, back_gmid, back_wr = again
    grad_chosen = gates * (grad_gates - jnp.sum(gates * grad_gates, axis=-1, keepdims=True))
    expert_ids = jnp.arange(EXPERTS, dtype=jnp.int32)
    grad_logits = jnp.sum(
        grad_chosen[:, :, None]
        * (routes[:, :, None] == expert_ids[None, None, :]).astype(single_float_type),
        axis=1,
    ).astype(brain_half_type)
    grad_wr = jnp.einsum(
        "td,te->de", normed_mid_b, grad_logits, preferred_element_type=single_float_type
    )
    grad_normed_mid = grad_normed_mid + jnp.einsum(
        "te,de->td", grad_logits, back_wr, preferred_element_type=single_float_type
    )
    _, pull_mid = jax.vjp(rms_scale, middle, back_gmid.astype(single_float_type))
    grad_middle_norm, grad_gmid = pull_mid(grad_normed_mid)
    grad_middle = upstream + grad_middle_norm
    grad_attn_b = grad_middle.astype(brain_half_type)
    grad_wo = jnp.einsum(
        "tc,td->cd", context_b, grad_attn_b, preferred_element_type=single_float_type
    )
    context_gradient_block = jnp.einsum(
        "td,cd->tc", grad_attn_b, back_wo, preferred_element_type=single_float_type
    ).astype(brain_half_type)
    context_gradient_block = context_gradient_block.reshape(
        tokens_per_device, KEY_VALUE_HEADS, query_groups, HEAD_SIZE
    )
    query_grads = []
    key_gradient_parts = []
    value_gradient_parts = []
    for key_value_head in range(KEY_VALUE_HEADS):
        scores = scores_for(key_value_head)
        probs_full = jnp.exp(scores - log_sums[key_value_head])
        probs_b = probs_full.astype(brain_half_type)
        grad_ctx_head = context_gradient_block[:, key_value_head]
        grad_probs = jnp.einsum(
            "tgd,sd->gts",
            grad_ctx_head,
            gathered_values[:, key_value_head],
            preferred_element_type=single_float_type,
        )
        value_gradient_parts.append(
            jnp.einsum(
                "gts,tgd->sd", probs_b, grad_ctx_head, preferred_element_type=single_float_type
            )
        )
        inner = jnp.sum(probs_full * grad_probs, axis=-1, keepdims=True)
        grad_scores = (probs_full * (grad_probs - inner)).astype(brain_half_type)
        query_grads.append(
            jnp.einsum(
                "gts,sd->tgd",
                grad_scores,
                gathered_keys[:, key_value_head],
                preferred_element_type=single_float_type,
            )
            * scaling
        )
        key_gradient_parts.append(
            jnp.einsum(
                "gts,tgd->sd",
                grad_scores,
                query_block[:, key_value_head],
                preferred_element_type=single_float_type,
            )
            * scaling
        )
    grad_query = jnp.stack(query_grads, axis=1).reshape(tokens_per_device, QUERY_HEADS, HEAD_SIZE)
    gathered_key_gradient = jnp.stack(key_gradient_parts, axis=1).reshape(
        sequence_length, KEY_VALUE_HEADS * HEAD_SIZE
    )
    gathered_value_gradient = jnp.stack(value_gradient_parts, axis=1).reshape(
        sequence_length, KEY_VALUE_HEADS * HEAD_SIZE
    )
    local_keys, own_values = tuple(
        (
            part.astype(jnp.float32)
            for part in in_one_piece(
                (
                    gathered_key_gradient.astype(jnp.bfloat16),
                    gathered_value_gradient.astype(jnp.bfloat16),
                ),
                "expert",
                0,
                1,
            )
        )
    )
    _, pull_query = jax.vjp(lambda heads: apply_rotary(heads, local_angles), query_linear)
    (grad_qlin,) = pull_query(grad_query)
    _, fetch_key = jax.vjp(lambda heads: apply_rotary(heads, local_angles), key_linear)
    (key_linear_gradient,) = fetch_key(
        local_keys.reshape(tokens_per_device, KEY_VALUE_HEADS, HEAD_SIZE)
    )
    grad_qlin_b = grad_qlin.reshape(tokens_per_device, QUERY_HEADS * HEAD_SIZE).astype(
        brain_half_type
    )
    key_linear_gradient_block = key_linear_gradient.reshape(
        tokens_per_device, KEY_VALUE_HEADS * HEAD_SIZE
    ).astype(brain_half_type)
    grad_vlin_b = own_values.astype(brain_half_type)
    grad_wq = jnp.einsum(
        "td,tc->dc", normalized_block, grad_qlin_b, preferred_element_type=single_float_type
    )
    grad_wk = jnp.einsum(
        "td,tc->dc",
        normalized_block,
        key_linear_gradient_block,
        preferred_element_type=single_float_type,
    )
    grad_wv = jnp.einsum(
        "td,tc->dc", normalized_block, grad_vlin_b, preferred_element_type=single_float_type
    )
    grad_normed = jnp.einsum(
        "tc,dc->td", grad_qlin_b, back_wq, preferred_element_type=single_float_type
    )
    grad_normed = grad_normed + jnp.einsum(
        "tc,dc->td", key_linear_gradient_block, back_wk, preferred_element_type=single_float_type
    )
    grad_normed = grad_normed + jnp.einsum(
        "tc,dc->td", grad_vlin_b, back_wv, preferred_element_type=single_float_type
    )
    _, pull_in = jax.vjp(rms_scale, inputs, back_gin.astype(single_float_type))
    grad_inputs_norm, grad_gin = pull_in(grad_normed)
    grad_tokens = grad_middle + grad_inputs_norm
    summed = tuple(
        (
            part.astype(jnp.float32)
            for part in sent_together_3(
                (
                    grad_gin.astype(jnp.bfloat16),
                    grad_wq.astype(jnp.bfloat16),
                    grad_wk.astype(jnp.bfloat16),
                    grad_wv.astype(jnp.bfloat16),
                    grad_wo.astype(jnp.bfloat16),
                    grad_gmid.astype(jnp.bfloat16),
                    grad_wr.astype(jnp.bfloat16),
                ),
                "dp",
                0,
                1,
            )
        )
    )
    summed = tuple(
        (
            part.astype(jnp.float32)
            for part in together(
                (
                    summed[0].astype(jnp.bfloat16),
                    summed[1].astype(jnp.bfloat16),
                    summed[2].astype(jnp.bfloat16),
                    summed[3].astype(jnp.bfloat16),
                    summed[4].astype(jnp.bfloat16),
                    summed[5].astype(jnp.bfloat16),
                    summed[6].astype(jnp.bfloat16),
                ),
                "expert",
            )
        )
    )
    expert_sums = (
        lax.psum(grad_wgate.astype(jnp.bfloat16), "dp").astype(jnp.float32),
        lax.psum(grad_wup.astype(jnp.bfloat16), "dp").astype(jnp.float32),
        lax.psum(grad_wdown.astype(jnp.bfloat16), "dp").astype(jnp.float32),
    )
    return (
        mixed,
        grad_tokens,
        summed[0],
        summed[1],
        summed[2],
        summed[3],
        summed[4],
        summed[5],
        summed[6],
        expert_sums[0],
        expert_sums[1],
        expert_sums[2],
    )


def solution(mesh):
    placed = (
        P(("dp", "expert"), None),
        P(("dp", "expert"), None),
        P("dp"),
        P("dp", None),
        P("dp", None),
        P("dp", None),
        P("dp", None),
        P("dp"),
        P("dp", None),
        P("expert", None, None),
        P("expert", None, None),
        P("expert", None, None),
        P(("dp", "expert"), None),
        P("dp", None),
    )
    return jax.shard_map(
        on_device,
        mesh=mesh,
        in_specs=placed,
        out_specs=(
            P(("dp", "expert"), None),
            P(("dp", "expert"), None),
            P("dp"),
            P("dp", None),
            P("dp", None),
            P("dp", None),
            P("dp", None),
            P("dp"),
            P("dp", None),
            P("expert", None, None),
            P("expert", None, None),
            P("expert", None, None),
        ),
        check_vma=False,
    )
```

profile of v0, /device:TPU:1, one launch (start us, length us, event | category | flops | bytes accessed | tf_op | source)
XLA Modules:
  0.0 883.8 jit_solution(5989187266640511610)
XLA Ops:
  16.4 83.8 %all-gather.3.cloned.1.call-done = bf16[1536,3594]{1,0:T(8,128)(2,1)} async-done(((bf16[96,3594]{1,0:T(8,128)(2,1)}), bf16[1536,3594]{1,0:T(8,128)(2,1)}) %all-gather.3.cloned.1.call-update) | async-done | bytes 11040784 | tf_op jit(solution)/shard_map/all_gather | solution.py:24
  121.4 7.8 scatter_custom_fusion.1
  133.1 6.6 fusion.25
  148.8 6.1 fusion.141
  157.1 10.8 %fusion.6 = f32[6,256]{1,0:T(8,128)S(1)} fusion(f32[6,256,2048]{1,2,0:T(8,128)} %get-tuple-element.96, f32[6,256]{1,0:T(8,128)S(1)} %get-tuple-element.95), kind=kLoop, calls=%fused_computation.25 | loop fusion | flops 6289920 | bytes 12595200 | tf_op jit(solution)/shard_map/reduce_sum | solution.py:199
  167.9 7.0 fusion.92
  179.3 4.9 multiply_reduce_fusion.2
  185.6 5.7 gather_fusion
  193.7 47.2 %all_to_all.20 = bf16[1,8,144,1536]{3,2,0,1:T(8,128)(2,1)S(1)} all-to-all(bf16[1,8,144,1536]{3,2,0,1:T(8,128)(2,1)S(1)} %broadcast_multiply_fusion.1), channel_id=1, replica_groups=mesh['dp'=16,'expert'=8] {'expert'}, dimensions={1} | all-to-all | bytes 7077888 | tf_op jit(solution)/shard_map/all_to_all | solution.py:245
  243.8 5.2 multiply_convert_fusion.2
  249.0 4.3 convolution_convert_fusion.2
  253.4 5.6 all-to-all-start.1
  260.9 4.7 mul.495
  265.6 7.7 mul.496
  275.3 6.6 gather_fusion.4
  282.4 18.5 %all-to-all-done.1 = bf16[1,8,144,1536]{3,2,0,1:T(8,128)(2,1)} async-done(((bf16[1,8,144,1536]{3,2,0,1:T(8,128)(2,1)}), bf16[1,8,144,1536]{3,2,0,1:T(8,128)(2,1)}, u32[]{:S(2)}, u32[]{:S(2)}) %all-to-all-start.1) | async-done | bytes 3538976 | tf_op jit(solution)/shard_map/all_to_all | solution.py:255
  300.8 9.7 %gather_fusion.1 = bf16[1024,1536]{1,0:T(8,128)(2,1)} fusion(bf16[1152,1536]{1,0:T(8,128)(2,1)} %bitcast.44, s32[1024]{0:T(1024)S(1)} %copy-done.50), kind=kCustom, calls=%fused_computation.1 | custom fusion | bytes 6295552 | tf_op jit(solution)/shard_map/gather | solution.py:258
  310.5 6.2 reshape.552
  316.8 5.4 fusion.86
  323.1 4.9 multiply_convert_fusion
  328.1 11.0 %gather_fusion.2 = bf16[1152,1536]{1,0:T(8,128)(2,1)} fusion(bf16[1024,1536]{1,0:T(8,128)(2,1)} %multiply_convert_fusion, s32[2048]{0:T(1024)S(1)} %copy-done.58), kind=kCustom, calls=%fused_computation.2 | custom fusion | bytes 7082496 | tf_op jit(solution)/shard_map/gather | solution.py:268
  341.4 46.2 %all_to_all.21 = bf16[1,8,144,1536]{3,2,0,1:T(8,128)(2,1)S(1)} all-to-all(bf16[1,8,144,1536]{3,2,0,1:T(8,128)(2,1)S(1)} %broadcast_multiply_fusion), channel_id=1, replica_groups=mesh['dp'=16,'expert'=8] {'expert'}, dimensions={1} | all-to-all | bytes 7077888 | tf_op jit(solution)/shard_map/all_to_all | solution.py:271
  387.7 5.2 multiply_convert_fusion.1
  396.0 4.5 fusion.10
  400.5 5.4 all-to-all-start.3
  406.2 4.8 fusion.142
  411.0 36.8 %all-to-all-done.3 = bf16[1,8,144,1536]{3,2,0,1:T(8,128)(2,1)} async-done(((bf16[1,8,144,1536]{3,2,0,1:T(8,128)(2,1)}), bf16[1,8,144,1536]{3,2,0,1:T(8,128)(2,1)}, u32[]{:S(2)}, u32[]{:S(2)}) %all-to-all-start.3) | async-done | bytes 3538976 | tf_op jit(solution)/shard_map/all_to_all | solution.py:297
  447.8 10.1 %gather_fusion.3 = bf16[1024,1536]{1,0:T(8,128)(2,1)} fusion(bf16[1152,1536]{1,0:T(8,128)(2,1)} %bitcast.51, s32[1024]{0:T(1024)S(1)} %copy-done.51), kind=kCustom, calls=%fused_computation.3 | custom fusion | bytes 6295552 | tf_op jit(solution)/shard_map/gather | solution.py:301
  457.9 6.6 reshape.569
  464.5 7.8 reduce_sum.188
  477.3 4.4 fusion.39
  482.0 10.3 %fusion.3 = (f32[6,256]{1,0:T(8,128)S(1)}, f32[2048,256,6]{1,0,2:T(8,128)}) fusion(f32[6,256,2048]{1,2,0:T(8,128)} %get-tuple-element.96, f32[6,256]{1,0:T(8,128)S(1)} %log_add_fusion.1, bf16[256,2,6,128]{0,3,2,1:T(8,128)(2,1)S(1)} %bitcast.289, bf16[2048,2,128]{0,2,1:T(8,128)(2,1)S(1)} %bitcast.304), kind=kOutput, calls=%fused_computation.14 | convolution fusion | flops 814742016 | bytes 26097664 | tf_op jit(solution)/shard_map/tgd,sd->gts/dot_general | solution.py:353
  492.4 7.0 fusion.68
  499.4 6.6 fusion
  508.3 9.1 %fusion.5 = bf16[6,256,2048]{1,2,0:T(8,128)(2,1)} fusion(f32[2048,256,6]{1,0,2:T(8,128)} %get-tuple-element.105, f32[6,256,2048]{1,2,0:T(8,128)S(1)} %bitcast.280, f32[6,256]{1,0:T(8,128)S(1)} %get-tuple-element.104, f32[6,256]{1,0:T(8,128)S(1)} %log_add_fusion.1), kind=kLoop, calls=%fused_computation.16 | loop fusion | flops 12582912 | bytes 31469568 | tf_op jit(solution)/shard_map/convert_element_type | solution.py:365
  517.4 5.1 fusion.75
  522.5 6.2 fusion.2
  533.3 7.4 fusion.36
  540.7 4.6 fusion.34
  545.3 4.6 fusion.35
  567.8 6.5 fusion.23
  582.6 58.2 %concatenate.36 = bf16[1536,3594]{0,1:T(8,128)(2,1)} concatenate(bf16[1536,1]{0,1:T(2,128)(2,1)S(1)} %convert_element_type.308, bf16[1536,1536]{0,1:T(8,128)(2,1)} %convolution_convert_fusion, bf16[1536,256]{0,1:T(8,128)(2,1)S(1)} %convolution_convert_fusion.7, bf16[1536,256]{0,1:T(8,128)(2,1)S(1)} %convolution_convert_fusion.6, bf16[1536,1536]{0,1:T(8,128)(2,1)} %convolution_convert_fusion.1, ...), dimensions={1} | concatenate | bytes 22081536 | tf_op jit(solution)/shard_map/concatenate | solution.py:54
  640.8 14.8 %copy.216 = bf16[1536,3594]{1,0:T(8,128)(2,1)} copy(bf16[1536,3594]{0,1:T(8,128)(2,1)} %concatenate.36) | data formatting | bytes 22081536
  655.9 42.3 %all-reduce.10.cloned.1.call-done = (bf16[1,1536,768]{2,1,0:T(8,128)(2,1)}, bf16[1,1536,768]{2,1,0:T(8,128)(2,1)}, bf16[1,768,1536]{2,1,0:T(8,128)(2,1)}) async-done(((bf16[1,1536,768]{2,1,0:T(8,128)(2,1)}, bf16[1,1536,768]{2,1,0:T(8,128)(2,1)}, bf16[1,768,1536]{2,1,0:T(8,128)(2,1)}), (bf16[1,1536,768]{2,1,0:T(8,128)(2,1)}, bf16[1,1536,768]{2,1,0:T(8,128)(2,1)}, ...) | async-done | bytes 7077904 | tf_op jit(solution)/shard_map/psum | solution.py:479
  698.2 4.4 convert_element_type.330
  707.9 85.4 %reduce-scatter.7.cloned.1.call-done = bf16[96,3594]{1,0:T(8,128)(2,1)} async-done(((bf16[1536,3594]{1,0:T(8,128)(2,1)}), bf16[96,3594]{1,0:T(8,128)(2,1)}) %reduce-scatter.7.cloned.1.call-update) | async-done | bytes 690064
  798.4 11.5 %concatenate.37 = bf16[345024]{0:T(1024)(128)(2,1)} concatenate(bf16[96]{0:T(256)(128)(2,1)S(1)} %bitcast.337, bf16[147456]{0:T(1024)(128)(2,1)S(1)} %reshape.561, bf16[24576]{0:T(1024)(128)(2,1)S(1)} %bitcast.326, bf16[24576]{0:T(1024)(128)(2,1)S(1)} %bitcast.327, bf16[147456]{0:T(1024)(128)(2,1)S(1)} %reshape.564, bf16[96]{0:T(256)(128)(2,1)S(1)} %bitcast.338, ...), dimensions={0} | concatenate | bytes 1380096 | tf_op jit(solution)/shard_map/concatenate | solution.py:66
  813.6 54.7 %all-reduce.8.cloned.1.call-done = bf16[345024]{0:T(1024)(128)(2,1)} async-done(((bf16[345024]{0:T(1024)(128)(2,1)}), bf16[345024]{0:T(1024)(128)(2,1)}) %all-reduce.8.cloned.1.call-update) | async-done | bytes 690064 | tf_op jit(solution)/shard_map/psum | solution.py:66
  (326 shorter events, 127.7 us)
Async XLA Ops:
  7.2 241.8 %copy-start = (bf16[1,768,1536]{2,1,0:T(8,128)(2,1)S(1)}, bf16[1,768,1536]{2,1,0:T(8,128)(2,1)}, u32[]{:S(2)}) copy-start(bf16[1,768,1536]{2,1,0:T(8,128)(2,1)} %param.25) | copy-start | bytes 7077892
  7.2 94.6 %copy-start.10 = (bf16[256,1536]{1,0:T(8,128)(2,1)S(1)}, bf16[256,1536]{1,0:T(8,128)(2,1)}, u32[]{:S(2)}) copy-start(bf16[256,1536]{1,0:T(8,128)(2,1)} %param.14) | copy-start | bytes 2359300
  7.2 93.0 %all-gather.3.cloned.1.call-start = ((), (), s32[]{:S(2)}) async-start(), calls=%async_computation.6 | async-start | bytes 12115968 | tf_op jit(solution)/shard_map/all_gather | solution.py:24
  12.2 134.4 %all-gather.5.cloned.1.call-start = ((), (), s32[]{:S(2)}) async-start(), calls=%async_computation.7 | async-start | bytes 2359296 | tf_op jit(solution)/shard_map/all_gather | solution.py:34
  16.0 88.0 %copy-start.65 = (f32[256]{0:T(256)}, f32[256]{0:T(256)S(1)}, u32[]{:S(2)}) copy-start(f32[256]{0:T(256)S(1)} %fusion.125) | copy-start | bytes 3076
  16.4 123.4 %copy-start.33 = (f32[256,64]{0,1:T(8,128)}, f32[256,64]{0,1:T(8,128)S(1)}, u32[]{:S(2)}) copy-start(f32[256,64]{0,1:T(8,128)S(1)} %get-tuple-element.91) | copy-start | bytes 196612
  16.4 123.4 %copy-start.35 = (f32[256,64]{0,1:T(8,128)}, f32[256,64]{0,1:T(8,128)S(1)}, u32[]{:S(2)}) copy-start(f32[256,64]{0,1:T(8,128)S(1)} %get-tuple-element.92) | copy-start | bytes 196612
  101.8 31.4 %copy-start.43 = (f32[1536]{0:T(1024)}, f32[1536]{0:T(1024)S(1)}, u32[]{:S(2)}) copy-start(f32[1536]{0:T(1024)S(1)} %get-tuple-element.49) | copy-start | bytes 18436
  101.8 82.5 %copy-start.41 = (f32[1536]{0:T(1024)}, f32[1536]{0:T(1024)S(1)}, u32[]{:S(2)}) copy-start(f32[1536]{0:T(1024)S(1)} %get-tuple-element.48) | copy-start | bytes 18436
  107.8 31.9 %copy-start.28 = (s32[256,4]{1,0:T(8,128)}, s32[256,4]{1,0:T(8,128)S(1)}, u32[]{:S(2)}) copy-start(s32[256,4]{1,0:T(8,128)S(1)} %copy.159) | copy-start | bytes 12292
  117.0 13.5 %copy-start.63 = (s32[1024,1]{0,1:T(1,128)}, s32[1024,1]{0,1:T(1,128)S(1)}, u32[]{:S(2)}) copy-start(s32[1024,1]{0,1:T(1,128)S(1)} %compare_select_fusion) | copy-start | bytes 12292
  146.5 8.4 copy-start.20
  148.4 28.1 %copy-start.23 = (bf16[2048,256]{0,1:T(8,128)(2,1)}, bf16[2048,256]{0,1:T(8,128)(2,1)S(1)}, u32[]{:S(2)}) copy-start(bf16[2048,256]{0,1:T(8,128)(2,1)S(1)} %get-tuple-element.63) | copy-start | bytes 3145732
  154.9 13.0 %copy-start.52 = (f32[6,256]{1,0:T(8,128)}, f32[6,256]{1,0:T(8,128)S(1)}, u32[]{:S(2)}) copy-start(f32[6,256]{1,0:T(8,128)S(1)} %get-tuple-element.95) | copy-start | bytes 18436
  157.1 19.4 %copy-start.4 = (f32[6,256,2048]{1,2,0:T(8,128)}, f32[6,256,2048]{1,2,0:T(8,128)S(1)}, u32[]{:S(2)}) copy-start(f32[6,256,2048]{1,2,0:T(8,128)S(1)} %get-tuple-element.94) | copy-start | bytes 37748740
  157.1 19.4 %copy-start.45 = (f32[6,256]{1,0:T(8,128)}, f32[6,256]{1,0:T(8,128)S(1)}, u32[]{:S(2)}) copy-start(f32[6,256]{1,0:T(8,128)S(1)} %get-tuple-element.93) | copy-start | bytes 18436
  167.9 7.0 copy-start.54
  184.2 7.1 copy-start.72
  185.6 88.3 %copy-start.2 = (bf16[256,1536]{1,0:T(8,128)(2,1)}, bf16[256,1536]{1,0:T(8,128)(2,1)S(1)}, u32[]{:S(2)}) copy-start(bf16[256,1536]{1,0:T(8,128)(2,1)S(1)} %multiply_convert_fusion.3) | copy-start | bytes 2359300
  193.7 47.2 %copy-start.74 = (bf16[1,1536,768]{2,1,0:T(8,128)(2,1)S(1)}, bf16[1,1536,768]{2,1,0:T(8,128)(2,1)}, u32[]{:S(2)}) copy-start(bf16[1,1536,768]{2,1,0:T(8,128)(2,1)} %param.23) | copy-start | bytes 7077892
  253.4 6.6 copy-start.29
  253.4 47.5 %all-to-all-start.1 = ((bf16[1,8,144,1536]{3,2,0,1:T(8,128)(2,1)}), bf16[1,8,144,1536]{3,2,0,1:T(8,128)(2,1)}, u32[]{:S(2)}, u32[]{:S(2)}) async-start(bf16[1,8,144,1536]{3,2,0,1:T(8,128)(2,1)} %bitcast.314), calls=%async_computation.1 | async-start | bytes 7077888 | tf_op jit(solution)/shard_map/all_to_all | solution.py:255
  265.6 7.7 copy-start.64
  275.3 6.7 copy-start.39
  275.3 25.5 %copy-start.50 = (s32[1024]{0:T(1024)S(1)}, s32[1024]{0:T(1024)}, u32[]{:S(2)}) copy-start(s32[1024]{0:T(1024)} %broadcast_clamp_fusion) | copy-start | bytes 12292
  282.2 18.7 %copy-start.67 = (f32[256]{0:T(256)}, f32[256]{0:T(256)S(1)}, u32[]{:S(2)}) copy-start(f32[256]{0:T(256)S(1)} %get-tuple-element.59) | copy-start | bytes 3076
  328.1 11.1 %copy-start.49 = (bf16[8,144]{1,0:T(8,128)(2,1)S(1)}, bf16[8,144]{1,0:T(8,128)(2,1)}, u32[]{:S(2)}) copy-start(bf16[8,144]{1,0:T(8,128)(2,1)} %mul.485) | copy-start | bytes 6916
  341.4 46.3 %copy-start.82 = (f32[1152,768]{1,0:T(8,128)S(1)}, f32[1152,768]{1,0:T(8,128)}, u32[]{:S(2)}) copy-start(f32[1152,768]{1,0:T(8,128)} %copy-done.81) | copy-start | bytes 10616836
  341.4 46.3 %copy-start.83 = (f32[1152,768]{1,0:T(8,128)S(1)}, f32[1152,768]{1,0:T(8,128)}, u32[]{:S(2)}) copy-start(f32[1152,768]{1,0:T(8,128)} %get-tuple-element.100) | copy-start | bytes 10616836
  400.5 47.3 %all-to-all-start.3 = ((bf16[1,8,144,1536]{3,2,0,1:T(8,128)(2,1)}), bf16[1,8,144,1536]{3,2,0,1:T(8,128)(2,1)}, u32[]{:S(2)}, u32[]{:S(2)}) async-start(bf16[1,8,144,1536]{3,2,0,1:T(8,128)(2,1)} %bitcast.315), calls=%async_computation.3 | async-start | bytes 7077888 | tf_op jit(solution)/shard_map/all_to_all | solution.py:297
  405.9 41.9 %copy-start.51 = (s32[1024]{0:T(1024)S(1)}, s32[1024]{0:T(1024)}, u32[]{:S(2)}) copy-start(s32[1024]{0:T(1024)} %broadcast_clamp_fusion) | copy-start | bytes 12292
  405.9 168.4 %reduce-scatter.5.cloned.1.call-start = ((), (), s32[]{:S(2)}) async-start(), calls=%async_computation.8 | async-start | bytes 2359296 | tf_op jit(solution)/shard_map/reduce_scatter | solution.py:48
  464.5 7.8 copy-start.7
  464.5 7.8 copy-start.42
  464.5 7.8 copy-start.61
  482.0 17.3 %slice-start = ((s8[12582912]{0:T(1024)(128)(4,1)}), s8[4194304]{0:T(1024)(128)(4,1)S(1)}, s32[]{:S(2)}) async-start(s8[12582912]{0:T(1024)(128)(4,1)} %bitcast.277), calls=%async_computation.12 | async-start | bytes 8388608
  482.0 17.3 %slice-start.1 = ((s8[12582912]{0:T(1024)(128)(4,1)}), s8[4194304]{0:T(1024)(128)(4,1)S(1)}, s32[]{:S(2)}) async-start(s8[12582912]{0:T(1024)(128)(4,1)} %bitcast.277), calls=%async_computation.13 | async-start | bytes 8388608
  492.4 7.0 slice-start.2
  499.4 8.9 %slice-start.3 = ((s8[12582912]{0:T(1024)(128)(4,1)}), s8[4194304]{0:T(1024)(128)(4,1)S(1)}, s32[]{:S(2)}) async-start(s8[12582912]{0:T(1024)(128)(4,1)} %bitcast.279), calls=%async_computation.15 | async-start | bytes 8388608
  499.4 8.9 %slice-start.4 = ((s8[12582912]{0:T(1024)(128)(4,1)}), s8[4194304]{0:T(1024)(128)(4,1)S(1)}, s32[]{:S(2)}) async-start(s8[12582912]{0:T(1024)(128)(4,1)} %bitcast.279), calls=%async_computation.16 | async-start | bytes 8388608
  508.3 9.2 %copy-start.13 = (bf16[256,12,64]{2,0,1:T(8,128)(2,1)S(1)}, bf16[256,12,64]{2,0,1:T(8,128)(2,1)}, u32[]{:S(2)}) copy-start(bf16[256,12,64]{2,0,1:T(8,128)(2,1)} %copy.150) | copy-start | bytes 1179652
  508.3 9.1 %copy-start.15 = (bf16[256,12,64]{2,0,1:T(8,128)(2,1)S(1)}, bf16[256,12,64]{2,0,1:T(8,128)(2,1)}, u32[]{:S(2)}) copy-start(bf16[256,12,64]{2,0,1:T(8,128)(2,1)} %copy.151) | copy-start | bytes 1179652
  533.2 7.5 copy-start.80
  533.2 165.0 %all-reduce.10.cloned.1.call-start = ((), (), s32[]{:S(2)}) async-start(), calls=%async_computation.11 | async-start | bytes 14155776 | tf_op jit(solution)/shard_map/psum | solution.py:479
  533.3 7.4 copy-start.26
  549.9 243.4 %reduce-scatter.7.cloned.1.call-start = ((), (), s32[]{:S(2)}) async-start(), calls=%async_computation.10 | async-start | bytes 12115968
  655.6 212.7 %all-reduce.8.cloned.1.call-start = ((), (), s32[]{:S(2)}) async-start(), calls=%async_computation.9 | async-start | bytes 1380352 | tf_op jit(solution)/shard_map/psum | solution.py:66
  810.0 66.5 %copy-start.1 = (bf16[1,768,1536]{2,1,0:T(8,128)(2,1)S(1)}, bf16[1,768,1536]{2,1,0:T(8,128)(2,1)}, u32[]{:S(2)}) copy-start(bf16[1,768,1536]{2,1,0:T(8,128)(2,1)} %param.25) | copy-start | bytes 7077892
  (52 other events, 189.8 us)
Sparse Core Ops, SparseCore 0:
  12.3 87.8 all-gather.2
  107.1 27.1 all-gather.4
  533.3 28.7 reduce-scatter.4
  566.3 131.8 all-reduce.9
  701.9 91.3 reduce-scatter.6
  810.1 58.1 all-reduce.7
where the time goes:
time: 897 us; the launch traced here: 884 us
  waiting for transfers between devices  322 us (36%)
  local copies, waits for them, and re-layouts  198 us (22%)
  matrix products  156 us (17%)
  blocking collectives  93.4 us (10%)
  other arithmetic  86.5 us (10%)
  between operations  16 us (2%)
  starting transfers between devices  11.7 us (1%)
    unnamed x7, waiting for transfers between devices  85.5 us
    all_gather x1, waiting for transfers between devices, sent_together(): lax.all_gather(both, axis, axis=dim, tiled=True)  83.8 us
    concatenate x1, local copies, waits for them, and re-layouts, sent_together_3(): jnp.concatenate([a.reshape(*a.shape[:along], w) for a, w in zip(arrays, w...  58.2 us
    psum x1, waiting for transfers between devices, together(): subtotal = lax.psum(jnp.concatenate([a.ravel() for a in arrays]), axis)  54.7 us
    all_to_all x1, blocking collectives, on_device(): lax.all_to_all(outgoing, 'expert', split_axis=1, concat_axis=1, tiled=True)  47.2 us
    all_to_all x1, blocking collectives, on_device(): lax.all_to_all(outgoing_grads, 'expert', split_axis=1, concat_axis=1, til...  46.2 us
    psum x1, waiting for transfers between devices, on_device(): lax.psum(grad_wgate.astype(jnp.bfloat16), 'dp').astype(jnp.float32)  42.3 us
    all_to_all x1, waiting for transfers between devices, on_device(): lax.all_to_all(grad_rows, 'expert', split_axis=1, concat_axis=1, tiled=True)  36.8 us
  transfers between devices with their start and end apart: 8, of which 6 were waited for; matrix products, arithmetic and copies ran while one was open for 23% of the time, Pallas kernels for 0%

commit v1 on v0

v1 whole, which is shorter than its diff:
```python
import functools

import jax
import jax.numpy as jnp
from jax import lax
from jax.experimental import pallas as pl
from jax.experimental.pallas import tpu as pltpu
from jax.sharding import PartitionSpec as P

QUERY_HEADS = 12
KEY_VALUE_HEADS = 2
HEAD_SIZE = 128
TOPK = 4
EXPERTS = 8
DOCS = 4
GROUP = QUERY_HEADS // KEY_VALUE_HEADS

EPSILON = 1e-06
ROPE_BASE = 1000000.0
MASK_FILL = -1e30
F32 = jnp.float32
BF16 = jnp.bfloat16

PARTNER = [(i, i ^ 1) for i in range(8)]
SAME_CORE = [[0, 2, 4, 6], [1, 3, 5, 7]]


def dot(a, b, dims):
    return lax.dot_general(a, b, (dims, ((), ())), preferred_element_type=F32)


def mm(a, b):
    return dot(a, b, ((1,), (0,)))


def mm_nt(a, b):
    return dot(a, b, ((1,), (1,)))


def mm_tn(a, b):
    return dot(a, b, ((0,), (0,)))


def rms_scale(value_rows, gain):
    inverse = lax.rsqrt(jnp.mean(value_rows * value_rows, axis=-1, keepdims=True) + EPSILON)
    return value_rows * inverse * gain


def rms_back(value_rows, gain, grad):
    inverse = lax.rsqrt(jnp.mean(value_rows * value_rows, axis=-1, keepdims=True) + EPSILON)
    scaled = value_rows * inverse
    weighted = grad * gain
    inner = jnp.mean(weighted * scaled, axis=-1, keepdims=True)
    return inverse * (weighted - scaled * inner), jnp.sum(grad * scaled, axis=0)


def doc_positions(seg_row):
    labels = jnp.arange(DOCS, dtype=jnp.int32)
    member = (seg_row[:, None] == labels[None, :]).astype(jnp.int32)
    counts = jnp.sum(member, axis=0)
    starts = jnp.cumsum(counts) - counts
    leading = jnp.sum(member * starts[None, :], axis=1)
    return jnp.arange(seg_row.shape[0], dtype=jnp.int32) - leading


def angles_for(positions):
    half_width = HEAD_SIZE // 2
    freqs = ROPE_BASE ** (-2.0 * jnp.arange(half_width, dtype=F32) / HEAD_SIZE)
    return positions.astype(F32)[:, None] * freqs[None, :]


def rotate(flat, cosine, sine, sign):
    heads = flat.reshape(flat.shape[0], -1, HEAD_SIZE)
    a, b = jnp.split(heads, 2, axis=-1)
    c, s = cosine[:, None, :], sign * sine[:, None, :]
    return jnp.concatenate([a * c - b * s, b * c + a * s], axis=-1).reshape(flat.shape)


def pp_core(x):
    return lax.ppermute(x, "expert", PARTNER)


def gather_dense(shard, core):
    half = shard.shape[1] // 2
    mine = lax.dynamic_slice_in_dim(shard, core * half, half, 1)
    got = lax.all_gather(mine, "dp", axis=0, tiled=True)
    other = pp_core(got)
    first = jnp.where(core == 0, got, other)
    second = jnp.where(core == 0, other, got)
    return jnp.concatenate([first, second], axis=1)


def ag_x(block):
    return lax.all_gather(block, "expert", axis=0, tiled=True)


def rs_x(blocks):
    return lax.psum_scatter(blocks, "expert", scatter_dimension=0, tiled=True)


MESH = pl.DeviceIdType.MESH
ANY = pl.BlockSpec(memory_space=pl.ANY)
VMEM = pl.BlockSpec(memory_space=pltpu.VMEM)


class Sends:
    def __init__(self, send_sems, recv_sems):
        self.send_sems, self.recv_sems, self.made = send_sems, recv_sems, []

    def start(self, src, dst, to):
        at = len(self.made)
        copy = pltpu.make_async_remote_copy(
            src_ref=src,
            dst_ref=dst,
            send_sem=self.send_sems.at[at],
            recv_sem=self.recv_sems.at[at],
            device_id=to,
            device_id_type=MESH,
        )
        copy.start()
        self.made.append(copy)
        return copy

    def finish(self):
        for copy in self.made:
            copy.wait_send()


def meet(*others):
    barrier = pltpu.get_barrier_semaphore()
    for other in others:
        pl.semaphore_signal(barrier, inc=1, device_id=other, device_id_type=MESH)
    pl.semaphore_wait(barrier, len(others))


def around_x():
    part = lax.axis_index("expert")
    x, core = part // 2, part % 2
    at = lambda dx: ((x + dx) % 4) * 2 + core
    return part, core, at(1), at(3), at(2), 2 * x + (1 - core)


def gather_x_kernel(block_ref, out_ref, local_sem, send_sems, recv_sems):
    part, core, right, left, far, partner = around_x()
    to = lambda i: {"expert": i}
    meet(to(partner), to(right), to(left))
    sends = Sends(send_sems, recv_sems)
    half = block_ref.shape[0] // 2
    own = pltpu.make_async_copy(block_ref, out_ref.at[part], local_sem)
    go_right = sends.start(block_ref, out_ref.at[part], to(right))
    go_left = sends.start(block_ref, out_ref.at[part], to(left))
    across = [sends.start(block_ref, out_ref.at[part], to(partner))]
    own.start()
    go_right.wait_recv()
    first = out_ref.at[left, pl.ds(0, half)]
    far_first = sends.start(first, first, to(right))
    across.append(sends.start(out_ref.at[left], out_ref.at[left], to(partner)))
    go_left.wait_recv()
    second = out_ref.at[right, pl.ds(half, half)]
    far_second = sends.start(second, second, to(left))
    across.append(sends.start(out_ref.at[right], out_ref.at[right], to(partner)))
    far_first.wait_recv()
    piece = out_ref.at[far, pl.ds(0, half)]
    across.append(sends.start(piece, piece, to(partner)))
    far_second.wait_recv()
    piece = out_ref.at[far, pl.ds(half, half)]
    across.append(sends.start(piece, piece, to(partner)))
    for copy in across:
        copy.wait_recv()
    own.wait()
    sends.finish()


def gather_x(block, collective_id):
    return pl.pallas_call(
        gather_x_kernel,
        out_shape=jax.ShapeDtypeStruct((8, *block.shape), block.dtype),
        in_specs=[ANY],
        out_specs=ANY,
        scratch_shapes=[
            pltpu.SemaphoreType.DMA,
            pltpu.SemaphoreType.DMA((9,)),
            pltpu.SemaphoreType.DMA((9,)),
        ],
        compiler_params=pltpu.CompilerParams(collective_id=collective_id, has_side_effects=True),
    )(block)


def reduce_x_kernel(
    blocks_ref, out_ref, mine, theirs, total, from_left, from_right, local_sems, send_sems, recv_sems
):
    part, core, right, left, far, partner = around_x()
    to = lambda i: {"expert": i}
    meet(to(partner), to(right), to(left))
    sends = Sends(send_sems, recv_sems)
    rows = out_ref.shape[0]
    half = rows // 2
    low, high = pl.ds(0, half), pl.ds(half, half)
    order = (far, right, left, part)
    flip = 1 - 2 * core
    swaps, loads = [], []
    for k, dest in enumerate(order):
        swaps.append(sends.start(blocks_ref.at[dest + flip], theirs.at[k], to(partner)))
        load = pltpu.make_async_copy(blocks_ref.at[dest], mine.at[k], local_sems.at[k])
        load.start()
        loads.append(load)

    def add_up(k):
        loads[k].wait()
        swaps[k].wait_recv()
        total[k] = (mine[k].astype(F32) + theirs[k].astype(F32)).astype(BF16)

    add_up(0)
    far_low = sends.start(total.at[0, low], from_left.at[0], to(right))
    far_high = sends.start(total.at[0, high], from_right.at[0], to(left))
    add_up(1)
    right_high = sends.start(total.at[1, high], from_left.at[2], to(right))
    add_up(2)
    left_low = sends.start(total.at[2, low], from_right.at[2], to(left))
    far_low.wait_recv()
    total[1, low] = (total[1, low].astype(F32) + from_left[0].astype(F32)).astype(BF16)
    right_low = sends.start(total.at[1, low], from_left.at[1], to(right))
    far_high.wait_recv()
    total[2, high] = (total[2, high].astype(F32) + from_right[0].astype(F32)).astype(BF16)
    left_high = sends.start(total.at[2, high], from_right.at[1], to(left))
    loads[3].wait()
    swaps[3].wait_recv()
    out_ref[...] = mine[3].astype(F32) + theirs[3].astype(F32)
    right_high.wait_recv()
    out_ref[high] += from_left[2].astype(F32)
    left_low.wait_recv()
    out_ref[low] += from_right[2].astype(F32)
    right_low.wait_recv()
    out_ref[low] += from_left[1].astype(F32)
    left_high.wait_recv()
    out_ref[high] += from_right[1].astype(F32)
    sends.finish()


def reduce_x(blocks, collective_id):
    _, rows, columns = blocks.shape
    part = (rows // 2, columns)
    return pl.pallas_call(
        reduce_x_kernel,
        out_shape=jax.ShapeDtypeStruct((rows, columns), F32),
        in_specs=[ANY],
        out_specs=VMEM,
        scratch_shapes=[
            pltpu.VMEM((4, rows, columns), BF16),
            pltpu.VMEM((4, rows, columns), BF16),
            pltpu.VMEM((3, rows, columns), BF16),
            pltpu.VMEM((3, *part), BF16),
            pltpu.VMEM((3, *part), BF16),
            pltpu.SemaphoreType.DMA((4,)),
            pltpu.SemaphoreType.DMA((10,)),
            pltpu.SemaphoreType.DMA((10,)),
        ],
        compiler_params=pltpu.CompilerParams(
            collective_id=collective_id, has_side_effects=True, vmem_limit_bytes=50 * 2**20
        ),
    )(blocks)


def around_yz():
    place = lax.axis_index("dp")
    y, z = place // 4, place % 4
    turn = lambda v, d: (v + d) % 4
    y_ring = [turn(y, d) for d in (1, 3, 2)]
    z_ring = [turn(z, d) for d in (1, 3, 2)]
    return y, z, y_ring, z_ring


def gather_yz_kernel(shard_ref, small_ref, out_ref, small_out, local_sems, send_sems, recv_sems):
    y, z, y_ring, z_ring = around_yz()
    part = lax.axis_index("expert")
    core = part % 2
    partner = {"expert": part + 1 - 2 * core}
    y_to = [{"dp": v * 4 + z} for v in y_ring[:2]]
    z_to = [{"dp": y * 4 + v} for v in z_ring[:2]]
    meet(partner, *y_to, *z_to)
    rows, columns = shard_ref.shape
    quarter = columns // 4
    sends = Sends(send_sems, recv_sems)

    def strip(p):
        return pl.ds(pl.multiple_of((2 * core + p) * quarter, 128), quarter)

    own = [
        pltpu.make_async_copy(
            shard_ref.at[:, strip(p)], out_ref.at[y, z, :, strip(p)], local_sems.at[p]
        )
        for p in range(2)
    ]
    own.append(pltpu.make_async_copy(small_ref, small_out.at[y, z], local_sems.at[2]))

    class Piece:
        def __init__(self, src, out, cols, z_first):
            self.src, self.out, self.cols, self.z_first = src, out, cols, z_first

        def ring(self, first):
            if self.z_first == first:
                return z, z_ring, z_to
            return y, y_ring, y_to

        def view(self, first, where, piece=None):
            if first:
                at = pl.ds(0, rows) if piece is None else pl.ds(piece * rows // 2, rows // 2)
                if self.z_first:
                    return self.out.at[y, where, at, self.cols]
                return self.out.at[where, z, at, self.cols]
            span = pl.ds(0, 4) if piece is None else pl.ds(2 * piece, 2)
            if self.z_first:
                return self.out.at[where, span, :, self.cols]
            return self.out.at[span, where, :, self.cols]

    strips = [
        Piece(small_ref, small_out, pl.ds(0, small_ref.shape[1]), True),
        Piece(shard_ref, out_ref, strip(0), True),
        Piece(shard_ref, out_ref, strip(1), False),
    ]
    across = []

    def send_across(s, view):
        if s.src is shard_ref:
            across.append(sends.start(view, view, partner))

    for first in (True, False):
        stage = []
        for s in strips:
            me, _, to = s.ring(first)
            src = s.src.at[:, s.cols] if first else s.view(first, me)
            stage.append([sends.start(src, s.view(first, me), to[i]) for i in range(2)])
        if first:
            for copy in own:
                copy.start()
        else:
            for s in strips:
                send_across(s, s.view(first, s.ring(first)[0]))
        onward = []
        for s, came in zip(strips, stage):
            _, (right, left, _), to = s.ring(first)
            pair = []
            for i, origin in enumerate((left, right)):
                came[i].wait_recv()
                view = s.view(first, origin, i)
                pair.append(sends.start(view, view, to[i]))
                if not first:
                    send_across(s, s.view(first, origin))
            onward.append(pair)
        for s, pair in zip(strips, onward):
            far = s.ring(first)[1][2]
            for i in range(2):
                pair[i].wait_recv()
                if not first:
                    send_across(s, s.view(first, far, i))
        if first:
            for copy in own:
                copy.wait()
    for copy in across:
        copy.wait_recv()
    sends.finish()


def gather_yz(shard, small, collective_id):
    return pl.pallas_call(
        gather_yz_kernel,
        out_shape=[
            jax.ShapeDtypeStruct((4, 4, *shard.shape), shard.dtype),
            jax.ShapeDtypeStruct((4, 4, *small.shape), small.dtype),
        ],
        in_specs=[ANY, ANY],
        out_specs=[ANY, ANY],
        scratch_shapes=[
            pltpu.SemaphoreType.DMA((3,)),
            pltpu.SemaphoreType.DMA((41,)),
            pltpu.SemaphoreType.DMA((41,)),
        ],
        compiler_params=pltpu.CompilerParams(collective_id=collective_id, has_side_effects=True),
    )(shard, small)


class Strip:
    def __init__(self, source, cols, theirs_cols, y_first, bufs):
        self.source, self.cols, self.theirs_cols, self.y_first = source, cols, theirs_cols, y_first
        self.total, self.theirs, self.big, self.far, self.mid, self.midfar, self.near = bufs


def strip_buffers(rows, columns):
    return [
        pltpu.VMEM((4, 4, rows, columns), BF16),
        pltpu.VMEM((4, 4, rows, columns), BF16),
        pltpu.VMEM((2, 2, 2, rows, columns), BF16),
        pltpu.VMEM((2, 2, rows, columns), BF16),
        pltpu.VMEM((2, 2, rows // 2, columns), BF16),
        pltpu.VMEM((2, rows // 2, columns), BF16),
        pltpu.VMEM((4, rows, columns), BF16),
    ]


def reduce_yz_kernel(n_wide, *refs):
    grads, small_ref = refs[:n_wide], refs[n_wide]
    outs, small_out = refs[n_wide + 1 : 2 * n_wide + 1], refs[2 * n_wide + 1]
    bufs = refs[2 * n_wide + 2 : -3]
    local_sems, send_sems, recv_sems = refs[-3:]
    y, z, y_ring, z_ring = around_yz()
    part, core, x_right, x_left, x_far, partner = around_x()
    partner = {"expert": partner}
    x_to = [{"expert": i} for i in (x_right, x_left, x_far)]
    y_to = [{"dp": v * 4 + z} for v in y_ring[:2]]
    z_to = [{"dp": y * 4 + v} for v in z_ring[:2]]
    meet(partner, *y_to, *z_to, *x_to)
    sends = Sends(send_sems, recv_sems)
    strips, owners = [], []
    for g, out in zip(grads, outs):
        quarter = g.shape[-1] // 4
        for p in range(2):
            cols = [
                pl.ds(pl.multiple_of((2 * c + p) * quarter, 128), quarter)
                for c in (core, 1 - core)
            ]
            at = 7 * len(strips)
            strips.append(Strip(g, cols[0], cols[1], p == 0, bufs[at : at + 7]))
            owners.append(out)
    at = 7 * len(strips)
    every = pl.ds(0, small_ref.shape[-1])
    strips.append(Strip(small_ref, every, None, True, bufs[at : at + 7]))
    owners.append(small_out)

    def ring(s, first):
        return (y, y_ring, y_to) if s.y_first == first else (z, z_ring, z_to)

    def block(ref, s, w):
        return ref.at[w] if s.y_first else ref.at[:, w]

    def columns(s, w, cols):
        return s.source.at[w, :, :, cols] if s.y_first else s.source.at[:, w, :, cols]

    def add(ref, *others):
        got = ref[...].astype(F32)
        for other in others:
            got += other[...].astype(F32)
        ref[...] = got.astype(BF16)

    swaps, loads = {}, {}
    for k in range(4):
        for i, s in enumerate(strips):
            me, (right, left, far), _ = ring(s, True)
            w = (far, right, left, me)[k]
            if s.theirs_cols is not None:
                swaps[k, i] = sends.start(
                    columns(s, w, s.theirs_cols), block(s.theirs, s, w), partner
                )
            load = pltpu.make_async_copy(
                columns(s, w, s.cols), block(s.total, s, w), local_sems.at[k * len(strips) + i]
            )
            load.start()
            loads[k, i] = load

    def joined(k, i, s, w):
        loads[k, i].wait()
        if s.theirs_cols is not None:
            swaps[k, i].wait_recv()
            add(block(s.total, s, w), block(s.theirs, s, w))

    def ring_sum(first, view, whole, farther, ready):
        going = []
        for i, s in enumerate(strips):
            _, (right, left, far), to = ring(s, first)
            ready(0, i, s, far)
            going.append(
                [sends.start(view(s, far, h), farther(s).at[h], to[h]) for h in range(2)]
            )
        for i, s in enumerate(strips):
            _, (right, left, far), to = ring(s, first)
            ready(1, i, s, right)
            ready(2, i, s, left)
            going[i].append(sends.start(view(s, right, 1), whole(s).at[0, 1], to[0]))
            going[i].append(sends.start(view(s, left, 0), whole(s).at[1, 0], to[1]))
        for i, s in enumerate(strips):
            _, (right, left, far), to = ring(s, first)
            for h, w in enumerate((right, left)):
                going[i][h].wait_recv()
                add(view(s, w, h), farther(s).at[h])
                going[i].append(sends.start(view(s, w, h), whole(s).at[h, h], to[h]))
        for i, s in enumerate(strips):
            me, _, _ = ring(s, first)
            ready(3, i, s, me)
            for copy in going[i][2:]:
                copy.wait_recv()
            for h in range(2):
                add(view(s, me, h), whole(s).at[0, h], whole(s).at[1, h])

    def big(s, w, h):
        span = pl.ds(2 * h, 2)
        return s.total.at[w, span] if s.y_first else s.total.at[span, w]

    def small(s, w, h):
        half = s.total.shape[2] // 2
        at = pl.ds(h * half, half)
        return s.total.at[y, w, at] if s.y_first else s.total.at[w, z, at]

    ring_sum(True, big, lambda s: s.big, lambda s: s.far, joined)
    ring_sum(False, small, lambda s: s.mid, lambda s: s.midfar, lambda *_: None)

    shares, back = [], []
    for s in strips:
        shares.append(
            [sends.start(s.total.at[y, z], s.near.at[i], x_to[i]) for i in range(3)]
        )
    for s, share in zip(strips, shares):
        for copy in share:
            copy.wait_recv()
        got = s.total[y, z].astype(F32)
        for i in range(3):
            got += s.near[i].astype(F32)
        s.theirs[y, z] = got.astype(BF16)
        back.append(sends.start(s.theirs.at[y, z], s.near.at[3], partner))
    for s, out, copy in zip(strips, owners, back):
        copy.wait_recv()
        if s.theirs_cols is None:
            out[...] = s.theirs[y, z].astype(F32) + s.near[3].astype(F32)
        else:
            out[:, s.cols] = s.theirs[y, z].astype(F32)
            out[:, s.theirs_cols] = s.near[3].astype(F32)
    sends.finish()


def reduce_yz(grads, small, collective_id):
    every = [*grads, small]
    buffers = []
    for g in grads:
        for _ in range(2):
            buffers += strip_buffers(g.shape[2], g.shape[3] // 4)
    buffers += strip_buffers(*small.shape[2:])
    n_strips = 2 * len(grads) + 1
    return pl.pallas_call(
        functools.partial(reduce_yz_kernel, len(grads)),
        out_shape=[jax.ShapeDtypeStruct(g.shape[2:], F32) for g in every],
        in_specs=[ANY] * len(every),
        out_specs=[VMEM] * len(every),
        scratch_shapes=[
            *buffers,
            pltpu.SemaphoreType.DMA((4 * n_strips,)),
            pltpu.SemaphoreType.DMA((20 * n_strips,)),
            pltpu.SemaphoreType.DMA((20 * n_strips,)),
        ],
        compiler_params=pltpu.CompilerParams(
            collective_id=collective_id, has_side_effects=True, vmem_limit_bytes=56 * 2**20
        ),
    )(*every)


def on_device(
    tokens,
    d_out,
    gain_in,
    w_query,
    key_projection_weight,
    value_projection_weight,
    w_out,
    gain_mid,
    w_router,
    w_gate,
    w_up,
    w_down,
    routes,
    segments,
):
    rows, width = tokens.shape
    length = segments.shape[1]
    scaling = HEAD_SIZE ** (-0.5)
    part = lax.axis_index("expert")
    parts = lax.axis_size("expert")
    core = part % 2
    capacity = rows * 9 // 16
    seg_row = segments[0]
    offset = part * rows
    angles = angles_for(lax.dynamic_slice_in_dim(doc_positions(seg_row), offset, rows, 0))
    cosine, sine = jnp.cos(angles), jnp.sin(angles)
    my_seg = lax.dynamic_slice_in_dim(seg_row, offset, rows, 0)
    my_rows = offset + jnp.arange(rows, dtype=jnp.int32)
    key_places = jnp.arange(length, dtype=jnp.int32)
    allowed = (my_seg[:, None] == seg_row[None, :]) & (my_rows[:, None] >= key_places[None, :])

    small = jnp.concatenate([gain_in[:, None], gain_mid[:, None], w_router], axis=1)
    small = jnp.pad(small, ((0, 0), (0, 128 - small.shape[1])))
    shard = jnp.concatenate([w_query, key_projection_weight, value_projection_weight], axis=1)
    wqkv, small = gather_yz(shard, small, 1)
    wqkv = wqkv.reshape(width, -1)
    small = small.reshape(width, -1)
    gain_in_all = small[:, 0].astype(F32)
    gain_mid_all = small[:, 1].astype(F32)
    wr = small[:, 2 : 2 + EXPERTS]
    wo = gather_dense(w_out, core)
    upstream_all = ag_x(d_out)
    routes_all = ag_x(routes.astype(BF16)).astype(jnp.int32)

    inputs = tokens.astype(F32)
    normed = rms_scale(inputs, gain_in_all).astype(BF16)
    kv_at = QUERY_HEADS * HEAD_SIZE
    kv_width = KEY_VALUE_HEADS * HEAD_SIZE
    kv_lin = mm(normed, wqkv[:, kv_at:])
    key_block = rotate(kv_lin[:, :kv_width], cosine, sine, 1.0).astype(BF16)
    kv_all = gather_x(
        jnp.concatenate([key_block, kv_lin[:, kv_width:].astype(BF16)], axis=1), 2
    ).reshape(length, -1)
    keys = kv_all[:, :kv_width].reshape(length, KEY_VALUE_HEADS, HEAD_SIZE)
    values = kv_all[:, kv_width:].reshape(length, KEY_VALUE_HEADS, HEAD_SIZE)
    query = rotate(mm(normed, wqkv[:, :kv_at]), cosine, sine, 1.0).astype(BF16)
    query = query.reshape(rows, KEY_VALUE_HEADS, GROUP, HEAD_SIZE)

    def scores_for(h):
        raw = jnp.einsum("tgd,sd->gts", query[:, h], keys[:, h], preferred_element_type=F32)
        return jnp.where(allowed[None], raw * scaling, MASK_FILL)

    contexts, log_sums = [], []
    for h in range(KEY_VALUE_HEADS):
        scores = scores_for(h)
        row_max = jnp.max(scores, axis=-1, keepdims=True)
        shifted = jnp.exp(scores - row_max)
        row_sum = jnp.sum(shifted, axis=-1, keepdims=True)
        probs = (shifted / row_sum).astype(BF16)
        contexts.append(
            jnp.einsum("gts,sd->tgd", probs, values[:, h], preferred_element_type=F32)
        )
        log_sums.append(row_max + jnp.log(row_sum))
    context = jnp.stack(contexts, axis=1).reshape(rows, kv_at).astype(BF16)
    middle = inputs + mm(context, wo)
    normed_mid = rms_scale(middle, gain_mid_all).astype(BF16)

    expert_ids = jnp.arange(EXPERTS, dtype=jnp.int32)

    def gates_for(logits, chosen_routes):
        chosen = jnp.sum(
            logits[:, None, :] * (chosen_routes[:, :, None] == expert_ids).astype(F32), axis=-1
        )
        return jax.nn.softmax(chosen, axis=-1)

    gates = gates_for(mm(normed_mid, wr), routes)
    normed_all = gather_x(normed_mid, 3).reshape(length, width)
    gates_all = gates_for(mm(normed_all, wr), routes_all)
    mine = routes_all == part
    gate_mine = jnp.sum(jnp.where(mine, gates_all, 0.0), axis=-1).reshape(parts, rows)
    member = jnp.any(mine, axis=-1).reshape(parts, rows)
    ranks = jnp.cumsum(member.astype(jnp.int32), axis=1) - 1
    slots = jnp.arange(capacity, dtype=jnp.int32)
    pick = (ranks[:, None, :] == slots[None, :, None]) & member[:, None, :]
    pick_b = pick.astype(BF16)

    def take(all_rows):
        got = jnp.einsum(
            "prt,ptd->prd", pick_b, all_rows.reshape(parts, rows, -1), preferred_element_type=F32
        )
        return got.astype(BF16).reshape(parts * capacity, -1)

    def put_back(slot_rows):
        got = jnp.einsum(
            "prt,prd->ptd",
            pick_b,
            slot_rows.reshape(parts, capacity, -1),
            preferred_element_type=F32,
        )
        return got.astype(BF16).reshape(parts * rows, -1)

    gate_slot = jnp.sum(jnp.where(pick, gate_mine[:, None, :], 0.0), axis=-1).reshape(-1, 1)
    arrived = take(normed_all)
    up_slot = take(upstream_all).astype(F32)
    pair_grad = (gate_slot * up_slot).astype(BF16)
    wg, wu, wd = w_gate[0], w_up[0], w_down[0]
    gate_pre = mm(arrived, wg)
    up_pre = mm(arrived, wu)

    def glu_act(a, b):
        return jax.nn.gelu(a, approximate=True) * b

    hidden_f, pull_act = jax.vjp(glu_act, gate_pre, up_pre)
    hidden = hidden_f.astype(BF16)
    expert_out = mm(hidden, wd).astype(BF16).astype(F32)
    grad_gate_slot = jnp.sum(up_slot * expert_out, axis=-1)
    back_out = put_back((gate_slot * expert_out).astype(BF16))
    grad_hidden = mm_nt(pair_grad, wd)
    grad_gate_pre, grad_up_pre = pull_act(grad_hidden)
    grad_gate_b = grad_gate_pre.astype(BF16)
    grad_up_b = grad_up_pre.astype(BF16)
    grad_rows = (mm_nt(grad_gate_b, wg) + mm_nt(grad_up_b, wu)).astype(BF16)
    hot_mine = (jnp.arange(128) == part).astype(F32) + (jnp.arange(128) == part + EXPERTS) * 2.0
    gate_high = grad_gate_slot.astype(BF16).astype(F32)
    gate_parts = jnp.where(
        hot_mine == 1.0,
        gate_high[:, None],
        jnp.where(hot_mine == 2.0, (grad_gate_slot - gate_high)[:, None], 0.0),
    )
    returned = put_back(jnp.concatenate([grad_rows, gate_parts.astype(BF16)], axis=1))
    returned = reduce_x(returned.reshape(parts, rows, -1), 4)
    grad_mid_sum = returned[:, :width]
    grad_gates = returned[:, width : width + EXPERTS] + returned[
        :, width + EXPERTS : width + 2 * EXPERTS
    ]
    combined = rs_x(back_out).astype(F32)
    mixed = (middle + combined).astype(BF16)
    grad_wdown = mm_tn(hidden, pair_grad).astype(BF16)
    grad_wgate = mm_tn(arrived, grad_gate_b).astype(BF16)
    grad_wup = mm_tn(arrived, grad_up_b).astype(BF16)

    hot = (routes[:, :, None] == expert_ids).astype(F32)
    gate_by_expert = jnp.sum(gates[:, :, None] * hot, axis=1)
    gg = gate_by_expert * grad_gates
    grad_logits = (gg - gate_by_expert * jnp.sum(gg, axis=1, keepdims=True)).astype(BF16)
    upstream = d_out.astype(F32)
    grad_normed_mid = grad_mid_sum + mm_nt(grad_logits, wr)
    grad_wr = mm_tn(normed_mid, grad_logits)
    grad_middle_norm, grad_gmid = rms_back(middle, gain_mid_all, grad_normed_mid)
    grad_middle = upstream + grad_middle_norm
    grad_attn = grad_middle.astype(BF16)
    grad_wo = mm_tn(context, grad_attn)
    grad_ctx = mm_nt(grad_attn, wo).astype(BF16)
    grad_ctx = grad_ctx.reshape(rows, KEY_VALUE_HEADS, GROUP, HEAD_SIZE)

    query_grads, key_parts, value_parts = [], [], []
    for h in range(KEY_VALUE_HEADS):
        probs_full = jnp.exp(scores_for(h) - log_sums[h])
        ctx_h = grad_ctx[:, h]
        grad_probs = jnp.einsum("tgd,sd->gts", ctx_h, values[:, h], preferred_element_type=F32)
        value_parts.append(
            jnp.einsum("gts,tgd->sd", probs_full.astype(BF16), ctx_h, preferred_element_type=F32)
        )
        inner = jnp.sum(probs_full * grad_probs, axis=-1, keepdims=True)
        grad_scores = (probs_full * (grad_probs - inner)).astype(BF16)
        query_grads.append(
            jnp.einsum("gts,sd->tgd", grad_scores, keys[:, h], preferred_element_type=F32)
            * scaling
        )
        key_parts.append(
            jnp.einsum("gts,tgd->sd", grad_scores, query[:, h], preferred_element_type=F32)
            * scaling
        )
    grad_query = jnp.stack(query_grads, axis=1).reshape(rows, kv_at)
    kv_terms = jnp.concatenate([p.astype(BF16) for p in key_parts + value_parts], axis=1)
    kv_grad = reduce_x(kv_terms.reshape(parts, rows, -1), 5)
    grad_qlin = rotate(grad_query, cosine, sine, -1.0).astype(BF16)
    grad_klin = rotate(kv_grad[:, :kv_width], cosine, sine, -1.0).astype(BF16)
    grad_lin = jnp.concatenate([grad_qlin, grad_klin, kv_grad[:, kv_width:].astype(BF16)], axis=1)
    grad_wqkv = mm_tn(normed, grad_lin)
    grad_normed = mm_nt(grad_lin, wqkv)
    grad_inputs_norm, grad_gin = rms_back(inputs, gain_in_all, grad_normed)
    grad_tokens = grad_middle + grad_inputs_norm

    small_grads = jnp.concatenate([grad_gin[:, None], grad_gmid[:, None], grad_wr], axis=1)
    small_grads = jnp.pad(small_grads.astype(BF16), ((0, 0), (0, 128 - small_grads.shape[1])))
    qkv_sum, wo_sum, small_sum = reduce_yz(
        [g.astype(BF16).reshape(4, 4, width // 16, -1) for g in (grad_wqkv, grad_wo)],
        small_grads.reshape(4, 4, width // 16, -1),
        6,
    )
    expert_sums = [
        lax.psum(g[None], "dp").astype(F32) for g in (grad_wgate, grad_wup, grad_wdown)
    ]
    return (
        mixed,
        grad_tokens,
        small_sum[:, 0],
        qkv_sum[:, :kv_at],
        qkv_sum[:, kv_at : kv_at + kv_width],
        qkv_sum[:, kv_at + kv_width :],
        wo_sum,
        small_sum[:, 1],
        small_sum[:, 2 : 2 + EXPERTS],
        expert_sums[0],
        expert_sums[1],
        expert_sums[2],
    )


def solution(mesh):
    whole = P(("dp", "expert"), None)
    over_dp, by_dp, over_expert = P("dp"), P("dp", None), P("expert", None, None)
    return jax.shard_map(
        on_device,
        mesh=mesh,
        in_specs=(whole, whole, over_dp, by_dp, by_dp, by_dp, by_dp, over_dp, by_dp)
        + (over_expert,) * 3
        + (whole, by_dp),
        out_specs=(whole, whole, over_dp, by_dp, by_dp, by_dp, by_dp, over_dp, by_dp)
        + (over_expert,) * 3,
        check_vma=False,
    )
```

time: 897 us -> 614 us (0.68)
  waiting for transfers between devices: 322 us -> 101 us
  Pallas kernels: 0 us -> 212 us
  local copies, waits for them, and re-layouts: 198 us -> 39.5 us
  blocking collectives: 93.4 us -> 11.7 us
  other arithmetic: 86.5 us -> 64.6 us
  starting transfers between devices: 11.7 us -> 0.35 us
    pallas_call x0 -> x6, Pallas kernels: none -> 212 us  [the longest x1 65.3 us: reduce_yz(): pl.pallas_call(functools.partial(reduce_yz_kernel, len(grads)), out_shape...]
    all_to_all x2 -> x0, blocking collectives: 93.4 us -> none  [the longest x1 47.2 us: on_device(): lax.all_to_all(outgoing, 'expert', split_axis=1, concat_axis=1, tiled=True)]
    unnamed x7 -> x4, waiting for transfers between devices: 85.5 us -> 0.75 us
    all_gather x2, waiting for transfers between devices: 83.9 us -> 0.01 us  [the longest x1 0.01 us: gather_dense(): got = lax.all_gather(mine, 'dp', axis=0, tiled=True)]
    concatenate x3 -> x4, local copies, waits for them, and re-layouts: 72 us -> 5.47 us  [the longest x1 2.95 us: on_device(): jnp.concatenate([p.astype(BF16) for p in key_parts + value_parts], axis=1)]
    all_to_all x2 -> x0, waiting for transfers between devices: 55.3 us -> none  [the longest x1 36.8 us: on_device(): lax.all_to_all(grad_rows, 'expert', split_axis=1, concat_axis=1, tiled=True)]
    gather x7 -> x0, local copies, waits for them, and re-layouts: 43.5 us -> none  [the longest x1 11 us: on_device(): pair_grads[source_pair] * occupied[:, None]]
    reduce_scatter x1, waiting for transfers between devices: 0.01 us -> 34.3 us  [rs_x(): return lax.psum_scatter(blocks, 'expert', scatter_dimension=0, tiled=True)]
  transfers between devices with their start and end apart: 8 -> 5, of which waited for: 6 -> 2; matrix products, arithmetic and copies ran while one was open for 23% -> 23% of each run, Pallas kernels for 0% -> 22%
where the time goes in v1:
time: 614 us; the launch traced here: 606 us
  Pallas kernels  212 us (35%)
  matrix products  161 us (26%)
  waiting for transfers between devices  101 us (16%)
  other arithmetic  64.6 us (11%)
  local copies, waits for them, and re-layouts  39.5 us (6%)
  between operations  15.5 us (3%)
  blocking collectives  11.7 us (2%)
    dot_general x20, matrix products, dot(): return lax.dot_general(a, b, (dims, ((), ())), preferred_element_type=F32)  77.2 us
    psum x1, waiting for transfers between devices, on_device(): lax.psum(g[None], 'dp').astype(F32)  65.6 us
    pallas_call x1, Pallas kernels, reduce_yz(): pl.pallas_call(functools.partial(reduce_yz_kernel, len(grads)), out_shape...  65.3 us
    pallas_call x2, Pallas kernels, gather_x(): pl.pallas_call(gather_x_kernel, out_shape=jax.ShapeDtypeStruct((8, *block...  59.3 us
    pallas_call x2, Pallas kernels, reduce_x(): pl.pallas_call(reduce_x_kernel, out_shape=jax.ShapeDtypeStruct((rows, col...  48.9 us
    pallas_call x1, Pallas kernels, gather_yz(): pl.pallas_call(gather_yz_kernel, out_shape=[jax.ShapeDtypeStruct((4, 4, *...  38.9 us
    reduce_scatter x1, waiting for transfers between devices, rs_x(): return lax.psum_scatter(blocks, 'expert', scatter_dimension=0, tiled=True)  34.3 us
    dot_general x2, matrix products, scores_for(): jnp.einsum('tgd,sd->gts', query[:, h], keys[:, h], preferred_element_type...  16.1 us
  transfers between devices with their start and end apart: 5, of which 2 were waited for; matrix products, arithmetic and copies ran while one was open for 23% of the time, Pallas kernels for 22%

profile of v1, /device:TPU:1, one launch (start us, length us, event | category | flops | bytes accessed | tf_op | source)
XLA Modules:
  0.0 605.6 jit_solution(542505466893491913)
XLA Ops:
  13.7 38.9 %shard_map.229 = (bf16[4,4,96,2048]{3,2,1,0:T(8,128)(2,1)}, bf16[4,4,96,128]{3,2,1,0:T(8,128)(2,1)}) custom-call(bf16[96,2048]{1,0:T(8,128)(2,1)} %pad_maximum_fusion.16.shard_ref, bf16[96,128]{1,0:T(8,128)(2,1)} %pad.8.small_ref), custom_call_target="tpu_custom_call" | custom-call | tf_op jit(solution)/shard_map/pallas_call | solution.py:365
  55.1 5.6 fusion.23
  69.1 2.3 copy.190
  76.0 26.2 %shard_map.230 = bf16[8,256,512]{2,1,0:T(8,128)(2,1)} custom-call(bf16[256,512]{1,0:T(8,128)(2,1)} %pad_maximum_fusion.17.block_ref), custom_call_target="tpu_custom_call" | custom-call | tf_op jit(solution)/shard_map/pallas_call | solution.py:175
  102.2 3.0 fusion.124
  108.1 8.0 %fusion.127 = (f32[6,256]{1,0:T(8,128)S(1)}, f32[6,256,2048]{1,2,0:T(8,128)}) fusion(bf16[256,2,6,128]{3,0,2,1:T(8,128)(2,1)} %bitcast.260, bf16[2048,2,128]{0,2,1:T(8,128)(2,1)} %bitcast.254, pred[256,2048]{0,1:T(8,128)(4,1)S(1)} %fusion.69), kind=kOutput, calls=%fused_computation.236 | convolution fusion | flops 814742016 | bytes 14030848 | tf_op jit(solution)/shard_map/tgd,sd->gts/dot_general | solution.py:613
  118.3 11.7 %all_gather.10 = bf16[2048,4]{0,1:T(4,128)(2,1)S(1)} all-gather(bf16[256,4]{0,1:T(4,128)(2,1)S(1)} %convert_element_type.240), channel_id=1, replica_groups=mesh['dp'=16,'expert'=8] {'expert'}, dimensions={0}, use_global_device_ids=true | all-gather | bytes 18432 | tf_op jit(solution)/shard_map/all_gather | solution.py:94
  130.0 8.1 %fusion.128 = (f32[6,256]{1,0:T(8,128)S(1)}, f32[6,256,2048]{1,2,0:T(8,128)}) fusion(bf16[256,2,6,128]{3,0,2,1:T(8,128)(2,1)} %bitcast.261, bf16[2048,2,128]{0,2,1:T(8,128)(2,1)} %bitcast.255, pred[256,2048]{0,1:T(8,128)(4,1)} %copy-done.36), kind=kOutput, calls=%fused_computation.237 | convolution fusion | flops 814742016 | bytes 14030848 | tf_op jit(solution)/shard_map/tgd,sd->gts/dot_general | solution.py:613
  139.9 6.9 %fusion.6 = f32[6,256]{1,0:T(8,128)} fusion(f32[6,256,2048]{1,2,0:T(8,128)} %get-tuple-element.121, f32[6,256]{1,0:T(8,128)S(1)} %get-tuple-element.120), kind=kLoop, calls=%fused_computation.18 | loop fusion | flops 6289920 | bytes 12595200 | tf_op jit(solution)/shard_map/reduce_sum | solution.py:621
  146.8 3.3 fusion.84
  155.5 7.1 %fusion.83 = bf16[256,1,6,128]{0,3,2,1:T(8,128)(2,1)S(1)} fusion(f32[6,256,2048]{1,2,0:T(8,128)} %get-tuple-element.121, f32[6,256]{1,0:T(8,128)} %fusion.6, f32[6,256]{1,0:T(8,128)} %copy-done.56, bf16[2048,2,128]{0,2,1:T(8,128)(2,1)} %bitcast.250), kind=kOutput, calls=%fused_computation.126 | convolution fusion | flops 814940160 | bytes 13516800 | tf_op jit(solution)/shard_map/gts,sd->tgd/dot_general | solution.py:624
  169.4 33.1 %shard_map.231 = bf16[8,256,1536]{2,1,0:T(8,128)(2,1)} custom-call(bf16[256,1536]{1,0:T(8,128)(2,1)} %multiply_convert_fusion.2.block_ref), custom_call_target="tpu_custom_call" | custom-call | tf_op jit(solution)/shard_map/pallas_call | solution.py:175
  202.5 4.6 fusion.106
  207.8 4.0 convolution_convert_fusion.6
  211.9 4.7 fusion.67
  216.7 4.7 fusion.63
  221.4 4.5 fusion.13
  226.3 5.6 multiply_convert_fusion
  231.9 4.6 fusion.34
  236.5 4.6 fusion.35
  241.1 5.6 fusion.14
  246.7 4.6 fusion.36
  251.4 6.5 %convolution_convert_fusion.3 = bf16[8,256,1536]{2,1,0:T(8,128)(2,1)} fusion(bf16[8,144,1536]{2,1,0:T(8,128)(2,1)} %bitcast.258, s32[8,256]{1,0:T(8,128)S(1)} %add_bitcast_fusion, pred[8,256]{1,0:T(8,128)(4,1)S(1)} %and.25), kind=kOutput, calls=%fused_computation.41 | convolution fusion | flops 909705216 | bytes 9840640 | tf_op jit(solution)/shard_map/prt,prd->ptd/dot_general | solution.py:657
  261.2 5.3 fusion.65
  266.6 3.5 fusion.10
  270.8 5.0 convolution_convert_fusion.4.blocks_ref
  275.8 34.2 %shard_map.232 = f32[256,1664]{1,0:T(8,128)S(1)} custom-call(bf16[8,256,1664]{2,1,0:T(8,128)(2,1)} %convolution_convert_fusion.4.blocks_ref), custom_call_target="tpu_custom_call" | custom-call | tf_op jit(solution)/shard_map/pallas_call | solution.py:243
  310.5 3.3 multiply_reduce_fusion
  315.2 65.6 %all-reduce.5.cloned.1.call-done = (bf16[1,1536,768]{2,1,0:T(8,128)(2,1)}, bf16[1,1536,768]{2,1,0:T(8,128)(2,1)}, bf16[1,768,1536]{2,1,0:T(8,128)(2,1)}) async-done(((bf16[1,1536,768]{2,1,0:T(8,128)(2,1)}, bf16[1,1536,768]{2,1,0:T(8,128)(2,1)}, bf16[1,768,1536]{2,1,0:T(8,128)(2,1)}), (bf16[1,1536,768]{2,1,0:T(8,128)(2,1)}, bf16[1,1536,768]{2,1,0:T(8,128)(2,1)}, ...) | async-done | bytes 7077904 | tf_op jit(solution)/shard_map/psum | solution.py:756
  380.8 4.4 convert_element_type.286
  385.2 2.5 convert_element_type.288
  387.8 2.8 convert_element_type.291
  390.6 34.3 %reduce-scatter.2.cloned.1.call-done = bf16[256,1536]{1,0:T(8,128)(2,1)} async-done(((bf16[2048,1536]{1,0:T(8,128)(2,1)}), bf16[256,1536]{1,0:T(8,128)(2,1)}) %reduce-scatter.2.cloned.1.call-update) | async-done | bytes 786448 | tf_op jit(solution)/shard_map/reduce_scatter | solution.py:98
  424.9 3.1 multiply_add_fusion
  430.9 7.0 %fusion.49 = bf16[2048,128]{0,1:T(8,128)(2,1)S(1)} fusion(f32[6,256,2048]{1,2,0:T(8,128)} %get-tuple-element.119, f32[6,256]{1,0:T(8,128)S(1)} %copy-done.41, bf16[256,2,6,128]{0,3,2,1:T(8,128)(2,1)S(1)} %bitcast.242), kind=kOutput, calls=%fused_computation.80 | convolution fusion | flops 811859968 | bytes 13508608 | tf_op jit(solution)/shard_map/gts,tgd->sd/dot_general | solution.py:725
  437.9 8.9 %fusion = (f32[6,256]{1,0:T(8,128)S(1)}, f32[2048,256,6]{1,0,2:T(8,128)}) fusion(f32[6,256,2048]{1,2,0:T(8,128)} %get-tuple-element.119, f32[6,256]{1,0:T(8,128)S(1)} %copy-done.41, bf16[256,2,6,128]{0,3,2,1:T(8,128)(2,1)S(1)} %bitcast.243, bf16[2048,2,128]{0,2,1:T(8,128)(2,1)S(1)} %bitcast.252), kind=kOutput, calls=%fused_computation.2 | convolution fusion | flops 814742016 | bytes 26097664 | tf_op jit(solution)/shard_map/tgd,sd->gts/dot_general | solution.py:723
  449.2 6.0 fusion.3
  455.2 9.1 %fusion.2 = bf16[6,256,2048]{1,2,0:T(8,128)(2,1)} fusion(f32[2048,256,6]{1,0,2:T(8,128)} %get-tuple-element.128, f32[6,256,2048]{1,2,0:T(8,128)S(1)} %bitcast.225, f32[6,256]{1,0:T(8,128)S(1)} %get-tuple-element.127, f32[6,256]{1,0:T(8,128)S(1)} %copy-done.41), kind=kLoop, calls=%fused_computation.4 | loop fusion | flops 12582912 | bytes 31469568 | tf_op jit(solution)/shard_map/convert_element_type | solution.py:728
  464.3 5.0 fusion.48
  469.2 6.2 %fusion.5 = bf16[6,256,2048]{1,2,0:T(8,128)(2,1)S(1)} fusion(f32[2048,256,6]{1,0,2:T(8,128)} %get-tuple-element.130, f32[6,256,2048]{1,2,0:T(8,128)S(1)} %bitcast.227, f32[6,256]{1,0:T(8,128)S(1)} %get-tuple-element.129, f32[6,256]{1,0:T(8,128)S(1)} %log_add_fusion.1), kind=kLoop, calls=%fused_computation.9 | loop fusion | flops 12582912 | bytes 31469568 | tf_op jit(solution)/shard_map/convert_element_type | solution.py:728
  479.6 2.9 copy.215
  482.5 14.6 %shard_map.233 = f32[256,512]{1,0:T(8,128)S(1)} custom-call(bf16[8,256,512]{2,1,0:T(8,128)(2,1)S(1)} %bitcast.221), custom_call_target="tpu_custom_call" | custom-call | tf_op jit(solution)/shard_map/pallas_call | solution.py:243
  497.2 3.9 fusion.79
  506.6 6.1 %fusion.75 = (bf16[1536]{0:T(1024)(128)(2,1)S(1)}, f32[256]{0:T(256)S(1)}, f32[256,1536]{1,0:T(8,128)}) fusion(bf16[256,1536]{1,0:T(8,128)(2,1)S(1)} %copy-done.13, f32[256]{0:T(256)S(1)} %copy-done.64, f32[1536]{0:T(1024)S(1)} %copy-done.50, bf16[1536,2048]{1,0:T(8,128)(2,1)} %bitcast.282, bf16[256,256]{0,1:T(8,128)(2,1)S(1)} %copy.218, ...), kind=kOutput, calls=%fused_computation.109 | convolution fusion | flops 1616509184 | bytes 9710592 | tf_op jit(solution)/shard_map/dot_general | solution.py:29
  512.7 4.6 convolution_convert_fusion
  517.3 3.6 convolution_convert_fusion.1
  522.1 65.3 %shard_map.234 = (f32[96,2048]{1,0:T(8,128)}, f32[96,1536]{1,0:T(8,128)}, f32[96,128]{1,0:T(8,128)}) custom-call(bf16[4,4,96,2048]{3,2,1,0:T(8,128)(2,1)} %bitcast.229, bf16[4,4,96,1536]{3,2,1,0:T(8,128)(2,1)} %bitcast.230, bf16[4,4,96,128]{3,2,1,0:T(8,128)(2,1)} %bitcast.266), custom_call_target="tpu_custom_call" | custom-call | tf_op jit(solution)/shard_map/pallas_call | solution.py:536
  594.3 3.5 fusion.74
  (296 shorter events, 71.0 us)
Async XLA Ops:
  7.2 218.8 %copy-start = (bf16[1,768,1536]{2,1,0:T(8,128)(2,1)S(1)}, bf16[1,768,1536]{2,1,0:T(8,128)(2,1)}, u32[]{:S(2)}) copy-start(bf16[1,768,1536]{2,1,0:T(8,128)(2,1)} %param.25) | copy-start | bytes 7077892
  7.2 47.7 %copy-start.12 = (bf16[256,1536]{1,0:T(8,128)(2,1)S(1)}, bf16[256,1536]{1,0:T(8,128)(2,1)}, u32[]{:S(2)}) copy-start(bf16[256,1536]{1,0:T(8,128)(2,1)} %param.14) | copy-start | bytes 2359300
  7.2 142.9 %all-gather.3.cloned.1.call-start = ((), (), s32[]{:S(2)}) async-start(), calls=%async_computation.1 | async-start | bytes 2506752 | tf_op jit(solution)/shard_map/all_gather | solution.py:86
  9.1 212.3 %all-gather.5.cloned.1.call-start = ((), (), s32[]{:S(2)}) async-start(), calls=%async_computation.3 | async-start | bytes 7077888 | tf_op jit(solution)/shard_map/all_gather | solution.py:94
  9.8 371.0 %all-reduce.5.cloned.1.call-start = ((), (), s32[]{:S(2)}) async-start(), calls=%async_computation.4 | async-start | bytes 14155776 | tf_op jit(solution)/shard_map/psum | solution.py:756
  54.9 5.9 copy-start.49
  55.1 5.6 copy-start.63
  66.5 7.4 %copy-start.29 = (f32[256,64]{1,0:T(8,128)}, f32[256,64]{1,0:T(8,128)S(1)}, u32[]{:S(2)}) copy-start(f32[256,64]{1,0:T(8,128)S(1)} %copy.184) | copy-start | bytes 196612
  108.0 8.0 %copy-start.36 = (pred[256,2048]{0,1:T(8,128)(4,1)}, pred[256,2048]{0,1:T(8,128)(4,1)S(1)}, u32[]{:S(2)}) copy-start(pred[256,2048]{0,1:T(8,128)(4,1)S(1)} %fusion.69) | copy-start | bytes 1572868
  108.1 10.3 %copy-start.51 = (s32[256,4]{0,1:T(4,128)S(1)}, s32[256,4]{0,1:T(4,128)}, u32[]{:S(2)}) copy-start(s32[256,4]{0,1:T(4,128)} %param.26) | copy-start | bytes 12292
  116.0 22.1 %copy-start.53 = (f32[6,256]{1,0:T(8,128)}, f32[6,256]{1,0:T(8,128)S(1)}, u32[]{:S(2)}) copy-start(f32[6,256]{1,0:T(8,128)S(1)} %get-tuple-element.118) | copy-start | bytes 18436
  118.3 19.8 %slice-start = ((s8[12582912]{0:T(1024)(128)(4,1)}), s8[4194304]{0:T(1024)(128)(4,1)S(1)}, s32[]{:S(2)}) async-start(s8[12582912]{0:T(1024)(128)(4,1)} %bitcast.222), calls=%async_computation.5 | async-start | bytes 8388608
  130.0 20.9 %copy-start.39 = (bf16[2048,4]{0,1:T(4,128)(2,1)}, bf16[2048,4]{0,1:T(4,128)(2,1)S(1)}, u32[]{:S(2)}) copy-start(bf16[2048,4]{0,1:T(4,128)(2,1)S(1)} %all_gather.10) | copy-start | bytes 49156
  130.0 8.1 %slice-start.1 = ((s8[12582912]{0:T(1024)(128)(4,1)}), s8[4194304]{0:T(1024)(128)(4,1)S(1)}, s32[]{:S(2)}) async-start(s8[12582912]{0:T(1024)(128)(4,1)} %bitcast.222), calls=%async_computation.6 | async-start | bytes 8388608
  130.0 8.2 %slice-start.2 = ((s8[12582912]{0:T(1024)(128)(4,1)}), s8[4194304]{0:T(1024)(128)(4,1)S(1)}, s32[]{:S(2)}) async-start(s8[12582912]{0:T(1024)(128)(4,1)} %bitcast.222), calls=%async_computation.7 | async-start | bytes 8388608
  139.9 6.9 %copy-start.59 = (f32[6,256]{1,0:T(8,128)}, f32[6,256]{1,0:T(8,128)S(1)}, u32[]{:S(2)}) copy-start(f32[6,256]{1,0:T(8,128)S(1)} %fusion.7) | copy-start | bytes 18436
  139.9 6.9 %copy-start.16 = (bf16[2048,256]{0,1:T(8,128)(2,1)S(1)}, bf16[2048,256]{0,1:T(8,128)(2,1)}, u32[]{:S(2)}) copy-start(bf16[2048,256]{0,1:T(8,128)(2,1)} %copy.186) | copy-start | bytes 3145732
  139.9 6.9 %copy-start.54 = (f32[6,256]{1,0:T(8,128)S(1)}, f32[6,256]{1,0:T(8,128)}, u32[]{:S(2)}) copy-start(f32[6,256]{1,0:T(8,128)} %copy-done.53) | copy-start | bytes 18436
  146.8 6.1 %copy-start.28 = (bf16[1536,1]{1,0:T(8,128)(2,1)S(1)}, bf16[1536,1]{1,0:T(8,128)(2,1)}, u32[]{:S(2)}) copy-start(bf16[1536,1]{1,0:T(8,128)(2,1)} %get-tuple-element.113) | copy-start | bytes 9220
  150.1 12.7 %collective-permute-start = (bf16[1536,768]{1,0:T(8,128)(2,1)}, bf16[1536,768]{1,0:T(8,128)(2,1)}, u32[]{:S(2)}, u32[]{:S(2)}) collective-permute-start(bf16[1536,768]{1,0:T(8,128)(2,1)} %all-gather.3.cloned.1.call-done), channel_id=1, source_target_pairs={{0,1},{1,0},{2,3},{3,2},{4,5},{5,4},{6,7},{7,6},{8,9},{9,8},{10,11... | collective-permute-start | bytes 7077896 | tf_op jit(solution)/shard_map/ppermute | solution.py:80
  152.9 98.4 %copy-start.42 = (pred[8,256]{1,0:T(8,128)(4,1)}, pred[8,256]{1,0:T(8,128)(4,1)S(1)}, u32[]{:S(2)}) copy-start(pred[8,256]{1,0:T(8,128)(4,1)S(1)} %and.25) | copy-start | bytes 6148
  155.4 11.8 %copy-start.44 = (f32[1536]{0:T(1024)}, f32[1536]{0:T(1024)S(1)}, u32[]{:S(2)}) copy-start(f32[1536]{0:T(1024)S(1)} %convert_reduce_fusion.1) | copy-start | bytes 18436
  155.5 7.2 %copy-start.38 = (bf16[256,1,6,128]{0,3,2,1:T(8,128)(2,1)S(1)}, bf16[256,1,6,128]{0,3,2,1:T(8,128)(2,1)}, u32[]{:S(2)}) copy-start(bf16[256,1,6,128]{0,3,2,1:T(8,128)(2,1)} %fusion.84) | copy-start | bytes 1179652
  155.5 7.3 %copy-start.27 = (bf16[1536,768]{1,0:T(8,128)(2,1)S(1)}, bf16[1536,768]{1,0:T(8,128)(2,1)}, u32[]{:S(2)}) copy-start(bf16[1536,768]{1,0:T(8,128)(2,1)} %all-gather.3.cloned.1.call-done) | copy-start | bytes 7077892
  169.4 33.1 %copy-start.11 = (bf16[4,4,96,128]{3,2,1,0:T(8,128)(2,1)S(1)}, bf16[4,4,96,128]{3,2,1,0:T(8,128)(2,1)}, u32[]{:S(2)}) copy-start(bf16[4,4,96,128]{3,2,1,0:T(8,128)(2,1)} %get-tuple-element.17) | copy-start | bytes 1179652
  202.5 4.8 copy-start.40
  211.9 4.8 copy-start.9
  211.9 4.7 copy-start.70
  221.4 4.9 copy-start.74
  226.3 5.6 copy-start.10
  251.3 173.6 %reduce-scatter.2.cloned.1.call-start = ((), (), s32[]{:S(2)}) async-start(), calls=%async_computation.2 | async-start | bytes 7077888 | tf_op jit(solution)/shard_map/reduce_scatter | solution.py:98
  261.2 5.4 copy-start.71
  261.2 5.3 copy-start.76
  275.8 34.7 %copy-start.45 = (f32[1536]{0:T(1024)S(1)}, f32[1536]{0:T(1024)}, u32[]{:S(2)}) copy-start(f32[1536]{0:T(1024)} %copy-done.44) | copy-start | bytes 18436
  275.8 34.7 %copy-start.66 = (f32[256]{0:T(256)S(1)}, f32[256]{0:T(256)}, u32[]{:S(2)}) copy-start(f32[256]{0:T(256)} %copy-done.65) | copy-start | bytes 3076
  387.8 37.1 %copy-start.5 = (f32[256,1536]{1,0:T(8,128)S(1)}, f32[256,1536]{1,0:T(8,128)}, u32[]{:S(2)}) copy-start(f32[256,1536]{1,0:T(8,128)} %copy-done.4) | copy-start | bytes 4718596
  387.8 37.1 %copy-start.20 = (bf16[256,1536]{1,0:T(8,128)(2,1)S(1)}, bf16[256,1536]{1,0:T(8,128)(2,1)}, u32[]{:S(2)}) copy-start(bf16[256,1536]{1,0:T(8,128)(2,1)} %param.15) | copy-start | bytes 2359300
  387.8 37.1 %copy-start.67 = (f32[256]{0:T(256)S(1)}, f32[256]{0:T(256)}, u32[]{:S(2)}) copy-start(f32[256]{0:T(256)} %copy-done.65) | copy-start | bytes 3076
  430.9 7.0 %copy-start.17 = (bf16[2048,256]{0,1:T(8,128)(2,1)S(1)}, bf16[2048,256]{0,1:T(8,128)(2,1)}, u32[]{:S(2)}) copy-start(bf16[2048,256]{0,1:T(8,128)(2,1)} %copy.186) | copy-start | bytes 3145732
  430.9 16.0 %slice-start.6 = ((s8[12582912]{0:T(1024)(128)(4,1)}), s8[4194304]{0:T(1024)(128)(4,1)S(1)}, s32[]{:S(2)}) async-start(s8[12582912]{0:T(1024)(128)(4,1)} %bitcast.226), calls=%async_computation.11 | async-start | bytes 8388608
  430.9 15.9 %slice-start.7 = ((s8[12582912]{0:T(1024)(128)(4,1)}), s8[4194304]{0:T(1024)(128)(4,1)S(1)}, s32[]{:S(2)}) async-start(s8[12582912]{0:T(1024)(128)(4,1)} %bitcast.226), calls=%async_computation.12 | async-start | bytes 8388608
  437.9 8.9 %slice-start.8 = ((s8[12582912]{0:T(1024)(128)(4,1)}), s8[4194304]{0:T(1024)(128)(4,1)S(1)}, s32[]{:S(2)}) async-start(s8[12582912]{0:T(1024)(128)(4,1)} %bitcast.226), calls=%async_computation.13 | async-start | bytes 8388608
  446.9 8.3 %slice-start.3 = ((s8[12582912]{0:T(1024)(128)(4,1)}), s8[4194304]{0:T(1024)(128)(4,1)S(1)}, s32[]{:S(2)}) async-start(s8[12582912]{0:T(1024)(128)(4,1)} %bitcast.224), calls=%async_computation.8 | async-start | bytes 8388608
  446.9 8.3 %slice-start.4 = ((s8[12582912]{0:T(1024)(128)(4,1)}), s8[4194304]{0:T(1024)(128)(4,1)S(1)}, s32[]{:S(2)}) async-start(s8[12582912]{0:T(1024)(128)(4,1)} %bitcast.224), calls=%async_computation.9 | async-start | bytes 8388608
  449.2 6.0 slice-start.5
  455.2 9.1 %copy-start.19 = (bf16[256,12,128]{2,0,1:T(8,128)(2,1)S(1)}, bf16[256,12,128]{2,0,1:T(8,128)(2,1)}, u32[]{:S(2)}) copy-start(bf16[256,12,128]{2,0,1:T(8,128)(2,1)} %copy.190) | copy-start | bytes 2359300
  479.6 17.6 %copy-start.18 = (bf16[2048,256]{0,1:T(8,128)(2,1)S(1)}, bf16[2048,256]{0,1:T(8,128)(2,1)}, u32[]{:S(2)}) copy-start(bf16[2048,256]{0,1:T(8,128)(2,1)} %copy.243) | copy-start | bytes 3145732
  589.4 9.2 %copy-start.1 = (bf16[1,768,1536]{2,1,0:T(8,128)(2,1)S(1)}, bf16[1,768,1536]{2,1,0:T(8,128)(2,1)}, u32[]{:S(2)}) copy-start(bf16[1,768,1536]{2,1,0:T(8,128)(2,1)} %param.25) | copy-start | bytes 7077892
  (43 other events, 120.5 us)
Sparse Core Ops, SparseCore 0:
  10.8 49.0 all-gather.2
  61.6 49.8 all-gather.4
  251.4 129.3 all-reduce.4
  383.2 41.5 reduce-scatter.1

commit v2 on v1

v2 whole, which is shorter than its diff:
```python
import functools

import jax
import jax.numpy as jnp
from jax import lax
from jax.experimental import pallas as pl
from jax.experimental.pallas import tpu as pltpu
from jax.sharding import PartitionSpec as P

QUERY_HEADS = 12
KEY_VALUE_HEADS = 2
HEAD_SIZE = 128
TOPK = 4
EXPERTS = 8
DOCS = 4
GROUP = QUERY_HEADS // KEY_VALUE_HEADS

EPSILON = 1e-06
ROPE_BASE = 1000000.0
MASK_FILL = -1e30
F32 = jnp.float32
BF16 = jnp.bfloat16

PARTNER = [(i, i ^ 1) for i in range(8)]
SAME_CORE = [[0, 2, 4, 6], [1, 3, 5, 7]]


def dot(a, b, dims):
    return lax.dot_general(a, b, (dims, ((), ())), preferred_element_type=F32)


def mm(a, b):
    return dot(a, b, ((1,), (0,)))


def mm_nt(a, b):
    return dot(a, b, ((1,), (1,)))


def mm_tn(a, b):
    return dot(a, b, ((0,), (0,)))


def rms_back(value_rows, gain, grad):
    inverse = lax.rsqrt(jnp.mean(value_rows * value_rows, axis=-1, keepdims=True) + EPSILON)
    scaled = value_rows * inverse
    weighted = grad * gain
    inner = jnp.mean(weighted * scaled, axis=-1, keepdims=True)
    return inverse * (weighted - scaled * inner), jnp.sum(grad * scaled, axis=0)


def angles_for(positions):
    half_width = HEAD_SIZE // 2
    freqs = ROPE_BASE ** (-2.0 * jnp.arange(half_width, dtype=F32) / HEAD_SIZE)
    return positions.astype(F32)[:, None] * freqs[None, :]


def rotate(flat, cosine, sine):
    heads = flat.reshape(flat.shape[0], -1, HEAD_SIZE)
    turned = jnp.roll(heads, HEAD_SIZE // 2, axis=-1)
    return (heads * cosine[:, None, :] + turned * sine[:, None, :]).reshape(flat.shape)


def pp_core(x):
    return lax.ppermute(x, "expert", PARTNER)


def gather_dense(shard, core):
    half = shard.shape[1] // 2
    mine = lax.dynamic_slice_in_dim(shard, core * half, half, 1)
    got = lax.all_gather(mine, "dp", axis=0, tiled=True)
    other = pp_core(got)
    first = jnp.where(core == 0, got, other)
    second = jnp.where(core == 0, other, got)
    return jnp.concatenate([first, second], axis=1)


MESH = pl.DeviceIdType.MESH
ANY = pl.BlockSpec(memory_space=pl.ANY)
VMEM = pl.BlockSpec(memory_space=pltpu.VMEM)


class Sends:
    def __init__(self, send_sems, recv_sems):
        self.send_sems, self.recv_sems, self.made = send_sems, recv_sems, []

    def start(self, src, dst, to):
        at = len(self.made)
        copy = pltpu.make_async_remote_copy(
            src_ref=src,
            dst_ref=dst,
            send_sem=self.send_sems.at[at],
            recv_sem=self.recv_sems.at[at],
            device_id=to,
            device_id_type=MESH,
        )
        copy.start()
        self.made.append(copy)
        return copy

    def finish(self):
        for copy in self.made:
            copy.wait_send()


def meet(*others):
    barrier = pltpu.get_barrier_semaphore()
    for other in others:
        pl.semaphore_signal(barrier, inc=1, device_id=other, device_id_type=MESH)
    pl.semaphore_wait(barrier, len(others))


def around_x():
    part = lax.axis_index("expert")
    x, core = part // 2, part % 2
    at = lambda dx: ((x + dx) % 4) * 2 + core
    return part, core, at(1), at(3), at(2), 2 * x + (1 - core)


def x_sum(sends, blocks_ref, out_ref, mine, theirs, total, from_left, from_right, local_sems):
    part, core, right, left, far, partner = around_x()
    to = lambda i: {"expert": i}
    rows = out_ref.shape[0]
    half = rows // 2
    low, high = pl.ds(0, half), pl.ds(half, half)
    order = (far, right, left, part)
    flip = 1 - 2 * core
    swaps, loads = [], []
    for k, dest in enumerate(order):
        swaps.append(sends.start(blocks_ref.at[dest + flip], theirs.at[k], to(partner)))
        load = pltpu.make_async_copy(blocks_ref.at[dest], mine.at[k], local_sems.at[k])
        load.start()
        loads.append(load)

    def add_up(k):
        loads[k].wait()
        swaps[k].wait_recv()
        total[k] = (mine[k].astype(F32) + theirs[k].astype(F32)).astype(BF16)

    yield
    add_up(0)
    far_low = sends.start(total.at[0, low], from_left.at[0], to(right))
    far_high = sends.start(total.at[0, high], from_right.at[0], to(left))
    add_up(1)
    right_high = sends.start(total.at[1, high], from_left.at[2], to(right))
    add_up(2)
    left_low = sends.start(total.at[2, low], from_right.at[2], to(left))
    yield
    far_low.wait_recv()
    total[1, low] = (total[1, low].astype(F32) + from_left[0].astype(F32)).astype(BF16)
    right_low = sends.start(total.at[1, low], from_left.at[1], to(right))
    far_high.wait_recv()
    total[2, high] = (total[2, high].astype(F32) + from_right[0].astype(F32)).astype(BF16)
    left_high = sends.start(total.at[2, high], from_right.at[1], to(left))
    yield
    loads[3].wait()
    swaps[3].wait_recv()
    out_ref[...] = mine[3].astype(F32) + theirs[3].astype(F32)
    right_high.wait_recv()
    out_ref[high] += from_left[2].astype(F32)
    left_low.wait_recv()
    out_ref[low] += from_right[2].astype(F32)
    right_low.wait_recv()
    out_ref[low] += from_left[1].astype(F32)
    left_high.wait_recv()
    out_ref[high] += from_right[1].astype(F32)
    yield


def x_buffers(rows, columns):
    return [
        pltpu.VMEM((4, rows, columns), BF16),
        pltpu.VMEM((4, rows, columns), BF16),
        pltpu.VMEM((3, rows, columns), BF16),
        pltpu.VMEM((3, rows // 2, columns), BF16),
        pltpu.VMEM((3, rows // 2, columns), BF16),
        pltpu.SemaphoreType.DMA((4,)),
    ]


def reduce_x_kernel(blocks_ref, out_ref, *refs):
    part, core, right, left, far, partner = around_x()
    meet(*({"expert": i} for i in (partner, right, left)))
    sends = Sends(*refs[-2:])
    for _ in x_sum(sends, blocks_ref, out_ref, *refs[:-2]):
        pass
    sends.finish()


def reduce_x(blocks, collective_id):
    _, rows, columns = blocks.shape
    return pl.pallas_call(
        reduce_x_kernel,
        out_shape=jax.ShapeDtypeStruct((rows, columns), F32),
        in_specs=[ANY],
        out_specs=VMEM,
        scratch_shapes=[
            *x_buffers(rows, columns),
            pltpu.SemaphoreType.DMA((10,)),
            pltpu.SemaphoreType.DMA((10,)),
        ],
        compiler_params=pltpu.CompilerParams(
            collective_id=collective_id, has_side_effects=True, vmem_limit_bytes=50 * 2**20
        ),
    )(blocks)


def around_yz():
    place = lax.axis_index("dp")
    y, z = place // 4, place % 4
    turn = lambda v, d: (v + d) % 4
    y_ring = [turn(y, d) for d in (1, 3, 2)]
    z_ring = [turn(z, d) for d in (1, 3, 2)]
    return y, z, y_ring, z_ring


class Strip:
    def __init__(self, source, cols, theirs_cols, y_first, bufs):
        self.source, self.cols, self.theirs_cols, self.y_first = source, cols, theirs_cols, y_first
        self.total, self.theirs, self.big, self.far, self.mid, self.midfar, self.near = bufs


def strip_buffers(rows, columns):
    return [
        pltpu.VMEM((4, 4, rows, columns), BF16),
        pltpu.VMEM((4, 4, rows, columns), BF16),
        pltpu.VMEM((2, 2, 2, rows, columns), BF16),
        pltpu.VMEM((2, 2, rows, columns), BF16),
        pltpu.VMEM((2, 2, rows // 2, columns), BF16),
        pltpu.VMEM((2, rows // 2, columns), BF16),
        pltpu.VMEM((4, rows, columns), BF16),
    ]


def reduce_all_kernel(
    qkv_ref, wo_ref, small_ref, middle_ref, blocks_ref,
    wq_out, wk_out, wv_out, wo_out, small_out, mixed_out, *refs,
):
    grads, outs = (qkv_ref, wo_ref), (None, wo_out)
    bufs, x_bufs = refs[:35], refs[35:41]
    combined, local_sems, send_sems, recv_sems = refs[41:]
    y, z, y_ring, z_ring = around_yz()
    part, core, x_right, x_left, x_far, partner = around_x()
    partner = {"expert": partner}
    x_to = [{"expert": i} for i in (x_right, x_left, x_far)]
    y_to = [{"dp": v * 4 + z} for v in y_ring[:2]]
    z_to = [{"dp": y * 4 + v} for v in z_ring[:2]]
    meet(partner, *y_to, *z_to, *x_to)
    sends = Sends(send_sems, recv_sems)
    strips, owners = [], []
    for g, out in zip(grads, outs):
        quarter = g.shape[-1] // 4
        for p in range(2):
            cols = [
                pl.ds(pl.multiple_of((2 * c + p) * quarter, 128), quarter)
                for c in (core, 1 - core)
            ]
            at = 7 * len(strips)
            strips.append(Strip(g, cols[0], cols[1], p == 0, bufs[at : at + 7]))
            owners.append(out)
    at = 7 * len(strips)
    every = pl.ds(0, small_ref.shape[-1])
    strips.append(Strip(small_ref, every, None, True, bufs[at : at + 7]))
    owners.append(small_out)

    def ring(s, first):
        return (y, y_ring, y_to) if s.y_first == first else (z, z_ring, z_to)

    def block(ref, s, w):
        return ref.at[w] if s.y_first else ref.at[:, w]

    def columns(s, w, cols):
        return s.source.at[w, :, :, cols] if s.y_first else s.source.at[:, w, :, cols]

    def add(ref, *others):
        got = ref[...].astype(F32)
        for other in others:
            got += other[...].astype(F32)
        ref[...] = got.astype(BF16)

    x_steps = x_sum(sends, blocks_ref, combined, *x_bufs)

    swaps, loads = {}, {}
    for k in range(4):
        if k == 1:
            next(x_steps)
        for i, s in enumerate(strips):
            me, (right, left, far), _ = ring(s, True)
            w = (far, right, left, me)[k]
            if s.theirs_cols is not None:
                swaps[k, i] = sends.start(
                    columns(s, w, s.theirs_cols), block(s.theirs, s, w), partner
                )
            load = pltpu.make_async_copy(
                columns(s, w, s.cols), block(s.total, s, w), local_sems.at[k * len(strips) + i]
            )
            load.start()
            loads[k, i] = load

    def joined(k, i, s, w):
        loads[k, i].wait()
        if s.theirs_cols is not None:
            swaps[k, i].wait_recv()
            add(block(s.total, s, w), block(s.theirs, s, w))

    def ring_sum(first, view, whole, farther, ready):
        going = []
        for i, s in enumerate(strips):
            _, (right, left, far), to = ring(s, first)
            ready(0, i, s, far)
            going.append(
                [sends.start(view(s, far, h), farther(s).at[h], to[h]) for h in range(2)]
            )
        for i, s in enumerate(strips):
            _, (right, left, far), to = ring(s, first)
            ready(1, i, s, right)
            ready(2, i, s, left)
            going[i].append(sends.start(view(s, right, 1), whole(s).at[0, 1], to[0]))
            going[i].append(sends.start(view(s, left, 0), whole(s).at[1, 0], to[1]))
        next(x_steps)
        for i, s in enumerate(strips):
            _, (right, left, far), to = ring(s, first)
            for h, w in enumerate((right, left)):
                going[i][h].wait_recv()
                add(view(s, w, h), farther(s).at[h])
                going[i].append(sends.start(view(s, w, h), whole(s).at[h, h], to[h]))
        for i, s in enumerate(strips):
            me, _, _ = ring(s, first)
            ready(3, i, s, me)
            for copy in going[i][2:]:
                copy.wait_recv()
            for h in range(2):
                add(view(s, me, h), whole(s).at[0, h], whole(s).at[1, h])

    def big(s, w, h):
        span = pl.ds(2 * h, 2)
        return s.total.at[w, span] if s.y_first else s.total.at[span, w]

    def small(s, w, h):
        half = s.total.shape[2] // 2
        at = pl.ds(h * half, half)
        return s.total.at[y, w, at] if s.y_first else s.total.at[w, z, at]

    ring_sum(True, big, lambda s: s.big, lambda s: s.far, joined)
    ring_sum(False, small, lambda s: s.mid, lambda s: s.midfar, lambda *_: None)

    shares, back = [], []
    for s in strips:
        shares.append(
            [sends.start(s.total.at[y, z], s.near.at[i], x_to[i]) for i in range(3)]
        )
    next(x_steps)
    mixed_out[...] = (middle_ref[...] + combined[...]).astype(BF16)
    for s, share in zip(strips, shares):
        for copy in share:
            copy.wait_recv()
        got = s.total[y, z].astype(F32)
        for i in range(3):
            got += s.near[i].astype(F32)
        s.theirs[y, z] = got.astype(BF16)
        back.append(sends.start(s.theirs.at[y, z], s.near.at[3], partner))
    wide, narrow = wq_out.shape[1] // 4, wk_out.shape[1] // 2
    for i, (s, out, copy) in enumerate(zip(strips, owners, back)):
        copy.wait_recv()
        if s.theirs_cols is None:
            out[...] = s.theirs[y, z].astype(F32) + s.near[3].astype(F32)
            continue
        for c, got in ((core, s.theirs[y, z]), (1 - core, s.near[3])):
            got = got.astype(F32)
            if out is not None:
                out[:, s.cols if c is core else s.theirs_cols] = got
                continue
            at = pl.multiple_of((2 * c + i) * wide, 128)
            wq_out[:, pl.ds(at, wide)] = got[:, :wide]
            other = wk_out if i == 0 else wv_out
            other[:, pl.ds(pl.multiple_of(c * narrow, 128), narrow)] = got[:, wide:]
    sends.finish()


def reduce_all(grad_qkv, grad_wo, small, middle, blocks, narrow, collective_id):
    height = small.shape[2]
    width = grad_wo.shape[3]
    rows = middle.shape[0]
    buffers = []
    for g in (grad_qkv, grad_wo):
        for _ in range(2):
            buffers += strip_buffers(height, g.shape[3] // 4)
    buffers += strip_buffers(*small.shape[2:])
    sds = jax.ShapeDtypeStruct
    return pl.pallas_call(
        reduce_all_kernel,
        out_shape=[
            sds((height, width), F32),
            sds((height, narrow), F32),
            sds((height, narrow), F32),
            sds((height, width), F32),
            sds(small.shape[2:], F32),
            sds(middle.shape, BF16),
        ],
        in_specs=[ANY, ANY, ANY, VMEM, ANY],
        out_specs=[VMEM] * 6,
        scratch_shapes=[
            *buffers,
            *x_buffers(rows, width),
            pltpu.VMEM((rows, width), F32),
            pltpu.SemaphoreType.DMA((20,)),
            pltpu.SemaphoreType.DMA((110,)),
            pltpu.SemaphoreType.DMA((110,)),
        ],
        compiler_params=pltpu.CompilerParams(
            collective_id=collective_id, has_side_effects=True, vmem_limit_bytes=60 * 2**20
        ),
    )(grad_qkv, grad_wo, small, middle, blocks)


def gather_first_kernel(
    wq_ref, wk_ref, wv_ref, small_ref, rows_ref, note_ref,
    out_ref, small_out, rows_out, notes_out, local_sems, send_sems, recv_sems,
):
    y, z, y_ring, z_ring = around_yz()
    part, core, x_right, x_left, x_far, partner = around_x()
    others = [{"expert": lax.rem(part + d, 8)} for d in range(1, 8)]
    partner, x_right_to, x_left_to = ({"expert": i} for i in (partner, x_right, x_left))
    y_to = [{"dp": v * 4 + z} for v in y_ring[:2]]
    z_to = [{"dp": y * 4 + v} for v in z_ring[:2]]
    meet(*others, *y_to, *z_to)
    rows = wq_ref.shape[0]
    wide, narrow = wq_ref.shape[1] // 4, wk_ref.shape[1] // 2
    sends = Sends(send_sems, recv_sems)
    local = []

    def keep(src, dst):
        copy = pltpu.make_async_copy(src, dst, local_sems.at[len(local)])
        copy.start()
        local.append(copy)

    def columns(p, at, size):
        begin = (2 * core + p) * (wide + narrow) + at
        return pl.ds(pl.multiple_of(begin, 128), size)

    for p, other in enumerate((wk_ref, wv_ref)):
        begin = pl.multiple_of((2 * core + p) * wide, 128)
        keep(wq_ref.at[:, pl.ds(begin, wide)], out_ref.at[y, z, :, columns(p, 0, wide)])
        begin = pl.multiple_of(core * narrow, 128)
        keep(other.at[:, pl.ds(begin, narrow)], out_ref.at[y, z, :, columns(p, wide, narrow)])
    keep(small_ref, small_out.at[y, z])
    keep(rows_ref, rows_out.at[part])
    keep(note_ref, notes_out.at[part])

    half = rows_ref.shape[0] // 2
    x_ways = (x_right_to, x_left_to)
    x_came = [sends.start(rows_ref, rows_out.at[part], to) for to in x_ways]
    across = [sends.start(rows_ref, rows_out.at[part], partner)]
    across += [sends.start(note_ref, notes_out.at[part], to) for to in others]

    class Piece:
        def __init__(self, out, cols, z_first):
            self.out, self.cols, self.z_first = out, cols, z_first

        def ring(self, first):
            if self.z_first == first:
                return z, z_ring, z_to
            return y, y_ring, y_to

        def view(self, first, where, piece=None):
            if first:
                at = pl.ds(0, rows) if piece is None else pl.ds(piece * rows // 2, rows // 2)
                if self.z_first:
                    return self.out.at[y, where, at, self.cols]
                return self.out.at[where, z, at, self.cols]
            span = pl.ds(0, 4) if piece is None else pl.ds(2 * piece, 2)
            if self.z_first:
                return self.out.at[where, span, :, self.cols]
            return self.out.at[span, where, :, self.cols]

    pieces = [
        Piece(out_ref, columns(0, 0, wide + narrow), True),
        Piece(out_ref, columns(1, 0, wide + narrow), False),
        Piece(small_out, pl.ds(0, small_ref.shape[1]), True),
    ]

    def send_across(s, view):
        if s.out is out_ref:
            across.append(sends.start(view, view, partner))

    for first in (True, False):
        stage = []
        if first:
            for copy in local:
                copy.wait()
        for s in pieces:
            me, _, to = s.ring(first)
            view = s.view(first, me)
            stage.append([sends.start(view, view, to[i]) for i in range(2)])
        if not first:
            for s in pieces:
                send_across(s, s.view(first, s.ring(first)[0]))
            far_rows = []
            for i, origin in enumerate((x_left, x_right)):
                x_came[i].wait_recv()
                view = rows_out.at[origin, pl.ds(i * half, half)]
                far_rows.append(sends.start(view, view, x_ways[i]))
                view = rows_out.at[origin]
                across.append(sends.start(view, view, partner))
        onward = []
        for s, came in zip(pieces, stage):
            _, (right, left, _), to = s.ring(first)
            pair = []
            for i, origin in enumerate((left, right)):
                came[i].wait_recv()
                view = s.view(first, origin, i)
                pair.append(sends.start(view, view, to[i]))
                if not first:
                    send_across(s, s.view(first, origin))
            onward.append(pair)
        for s, pair in zip(pieces, onward):
            far = s.ring(first)[1][2]
            for i in range(2):
                pair[i].wait_recv()
                if not first:
                    send_across(s, s.view(first, far, i))
    for i in range(2):
        far_rows[i].wait_recv()
        view = rows_out.at[x_far, pl.ds(i * half, half)]
        across.append(sends.start(view, view, partner))
    for copy in across:
        copy.wait_recv()
    sends.finish()


def gather_first(wq, wk, wv, small, rows, note, collective_id):
    height, total = wq.shape[0], wq.shape[1] + wk.shape[1] + wv.shape[1]
    return pl.pallas_call(
        gather_first_kernel,
        out_shape=[
            jax.ShapeDtypeStruct((4, 4, height, total), wq.dtype),
            jax.ShapeDtypeStruct((4, 4, *small.shape), small.dtype),
            jax.ShapeDtypeStruct((8, *rows.shape), rows.dtype),
            jax.ShapeDtypeStruct((8, *note.shape), note.dtype),
        ],
        in_specs=[ANY] * 6,
        out_specs=[ANY] * 4,
        scratch_shapes=[
            pltpu.SemaphoreType.DMA((7,)),
            pltpu.SemaphoreType.DMA((50,)),
            pltpu.SemaphoreType.DMA((50,)),
        ],
        compiler_params=pltpu.CompilerParams(collective_id=collective_id, has_side_effects=True),
    )(wq, wk, wv, small, rows, note)


SCALE = HEAD_SIZE**-0.5
LOG2E = 1.4426950408889634
BLOCK = 512


def spin(z, cosine, sine):
    return z * cosine + pltpu.roll(z, HEAD_SIZE // 2, 1) * sine


def qkv_kernel(
    tokens_ref, w_ref, gain_ref, cos_ref, sin_ref, normed_ref, query_ref, kv_ref,
    own_kv, local_sem, send_sems, recv_sems,
):
    part, core, right, left, far, partner = around_x()
    to = lambda i: {"expert": i}
    barrier = pltpu.get_barrier_semaphore()
    for other in (partner, right, left):
        pl.semaphore_signal(barrier, inc=1, device_id=to(other), device_id_type=MESH)
    sends = Sends(send_sems, recv_sems)
    cosine, sine = cos_ref[...], sin_ref[...]
    inputs = tokens_ref[...].astype(F32)
    inverse = lax.rsqrt(jnp.mean(inputs * inputs, axis=-1, keepdims=True) + EPSILON)
    normed_ref[...] = (inputs * inverse * gain_ref[...]).astype(BF16)
    strip = w_ref.shape[1] // 4
    wide = strip - HEAD_SIZE
    for s in range(4):
        got = mm(normed_ref[...], w_ref[:, s * strip + wide : (s + 1) * strip])
        if s % 2 == 0:
            got = spin(got, cosine, sine)
        own_kv[:, s * HEAD_SIZE : (s + 1) * HEAD_SIZE] = got.astype(BF16)

    def queries(s):
        got = mm(normed_ref[...], w_ref[:, s * strip : s * strip + wide])
        for h in range(0, wide, HEAD_SIZE):
            head = spin(got[:, h : h + HEAD_SIZE], cosine, sine)
            query_ref[:, s * wide + h : s * wide + h + HEAD_SIZE] = head.astype(BF16)

    pl.semaphore_wait(barrier, 3)
    half = own_kv.shape[0] // 2
    own = pltpu.make_async_copy(own_kv, kv_ref.at[part], local_sem)
    own.start()
    ways = (to(right), to(left))
    came = [sends.start(own_kv, kv_ref.at[part], way) for way in ways]
    across = [sends.start(own_kv, kv_ref.at[part], to(partner))]
    queries(0)
    queries(1)
    onward = []
    for i, origin in enumerate((left, right)):
        came[i].wait_recv()
        view = kv_ref.at[origin, pl.ds(i * half, half)]
        onward.append(sends.start(view, view, ways[i]))
        view = kv_ref.at[origin]
        across.append(sends.start(view, view, to(partner)))
    queries(2)
    queries(3)
    for i in range(2):
        onward[i].wait_recv()
        view = kv_ref.at[far, pl.ds(i * half, half)]
        across.append(sends.start(view, view, to(partner)))
    for copy in across:
        copy.wait_recv()
    own.wait()
    sends.finish()


def qkv(tokens, w, gain, cosine, sine, collective_id):
    rows, width = tokens.shape
    kv_width = w.shape[1] - width
    return pl.pallas_call(
        qkv_kernel,
        out_shape=[
            jax.ShapeDtypeStruct((rows, width), BF16),
            jax.ShapeDtypeStruct((rows, width), BF16),
            jax.ShapeDtypeStruct((8, rows, kv_width), BF16),
        ],
        in_specs=[VMEM] * 5,
        out_specs=[VMEM, VMEM, ANY],
        scratch_shapes=[
            pltpu.VMEM((rows, kv_width), BF16),
            pltpu.SemaphoreType.DMA,
            pltpu.SemaphoreType.DMA((9,)),
            pltpu.SemaphoreType.DMA((9,)),
        ],
        compiler_params=pltpu.CompilerParams(
            collective_id=collective_id, has_side_effects=True, vmem_limit_bytes=40 * 2**20
        ),
    )(tokens, w, gain, cosine, sine)


def fill_bias(bias, start_ref, first_row):
    length, rows = bias.shape
    places = lax.broadcasted_iota(jnp.int32, (length, rows), 0)
    mine = first_row + lax.broadcasted_iota(jnp.int32, (length, rows), 1)
    keep = (places >= start_ref[...]) & (places <= mine)
    bias[...] = jnp.where(keep, 0.0, MASK_FILL)


def attend_kernel(start_ref, q_ref, kv_ref, ctx_ref, lse_ref, bias, v_t, scores):
    head = pl.program_id(0)
    length = bias.shape[0]

    @pl.when(head == 0)
    def _():
        fill_bias(bias, start_ref, start_ref.shape[1] * lax.axis_index("expert"))

    @pl.when(head % GROUP == 0)
    def _():
        v_t[...] = kv_ref[:, HEAD_SIZE:].astype(F32).T.astype(BF16)

    query = q_ref[...]
    top = None
    for at in range(0, length, BLOCK):
        span = pl.ds(at, BLOCK)
        s = mm_nt(kv_ref[span, :HEAD_SIZE], query) + bias[span]
        scores[span] = s
        here = jnp.max(s, axis=0, keepdims=True)
        top = here if top is None else jnp.maximum(top, here)
    total = jnp.zeros_like(top)
    context = jnp.zeros((HEAD_SIZE, query.shape[0]), F32)
    for at in range(0, length, BLOCK):
        span = pl.ds(at, BLOCK)
        p = jnp.exp2((scores[span] - top) * (SCALE * LOG2E))
        total += jnp.sum(p, axis=0, keepdims=True)
        context += mm(v_t[:, span], p.astype(BF16))
    ctx_ref[...] = (context / total).T.astype(BF16)
    lse_ref[0] = top * (SCALE * LOG2E) + jnp.log2(total)


def attend(start, query, kv):
    rows, width = query.shape
    length = kv.shape[0]
    by_head = pl.BlockSpec((rows, HEAD_SIZE), lambda h: (0, h))
    return pl.pallas_call(
        attend_kernel,
        grid=(QUERY_HEADS,),
        out_shape=[
            jax.ShapeDtypeStruct((rows, width), BF16),
            jax.ShapeDtypeStruct((QUERY_HEADS, 1, rows), F32),
        ],
        in_specs=[
            pl.BlockSpec((1, rows), lambda h: (0, 0)),
            by_head,
            pl.BlockSpec((length, 2 * HEAD_SIZE), lambda h: (0, h // GROUP)),
        ],
        out_specs=[by_head, pl.BlockSpec((1, 1, rows), lambda h: (h, 0, 0))],
        scratch_shapes=[
            pltpu.VMEM((length, rows), F32),
            pltpu.VMEM((HEAD_SIZE, length), BF16),
            pltpu.VMEM((length, rows), F32),
        ],
        compiler_params=pltpu.CompilerParams(vmem_limit_bytes=40 * 2**20),
        cost_estimate=pl.CostEstimate(
            flops=4 * rows * length * width, bytes_accessed=4 * length * width, transcendentals=0
        ),
    )(start, query, kv)


def attend_back_kernel(
    start_ref, q_ref, kv_ref, g_ref, lse_ref, cos_ref, sin_ref, gq_ref, gkv_ref,
    bias, k_t, gkv, probs, grad_probs,
):
    head = pl.program_id(0)
    length = bias.shape[0]

    @pl.when(head == 0)
    def _():
        fill_bias(bias, start_ref, start_ref.shape[1] * lax.axis_index("expert"))

    @pl.when(head % GROUP == 0)
    def _():
        k_t[...] = kv_ref[:, :HEAD_SIZE].astype(F32).T.astype(BF16)
        gkv[...] = jnp.zeros_like(gkv)

    query, grad = q_ref[...], g_ref[...]
    lse = lse_ref[0]
    inner = jnp.zeros_like(lse)
    for at in range(0, length, BLOCK):
        span = pl.ds(at, BLOCK)
        s = mm_nt(kv_ref[span, :HEAD_SIZE], query) + bias[span]
        p = jnp.exp2(s * (SCALE * LOG2E) - lse)
        gp = mm_nt(kv_ref[span, HEAD_SIZE:], grad)
        inner += jnp.sum(p * gp, axis=0, keepdims=True)
        probs[span] = p
        grad_probs[span] = gp
        gkv[span, HEAD_SIZE:] += mm(p.astype(BF16), grad)
    gq = jnp.zeros((HEAD_SIZE, query.shape[0]), F32)
    for at in range(0, length, BLOCK):
        span = pl.ds(at, BLOCK)
        gs = (probs[span] * (grad_probs[span] - inner)).astype(BF16)
        gkv[span, :HEAD_SIZE] += mm(gs, query)
        gq += mm(k_t[:, span], gs)
    gq_ref[...] = spin(gq.T * SCALE, cos_ref[...], -sin_ref[...]).astype(BF16)

    @pl.when(head % GROUP == GROUP - 1)
    def _():
        gkv_ref[:, :HEAD_SIZE] = (gkv[:, :HEAD_SIZE] * SCALE).astype(BF16)
        gkv_ref[:, HEAD_SIZE:] = gkv[:, HEAD_SIZE:].astype(BF16)


def attend_back(start, query, kv, grad, lse, cosine, sine):
    rows, width = query.shape
    length = kv.shape[0]
    by_head = pl.BlockSpec((rows, HEAD_SIZE), lambda h: (0, h))
    by_group = pl.BlockSpec((length, 2 * HEAD_SIZE), lambda h: (0, h // GROUP))
    table = pl.BlockSpec((rows, HEAD_SIZE), lambda h: (0, 0))
    return pl.pallas_call(
        attend_back_kernel,
        grid=(QUERY_HEADS,),
        out_shape=[
            jax.ShapeDtypeStruct((rows, width), BF16),
            jax.ShapeDtypeStruct(kv.shape, BF16),
        ],
        in_specs=[
            pl.BlockSpec((1, rows), lambda h: (0, 0)),
            by_head,
            by_group,
            by_head,
            pl.BlockSpec((1, 1, rows), lambda h: (h, 0, 0)),
            table,
            table,
        ],
        out_specs=[by_head, by_group],
        scratch_shapes=[
            pltpu.VMEM((length, rows), F32),
            pltpu.VMEM((HEAD_SIZE, length), BF16),
            pltpu.VMEM((length, 2 * HEAD_SIZE), F32),
            pltpu.VMEM((length, rows), F32),
            pltpu.VMEM((length, rows), F32),
        ],
        compiler_params=pltpu.CompilerParams(vmem_limit_bytes=40 * 2**20),
        cost_estimate=pl.CostEstimate(
            flops=10 * rows * length * width, bytes_accessed=4 * length * width, transcendentals=0
        ),
    )(start, query, kv, grad, lse, cosine, sine)


LOW, HIGH = 0, 1


def gelu_parts(a):
    k = (2.0 / jnp.pi) ** 0.5
    square = a * a
    t = jnp.tanh(k * a * (1.0 + 0.044715 * square))
    slope = 0.5 * (1.0 + t) + 0.5 * a * (1.0 - t * t) * k * (1.0 + 3 * 0.044715 * square)
    return 0.5 * a * (1.0 + t), slope


def experts_kernel(
    ctx_ref, tokens_ref, small_ref, gain_ref, member_ref, slot_ref, d_out_ref,
    up_all, wo_hbm, wg_hbm, wu_hbm, wd_hbm,
    middle_ref, grad_middle_ref, grad_ctx_ref, small_grad_ref,
    back_out, grad_gu, grad_d, grad_wo,
    wo_ref, wg_ref, wu_ref, wd_ref, rows_all, returns, arrived, pair_grad, hidden, grad_pre,
    theirs, from_left, from_right, tile, back_rows, gates_src, gates_all, gg_src, gg_all,
    local_sems, tile_sems, back_sems, send_sems, recv_sems,
):
    part, core, right, left, far, partner = around_x()
    chip = part // 2
    to = lambda i: {"expert": i}
    others = [lax.rem(part + d, 8) for d in range(1, 8)]
    barrier = pltpu.get_barrier_semaphore()
    for other in others:
        pl.semaphore_signal(barrier, inc=1, device_id=to(other), device_id_type=MESH)
    sends = Sends(send_sems, recv_sems)
    rows, width = ctx_ref.shape
    half = rows // 2
    halves = (pl.ds(0, half), pl.ds(half, half))
    ff = wg_ref.shape[1]
    capacity = arrived.shape[0] // 8

    loads = []
    for src, dst in ((wo_hbm, wo_ref), (wg_hbm, wg_ref), (wu_hbm, wu_ref), (wd_hbm, wd_ref)):
        loads.append(pltpu.make_async_copy(src, dst, local_sems.at[len(loads)]))
    chips = [lax.rem(chip + d, 4) for d in (0, 3, 1, 2)]
    for u in range(4):
        src = up_all.at[pl.ds(2 * chips[u], 2)]
        loads.append(pltpu.make_async_copy(src, returns.at[u], local_sems.at[4 + u]))
    for load in loads:
        load.start()

    loads[0].wait()
    middle = tokens_ref[...].astype(F32) + mm(ctx_ref[...], wo_ref[...])
    middle_ref[...] = middle
    inverse = lax.rsqrt(jnp.mean(middle * middle, axis=-1, keepdims=True) + EPSILON)
    normed = (middle * inverse * gain_ref[...]).astype(BF16)
    rows_all[part] = normed
    member = member_ref[...]
    logits = jnp.where(member > 0.0, mm(normed, small_ref[...]), MASK_FILL)
    weight = jnp.exp(logits - jnp.max(logits, axis=-1, keepdims=True)) * member
    gates = weight / jnp.sum(weight, axis=-1, keepdims=True)
    gates_src[...] = gates.T[:EXPERTS]

    pl.semaphore_wait(barrier, 7)
    mine = rows_all.at[part]
    go_right = sends.start(mine, mine, to(right))
    go_left = sends.start(mine, mine, to(left))
    swap_own = sends.start(mine, mine, to(partner))
    note_sends = [sends.start(gates_src, gates_all.at[part], to(i)) for i in others]
    gates_all[part] = gates_src[...]

    def pick_of(source):
        slots = lax.broadcasted_iota(jnp.int32, (capacity, rows), 0)
        return slots == slot_ref[source]

    for u in range(4):
        loads[4 + u].wait()
        for c in range(2):
            pick = pick_of(2 * chips[u] + c).astype(BF16)
            got = mm(pick, returns[u, c])
            pair_grad[pl.ds((2 * u + c) * capacity, capacity)] = got.astype(BF16)
    for load in loads[1:4]:
        load.wait()

    def unit(u):
        at = chips[u]
        picks = [pick_of(2 * at + c) for c in range(2)]
        picks_b = [pick.astype(BF16) for pick in picks]
        spans = [pl.ds((2 * u + c) * capacity, capacity) for c in range(2)]
        both = pl.ds(2 * u * capacity, 2 * capacity)
        gate = []
        for c in range(2):
            arrived[spans[c]] = mm(picks_b[c], rows_all[2 * at + c]).astype(BF16)
            row = gates_all[2 * at + c, pl.ds(part, 1)]
            gate.append(jnp.sum(jnp.where(picks[c], row, 0.0), axis=-1, keepdims=True))
        gate = jnp.concatenate(gate, axis=0)
        x = arrived[both]
        a, b = mm(x, wg_ref[...]), mm(x, wu_ref[...])
        act, slope = gelu_parts(a)
        h = (act * b).astype(BF16)
        hidden[both] = h
        out = mm(h, wd_ref[...]).astype(BF16).astype(F32)
        up = pair_grad[both].astype(F32)
        gg = jnp.sum(up * out, axis=-1, keepdims=True)
        weighted = (gate * out).astype(BF16)
        pg = (gate * up).astype(BF16)
        pair_grad[both] = pg
        if u > 0:
            for c in range(2):
                stores[u - 1][c].wait()
        stores.append([])
        for c in range(2):
            back_rows[c] = mm_tn(picks_b[c], weighted[c * capacity : (c + 1) * capacity]).astype(
                BF16
            )
            store = pltpu.make_async_copy(
                back_rows.at[c], back_out.at[2 * at + c], back_sems.at[c]
            )
            store.start()
            stores[u].append(store)
            gg_c = gg[c * capacity : (c + 1) * capacity]
            row = jnp.sum(jnp.where(picks[c], gg_c, 0.0), axis=0, keepdims=True)
            gg_src[u, c] = jnp.broadcast_to(row, (8, rows))
        grad_h = mm_nt(pg, wd_ref[...])
        grad_a = (grad_h * b * slope).astype(BF16)
        grad_b = (grad_h * act).astype(BF16)
        grad_pre[both, :ff] = grad_a
        grad_pre[both, ff:] = grad_b
        grad_rows = (mm_nt(grad_a, wg_ref[...]) + mm_nt(grad_b, wu_ref[...])).astype(BF16)
        for c in range(2):
            returns[u, c] = mm_tn(
                picks_b[c], grad_rows[c * capacity : (c + 1) * capacity]
            ).astype(BF16)
        swaps.append(sends.start(returns.at[u, 1 - core], theirs.at[u], to(partner)))
        if u == 0:
            gg_all[part] = gg_src[0, core]
            gg_sends.append(sends.start(gg_src.at[0, 1 - core], gg_all.at[part], to(partner)))
        else:
            for c in (core, 1 - core):
                gg_sends.append(sends.start(gg_src.at[u, c], gg_all.at[part], to(2 * at + c)))

    def joined(u):
        swaps[u].wait_recv()
        theirs[u] = (theirs[u].astype(F32) + returns[u, core].astype(F32)).astype(BF16)

    stores, swaps, gg_sends = [], [], []
    swap_own.wait_recv()
    for copy in note_sends:
        copy.wait_recv()
    unit(0)
    go_right.wait_recv()
    first = rows_all.at[left, halves[LOW]]
    far_low = sends.start(first, first, to(right))
    swap_left = sends.start(rows_all.at[left], rows_all.at[left], to(partner))
    go_left.wait_recv()
    second = rows_all.at[right, halves[HIGH]]
    far_high = sends.start(second, second, to(left))
    swap_right = sends.start(rows_all.at[right], rows_all.at[right], to(partner))
    swap_left.wait_recv()
    unit(1)
    swap_right.wait_recv()
    unit(2)
    swap_far = []
    for h, copy in enumerate((far_low, far_high)):
        copy.wait_recv()
        piece = rows_all.at[far, halves[h]]
        swap_far.append(sends.start(piece, piece, to(partner)))
    joined(1)
    joined(2)
    back_right = sends.start(theirs.at[2, halves[HIGH]], from_left.at[2], to(right))
    back_left = sends.start(theirs.at[1, halves[LOW]], from_right.at[2], to(left))
    for copy in swap_far:
        copy.wait_recv()
    unit(3)
    joined(3)
    back_far_low = sends.start(theirs.at[3, halves[LOW]], from_left.at[0], to(right))
    back_far_high = sends.start(theirs.at[3, halves[HIGH]], from_right.at[0], to(left))

    tall = tile.shape[1]

    def tiles(first_tile, count, lhs, rhs, out):
        def step(i, _):
            slot = lax.rem(first_tile + i, 2)

            @pl.when(first_tile + i >= 2)
            def _():
                pltpu.make_async_copy(
                    tile.at[slot], grad_d.at[pl.ds(0, tall)], tile_sems.at[slot]
                ).wait()

            cols = pl.ds(pl.multiple_of(i * tall, 128), tall)
            tile[slot] = mm_tn(lhs[:, cols], rhs[...]).astype(BF16)
            pltpu.make_async_copy(
                tile.at[slot], out.at[pl.ds(pl.multiple_of(i * tall, 16), tall)], tile_sems.at[slot]
            ).start()
            return 0

        lax.fori_loop(0, count, step, 0)

    tiles(0, ff // tall, hidden, pair_grad, grad_d)
    back_far_low.wait_recv()
    theirs[2, halves[LOW]] = (
        theirs[2, halves[LOW]].astype(F32) + from_left[0].astype(F32)
    ).astype(BF16)
    back_right_low = sends.start(theirs.at[2, halves[LOW]], from_left.at[1], to(right))
    back_far_high.wait_recv()
    theirs[1, halves[HIGH]] = (
        theirs[1, halves[HIGH]].astype(F32) + from_right[0].astype(F32)
    ).astype(BF16)
    back_left_high = sends.start(theirs.at[1, halves[HIGH]], from_right.at[1], to(left))
    tiles(ff // tall, width // tall, arrived, grad_pre, grad_gu)

    swaps[0].wait_recv()
    back_right.wait_recv()
    back_left.wait_recv()
    back_right_low.wait_recv()
    back_left_high.wait_recv()
    total = theirs[0].astype(F32) + returns[0, core].astype(F32)
    total += jnp.concatenate([from_left[1], from_left[2]], axis=0).astype(F32)
    total += jnp.concatenate([from_right[2], from_right[1]], axis=0).astype(F32)
    for copy in gg_sends:
        copy.wait_recv()
    grad_gates = jnp.concatenate([gg_all[e, :1] for e in range(EXPERTS)], axis=0)
    gates_t = gates_src[...]
    products = gates_t * grad_gates
    grad_logits = products - gates_t * jnp.sum(products, axis=0, keepdims=True)
    grad_logits = jnp.concatenate(
        [grad_logits, jnp.zeros((128 - EXPERTS, rows), F32)], axis=0
    ).T.astype(BF16)
    total += mm_nt(grad_logits, small_ref[...])
    middle = middle_ref[...]
    inverse = lax.rsqrt(jnp.mean(middle * middle, axis=-1, keepdims=True) + EPSILON)
    scaled = middle * inverse
    gain = gain_ref[...]
    normed = (scaled * gain).astype(BF16)
    grad_gain = jnp.sum(total * scaled, axis=0, keepdims=True)
    lanes = lax.broadcasted_iota(jnp.int32, (width, 128), 1)
    small_grad = mm_tn(normed, grad_logits)
    small_grad += jnp.where(lanes == EXPERTS, jnp.broadcast_to(grad_gain, (128, width)).T, 0.0)
    small_grad_ref[...] = small_grad.astype(BF16)
    weighted = total * gain
    inner = jnp.mean(weighted * scaled, axis=-1, keepdims=True)
    grad_middle = d_out_ref[...].astype(F32) + inverse * (weighted - scaled * inner)
    grad_middle_ref[...] = grad_middle
    grad_attn = grad_middle.astype(BF16)
    grad_ctx_ref[...] = mm_nt(grad_attn, wo_ref[...]).astype(BF16)
    pair_grad[pl.ds(0, rows)] = grad_attn
    done = ff // tall + width // tall

    def wo_tile(i, _):
        slot = lax.rem(done + i, 2)
        pltpu.make_async_copy(
            tile.at[slot], grad_d.at[pl.ds(0, tall)], tile_sems.at[slot]
        ).wait()
        cols = pl.ds(pl.multiple_of(i * tall, 128), tall)
        tile[slot] = mm_tn(ctx_ref[:, cols], pair_grad[pl.ds(0, rows)]).astype(BF16)
        pltpu.make_async_copy(
            tile.at[slot], grad_wo.at[pl.ds(pl.multiple_of(i * tall, 16), tall)], tile_sems.at[slot]
        ).start()
        return 0

    lax.fori_loop(0, width // tall, wo_tile, 0)
    for slot in range(2):
        pltpu.make_async_copy(
            tile.at[slot], grad_d.at[pl.ds(0, tall)], tile_sems.at[slot]
        ).wait()
    for c in range(2):
        stores[3][c].wait()
    sends.finish()


def experts(ctx, tokens, small, gain, member, slots, d_out, up_all, wo, wg, wu, wd, collective_id):
    rows, width = ctx.shape
    ff = wg.shape[1]
    capacity = rows * 9 // 16
    vmem, sds = pltpu.VMEM, jax.ShapeDtypeStruct
    return pl.pallas_call(
        experts_kernel,
        out_shape=[
            sds((rows, width), F32),
            sds((rows, width), F32),
            sds((rows, width), BF16),
            sds((width, 128), BF16),
            sds((8, rows, width), BF16),
            sds((width, 2 * ff), BF16),
            sds((ff, width), BF16),
            sds((width, width), BF16),
        ],
        in_specs=[VMEM] * 7 + [ANY] * 5,
        out_specs=[VMEM] * 4 + [ANY] * 4,
        scratch_shapes=[
            vmem((width, width), BF16),
            vmem((width, ff), BF16),
            vmem((width, ff), BF16),
            vmem((ff, width), BF16),
            vmem((8, rows, width), BF16),
            vmem((4, 2, rows, width), BF16),
            vmem((8 * capacity, width), BF16),
            vmem((8 * capacity, width), BF16),
            vmem((8 * capacity, ff), BF16),
            vmem((8 * capacity, 2 * ff), BF16),
            vmem((4, rows, width), BF16),
            vmem((3, rows // 2, width), BF16),
            vmem((3, rows // 2, width), BF16),
            vmem((2, 256, width), BF16),
            vmem((2, rows, width), BF16),
            vmem((8, rows), F32),
            vmem((8, 8, rows), F32),
            vmem((4, 2, 8, rows), F32),
            vmem((8, 8, rows), F32),
            pltpu.SemaphoreType.DMA((8,)),
            pltpu.SemaphoreType.DMA((2,)),
            pltpu.SemaphoreType.DMA((2,)),
            pltpu.SemaphoreType.DMA((40,)),
            pltpu.SemaphoreType.DMA((40,)),
        ],
        compiler_params=pltpu.CompilerParams(
            collective_id=collective_id, has_side_effects=True, vmem_limit_bytes=63 * 2**20
        ),
    )(ctx, tokens, small, gain, member, slots, d_out, up_all, wo, wg, wu, wd)


def widen_kernel(late_ref, gu_ref, d_ref, g_out, u_out, d_out):
    ff = g_out.shape[1]
    g_out[...] = gu_ref[:, :ff].astype(F32)
    u_out[...] = gu_ref[:, ff:].astype(F32)
    d_out[...] = d_ref[...].astype(F32)


def widen(sums, late):
    steps = 8
    (width, both), (ff, _) = sums[0].shape, sums[1].shape
    spec = lambda a, b: pl.BlockSpec((a // steps, b), lambda i: (i, 0))
    return pl.pallas_call(
        widen_kernel,
        grid=(steps,),
        out_shape=[jax.ShapeDtypeStruct(s, F32) for s in ((width, ff), (width, ff), (ff, width))],
        in_specs=[ANY, spec(width, both), spec(ff, width)],
        out_specs=[spec(width, ff), spec(width, ff), spec(ff, width)],
        cost_estimate=pl.CostEstimate(flops=0, bytes_accessed=21 * 2**20, transcendentals=0),
    )(late, *sums)


def on_device(
    tokens,
    d_out,
    gain_in,
    w_query,
    key_projection_weight,
    value_projection_weight,
    w_out,
    gain_mid,
    w_router,
    w_gate,
    w_up,
    w_down,
    routes,
    segments,
):
    rows, width = tokens.shape
    length = segments.shape[1]
    part = lax.axis_index("expert")
    parts = lax.axis_size("expert")
    core = part % 2
    capacity = rows * 9 // 16
    seg_row = segments[0]
    offset = part * rows
    my_seg = lax.dynamic_slice_in_dim(seg_row, offset, rows, 0)
    start = jnp.sum((seg_row[None, :] < my_seg[:, None]).astype(jnp.int32), axis=1)
    angles = angles_for(offset + jnp.arange(rows, dtype=jnp.int32) - start)
    cosine, sine = jnp.cos(angles), jnp.sin(angles)
    cosine = jnp.concatenate([cosine, cosine], axis=1)
    sine = jnp.concatenate([-sine, sine], axis=1)
    start = start[None, :]

    small = jnp.concatenate([w_router, gain_mid[:, None], gain_in[:, None]], axis=1)
    small = jnp.pad(small, ((0, 0), (0, 128 - small.shape[1])))
    note = jnp.pad(routes.T, ((0, 8 - TOPK), (0, 0)))
    w_strips, small, upstream_all, notes = gather_first(
        w_query, key_projection_weight, value_projection_weight, small, d_out, note, 1
    )
    w_strips = w_strips.reshape(width, -1)
    small = small.reshape(width, -1)
    gain_mid_row = small[:, EXPERTS].astype(F32)[None, :]
    gain_in_row = small[:, EXPERTS + 1].astype(F32)[None, :]
    wo = gather_dense(w_out, core)

    normed, query, kv_all = qkv(tokens, w_strips, gain_in_row, cosine, sine, 2)
    kv_all = kv_all.reshape(length, -1)
    context, lse = attend(start, query, kv_all)

    member = jnp.any(routes[:, :, None] == jnp.arange(128, dtype=jnp.int32), axis=1).astype(F32)
    chosen = jnp.any(notes[:, :TOPK] == part, axis=1)
    slots = jnp.where(chosen, jnp.cumsum(chosen.astype(jnp.int32), axis=1) - 1, -1)[:, None, :]
    middle, grad_middle, grad_ctx, small_grads, back_out, grad_gu, grad_d, grad_wo = experts(
        context, tokens, small, gain_mid_row, member, slots, d_out, upstream_all,
        wo, w_gate[0], w_up[0], w_down[0], 3,
    )

    kv_at = QUERY_HEADS * HEAD_SIZE
    grad_qlin, kv_terms = attend_back(start, query, kv_all, grad_ctx, lse, cosine, sine)
    kv_grad = reduce_x(kv_terms.reshape(parts, rows, -1), 5)
    gk0, gv0, gk1, gv1 = (kv_grad[:, i * HEAD_SIZE : (i + 1) * HEAD_SIZE] for i in range(4))
    grad_kv = jnp.concatenate(
        [rotate(gk0, cosine, -sine), gv0, rotate(gk1, cosine, -sine), gv1], axis=1
    ).astype(BF16)
    wide = kv_at // 4
    grad_lin = jnp.concatenate(
        [
            piece
            for s in range(4)
            for piece in (
                grad_qlin[:, s * wide : (s + 1) * wide],
                grad_kv[:, s * HEAD_SIZE : (s + 1) * HEAD_SIZE],
            )
        ],
        axis=1,
    )
    grad_wqkv = mm_tn(normed, grad_lin).astype(BF16)
    grad_normed = mm_nt(grad_lin, w_strips)
    grad_inputs_norm, grad_gin = rms_back(tokens.astype(F32), gain_in_row, grad_normed)
    grad_tokens = grad_middle + grad_inputs_norm
    lanes = jnp.arange(128)[None, :]
    small_grads = jnp.where(lanes == EXPERTS + 1, grad_gin[:, None].astype(BF16), small_grads)

    owned = lambda g: g.reshape(4, 4, width // 16, -1)
    g_wq, g_wk, g_wv, g_wo, small_sum, mixed = reduce_all(
        owned(grad_wqkv), owned(grad_wo), owned(small_grads), middle, back_out,
        key_projection_weight.shape[1], 6,
    )
    expert_sums = widen([lax.psum(g, "dp") for g in (grad_gu, grad_d)], small_sum)
    return (
        mixed,
        grad_tokens,
        small_sum[:, EXPERTS + 1],
        g_wq,
        g_wk,
        g_wv,
        g_wo,
        small_sum[:, EXPERTS],
        small_sum[:, :EXPERTS],
        *(g[None] for g in expert_sums),
    )


def solution(mesh):
    whole = P(("dp", "expert"), None)
    over_dp, by_dp, over_expert = P("dp"), P("dp", None), P("expert", None, None)
    return jax.shard_map(
        on_device,
        mesh=mesh,
        in_specs=(whole, whole, over_dp, by_dp, by_dp, by_dp, by_dp, over_dp, by_dp)
        + (over_expert,) * 3
        + (whole, by_dp),
        out_specs=(whole, whole, over_dp, by_dp, by_dp, by_dp, by_dp, over_dp, by_dp)
        + (over_expert,) * 3,
        check_vma=False,
    )
```

time: 614 us -> 387 us (0.63)
  matrix products: 161 us -> 7.62 us
  Pallas kernels: 212 us -> 322 us
  waiting for transfers between devices: 101 us -> 0.06 us
  other arithmetic: 64.6 us -> 16 us
  local copies, waits for them, and re-layouts: 39.5 us -> 18.9 us
  blocking collectives: 11.7 us -> 0 us
    pallas_call x4 -> x7, Pallas kernels: 164 us -> 307 us  [the longest x1 91.5 us: experts(): pl.pallas_call(experts_kernel, out_shape=[sds((rows, width), F32), sds((r...]
    dot_general x16 -> x0, matrix products: 83.7 us -> none  [the longest x2 16.1 us: scores_for(): jnp.einsum('tgd,sd->gts', query[:, h], keys[:, h], preferred_element_type...]
    dot_general x20 -> x2, matrix products: 77.2 us -> 7.62 us  [dot(): return lax.dot_general(a, b, (dims, ((), ())), preferred_element_type=F32)]
    psum x1, waiting for transfers between devices: 65.6 us -> 0.01 us  [on_device(): lax.psum(g, 'dp')]
    reduce_scatter x1 -> x0, waiting for transfers between devices: 34.3 us -> none  [rs_x(): return lax.psum_scatter(blocks, 'expert', scatter_dimension=0, tiled=True)]
    pallas_call x2 -> x1, Pallas kernels: 48.9 us -> 15.2 us  [reduce_x(): pl.pallas_call(reduce_x_kernel, out_shape=jax.ShapeDtypeStruct((rows, col...]
    convert_element_type x14 -> x3, other arithmetic: 28.6 us -> 2.34 us  [the longest x1 1.67 us: on_device(): gain_mid_row = small[:, EXPERTS].astype(F32)[None, :]]
    slice x13 -> x1, local copies, waits for them, and re-layouts: 15.2 us -> 1.59 us  [on_device(): small_sum[:, EXPERTS]]
  transfers between devices with their start and end apart: 5 -> 3, of which waited for: 2 -> 0; matrix products, arithmetic and copies ran while one was open for 23% -> 7% of each run, Pallas kernels for 22% -> 58%
where the time goes in v2:
time: 387 us; the launch traced here: 380 us
  Pallas kernels  322 us (83%)
  local copies, waits for them, and re-layouts  18.9 us (5%)
  other arithmetic  16 us (4%)
  between operations  15 us (4%)
  matrix products  7.62 us (2%)
    pallas_call x1, Pallas kernels, experts(): pl.pallas_call(experts_kernel, out_shape=[sds((rows, width), F32), sds((r...  91.5 us
    pallas_call x1, Pallas kernels, reduce_all(): pl.pallas_call(reduce_all_kernel, out_shape=[sds((height, width), F32), s...  73.6 us
    pallas_call x1, Pallas kernels, gather_first(): pl.pallas_call(gather_first_kernel, out_shape=[jax.ShapeDtypeStruct((4, 4...  73.1 us
    pallas_call x1, Pallas kernels, attend_back(): pl.pallas_call(attend_back_kernel, grid=(QUERY_HEADS,), out_shape=[jax.Sh...  25.7 us
    pallas_call x1, Pallas kernels, attend(): pl.pallas_call(attend_kernel, grid=(QUERY_HEADS,), out_shape=[jax.ShapeDt...  18.4 us
    pallas_call x1, Pallas kernels, qkv(): pl.pallas_call(qkv_kernel, out_shape=[jax.ShapeDtypeStruct((rows, width),...  15.4 us
    pallas_call x1, Pallas kernels, reduce_x(): pl.pallas_call(reduce_x_kernel, out_shape=jax.ShapeDtypeStruct((rows, col...  15.2 us
    unnamed x65, local copies, waits for them, and re-layouts  13.5 us
  transfers between devices with their start and end apart: 3, of which 0 were waited for; matrix products, arithmetic and copies ran while one was open for 7% of the time, Pallas kernels for 58%

profile of v2, /device:TPU:1, one launch (start us, length us, event | category | flops | bytes accessed | tf_op | source)
XLA Modules:
  0.0 379.8 jit_solution(14494145338973475227)
XLA Ops:
  7.3 0.9 copy-done
  8.1 0.7 constant_dynamic-slice_fusion
  8.9 0.7 pad_maximum_fusion.3
  9.6 0.1 copy.44
  9.7 1.3 pad.9.note_ref
  11.0 0.6 pad.8.small_ref
  11.7 73.1 %shard_map.229 = (bf16[4,4,96,2048]{3,2,1,0:T(8,128)(2,1)}, bf16[4,4,96,128]{3,2,1,0:T(8,128)(2,1)}, bf16[8,256,1536]{2,1,0:T(8,128)(2,1)}, s32[8,8,256]{2,1,0:T(8,128)}) custom-call(bf16[96,1536]{1,0:T(8,128)(2,1)} %wq_ref.1, bf16[96,256]{1,0:T(8,128)(2,1)} %wk_ref.1, bf16[96,256]{1,0:T(8,128)(2,1)} %wv_ref.1, bf16[96,128]{1,0:T(8,128)(2,1)} %pad.8.small_ref, ...), custom_call_target="tpu_custom_call" | custom-call | tf_op jit(solution)/shard_map/pallas_call | solution.py:533
  84.8 0.1 collective-permute-start
  84.9 1.7 convert_reduce_fusion.1
  86.6 0.6 reshape.181.gain_ref
  87.2 0.2 fusion.9
  87.4 0.7 convert_element_type.75.member_ref
  88.1 0.9 fusion.17
  88.9 0.6 reduce-window.6
  89.5 0.2 slice_reduce_fusion.2
  89.9 0.4 convert_reduce_fusion
  90.3 0.5 fusion.16
  90.8 0.1 pad_maximum_fusion.1
  91.0 0.5 copy-done.14
  91.5 2.8 copy-done.4
  94.3 15.4 %shard_map.230 = (bf16[256,1536]{1,0:T(8,128)(2,1)S(1)}, bf16[256,1536]{1,0:T(8,128)(2,1)S(1)}, bf16[8,256,512]{2,1,0:T(8,128)(2,1)S(1)}) custom-call(bf16[256,1536]{1,0:T(8,128)(2,1)S(1)} %copy-done.2, bf16[1536,2048]{1,0:T(8,128)(2,1)S(1)} %bitcast.40, f32[1,1536]{1,0:T(1,128)S(1)} %reshape.180.gain_ref, f32[256,128]{1,0:T(8,128)S(1)} %get-tuple-element.136.cos_ref, ...), custom_call_target="tpu_custom_call" | custom-call | tf_op jit(solution)/shard_map/pallas_call | solution.py:620
  109.7 0.7 copy_select_fusion.slot_ref
  110.4 18.4 %shard_map.231 = (bf16[256,1536]{1,0:T(8,128)(2,1)S(1)}, f32[12,1,256]{2,1,0:T(1,128)S(1)}) custom-call(s32[1,256]{1,0:T(1,128)S(1)} %bitcast.45, bf16[256,1536]{1,0:T(8,128)(2,1)S(1)} %get-tuple-element.43.q_ref, bf16[2048,512]{1,0:T(8,128)(2,1)S(1)} %bitcast.47), custom_call_target="tpu_custom_call" | custom-call | flops 3221225472 | bytes 12582912 | tf_op jit(solution)/shard_map/pallas_call | solution.py:684
  128.9 2.2 broadcast_select_fusion.1
  131.2 2.6 pad_maximum_fusion.wo_hbm
  133.7 91.5 %shard_map.232 = (f32[256,1536]{1,0:T(8,128)}, f32[256,1536]{1,0:T(8,128)}, bf16[256,1536]{1,0:T(8,128)(2,1)}, bf16[1536,128]{1,0:T(8,128)(2,1)}, bf16[8,256,153...) custom-call(bf16[256,1536]{1,0:T(8,128)(2,1)} %copy-done.5, ...), custom_call_target="tpu_custom_call" | custom-call | tf_op jit(solution)/shard_map/pallas_call | solution.py:1057
  225.3 1.1 copy-done.3
  226.3 0.2 fusion.8
  226.6 1.6 copy-done.9
  228.2 1.1 copy-done.12
  229.3 25.7 %shard_map.233 = (bf16[256,1536]{1,0:T(8,128)(2,1)S(1)}, bf16[2048,512]{1,0:T(8,128)(2,1)S(1)}) custom-call(s32[1,256]{1,0:T(1,128)S(1)} %bitcast.46, bf16[256,1536]{1,0:T(8,128)(2,1)S(1)} %copy-done.11, bf16[2048,512]{1,0:T(8,128)(2,1)S(1)} %bitcast.48, bf16[256,1536]{1,0:T(8,128)(2,1)S(1)} %copy-done.12, f32[12,1,256]{2,1,0:T(1,128)S(1)} %get-tuple-element.49.lse_ref, ...), custom_call_target="tpu_custom_call" | custom-call | flops 8053063680 | bytes 12582912 | tf_op jit(solution)/shard_map/pallas_call | solution.py:757
  255.0 15.2 %shard_map.234 = f32[256,512]{1,0:T(8,128)S(1)} custom-call(bf16[8,256,512]{2,1,0:T(8,128)(2,1)S(1)} %bitcast.44), custom_call_target="tpu_custom_call" | custom-call | tf_op jit(solution)/shard_map/pallas_call | solution.py:192
  270.4 0.1 slice_bitcast_fusion.3
  270.5 0.2 fusion.15
  270.9 0.2 fusion.14
  271.1 4.4 %convolution_convert_fusion = bf16[1536,2048]{1,0:T(8,128)(2,1)} fusion(bf16[256,1536]{1,0:T(8,128)(2,1)S(1)} %get-tuple-element.42, bf16[256,2048]{1,0:T(8,128)(2,1)S(1)} %slice_dynamic-update-slice_fusion.4), kind=kOutput, calls=%fused_computation | convolution fusion | flops 1613758464 | bytes 8126464 | tf_op jit(solution)/shard_map/dot_general | solution.py:29
  275.6 3.2 fusion.4
  278.8 1.0 broadcast_select_fusion.2
  279.8 73.6 %shard_map.235 = (f32[96,1536]{1,0:T(8,128)}, f32[96,256]{1,0:T(8,128)}, f32[96,256]{1,0:T(8,128)}, f32[96,1536]{1,0:T(8,128)}, f32[96,128]{1,0:T(8,128)}, /*index=5*/bf16[256,1536]{1,0:T(8,128)(2,1)}) custom-call(bf16[4,4,96,2048]{3,2,1,0:T(8,128)(2,1)} %bitcast.49, bf16[4,4,96,1536]{3,2,1,0:T(8,128)(2,1)} %bitcast.50, bf16[4,4,96,128]{3,2,1,0:T(8,128)(2,1)} %bitcast.56, ...), custom_call_target="tpu_custom_call" | custom-call | tf_op jit(solution)/shard_map/pallas_call | solution.py:390
  353.4 1.5 copy.47
  354.8 1.6 slice_reduce_fusion
  356.4 3.0 fusion.7
  359.4 9.3 %shard_map.236 = (f32[1536,768]{1,0:T(8,128)}, f32[1536,768]{1,0:T(8,128)}, f32[768,1536]{1,0:T(8,128)}) custom-call(f32[96,128]{1,0:T(8,128)} %get-tuple-element.58.late_ref, bf16[1536,1536]{1,0:T(8,128)(2,1)} %get-tuple-element.122.gu_ref, bf16[768,1536]{1,0:T(8,128)(2,1)} %get-tuple-element.123.d_ref), custom_call_target="tpu_custom_call" | custom-call | bytes 22020096 | tf_op jit(solution)/shard_map/pallas_call | solution.py:1114
  368.7 0.9 copy.63
  369.6 0.8 copy.64
  370.4 0.6 copy.65
  371.1 0.6 copy.66
  371.7 0.8 copy.67
  (77 shorter events, 0.8 us)
Async XLA Ops:
  7.2 1.0 copy-start
  7.2 80.0 %copy-start.23 = (s32[256,4]{0,1:T(4,128)S(1)}, s32[256,4]{0,1:T(4,128)}, u32[]{:S(2)}) copy-start(s32[256,4]{0,1:T(4,128)} %param.26) | copy-start | bytes 12292
  7.2 82.7 %copy-start.24 = (s32[1,2048]{1,0:T(1,128)S(1)}, s32[1,2048]{1,0:T(1,128)}, u32[]{:S(2)}) copy-start(s32[1,2048]{1,0:T(1,128)} %param.27) | copy-start | bytes 24580
  7.2 84.3 %copy-start.2 = (bf16[256,1536]{1,0:T(8,128)(2,1)S(1)}, bf16[256,1536]{1,0:T(8,128)(2,1)}, u32[]{:S(2)}) copy-start(bf16[256,1536]{1,0:T(8,128)(2,1)} %tokens_ref.3) | copy-start | bytes 2359300
  7.2 77.5 %all-gather.2.cloned.1.call-start = ((), (), s32[]{:S(2)}) async-start(), calls=%async_computation | async-start | bytes 2506752 | tf_op jit(solution)/shard_map/all_gather | solution.py:71
  8.8 350.6 %all-reduce.5.cloned.1.call-start = ((), (), s32[]{:S(2)}) async-start(), calls=%async_computation.1 | async-start | bytes 14155776 | tf_op jit(solution)/shard_map/psum | solution.py:1211
  84.8 44.1 %collective-permute-start = (bf16[1536,768]{1,0:T(8,128)(2,1)}, bf16[1536,768]{1,0:T(8,128)(2,1)}, u32[]{:S(2)}, u32[]{:S(2)}) collective-permute-start(bf16[1536,768]{1,0:T(8,128)(2,1)} %all-gather.2.cloned.1.call-done), channel_id=1, source_target_pairs={{0,1},{1,0},{2,3},{3,2},{4,5},{5,4},{6,7},{7,6},{8,9},{9,8},{10,11... | collective-permute-start | bytes 7077896 | tf_op jit(solution)/shard_map/ppermute | solution.py:65
  90.8 0.7 copy-start.14
  91.0 18.7 %copy-start.6 = (f32[256,128]{1,0:T(8,128)}, f32[256,128]{1,0:T(8,128)S(1)}, u32[]{:S(2)}) copy-start(f32[256,128]{1,0:T(8,128)S(1)} %get-tuple-element.136.cos_ref) | copy-start | bytes 393220
  91.5 2.8 copy-start.4
  109.7 19.1 %copy-start.8 = (bf16[8,256,512]{2,1,0:T(8,128)(2,1)}, bf16[8,256,512]{2,1,0:T(8,128)(2,1)S(1)}, u32[]{:S(2)}) copy-start(bf16[8,256,512]{2,1,0:T(8,128)(2,1)S(1)} %get-tuple-element.44) | copy-start | bytes 6291460
  109.7 19.1 %copy-start.10 = (bf16[256,1536]{1,0:T(8,128)(2,1)}, bf16[256,1536]{1,0:T(8,128)(2,1)S(1)}, u32[]{:S(2)}) copy-start(bf16[256,1536]{1,0:T(8,128)(2,1)S(1)} %get-tuple-element.43.q_ref) | copy-start | bytes 2359300
  110.4 18.5 %copy-start.13 = (bf16[1536,768]{1,0:T(8,128)(2,1)S(1)}, bf16[1536,768]{1,0:T(8,128)(2,1)}, u32[]{:S(2)}) copy-start(bf16[1536,768]{1,0:T(8,128)(2,1)} %all-gather.2.cloned.1.call-done) | copy-start | bytes 7077892
  128.9 2.3 copy-start.5
  225.2 1.1 copy-start.3
  225.2 1.4 copy-start.7
  225.2 1.4 copy-start.11
  226.6 1.6 copy-start.9
  228.2 1.1 copy-start.12
  255.0 15.5 %copy-start.15 = (f32[256,64]{1,0:T(8,128)S(1)}, f32[256,64]{1,0:T(8,128)}, u32[]{:S(2)}) copy-start(f32[256,64]{1,0:T(8,128)} %copy-done.14) | copy-start | bytes 196612
  270.9 4.7 %slice-start = ((s8[6291456]{0:T(1024)(128)(4,1)}), s8[4194304]{0:T(1024)(128)(4,1)S(1)}, s32[]{:S(2)}) async-start(s8[6291456]{0:T(1024)(128)(4,1)} %bitcast.41), calls=%async_computation.2 | async-start | bytes 8388608
  271.1 4.4 %slice-start.1 = ((s8[6291456]{0:T(1024)(128)(4,1)}), s8[2097152]{0:T(1024)(128)(4,1)S(1)}, s32[]{:S(2)}) async-start(s8[6291456]{0:T(1024)(128)(4,1)} %bitcast.41), calls=%async_computation.3 | async-start | bytes 4194304
  275.6 3.2 copy-start.20
  279.8 76.6 %copy-start.16 = (f32[256,1536]{1,0:T(8,128)S(1)}, f32[256,1536]{1,0:T(8,128)}, u32[]{:S(2)}) copy-start(f32[256,1536]{1,0:T(8,128)} %get-tuple-element.57) | copy-start | bytes 4718596
  359.4 9.3 %copy-start.17 = (bf16[256,1536]{1,0:T(8,128)(2,1)S(1)}, bf16[256,1536]{1,0:T(8,128)(2,1)}, u32[]{:S(2)}) copy-start(bf16[256,1536]{1,0:T(8,128)(2,1)} %get-tuple-element.150) | copy-start | bytes 2359300
  359.4 10.2 %copy-start.19 = (f32[96,1536]{1,0:T(8,128)S(1)}, f32[96,1536]{1,0:T(8,128)}, u32[]{:S(2)}) copy-start(f32[96,1536]{1,0:T(8,128)} %get-tuple-element.153) | copy-start | bytes 1769476
  359.4 13.1 %copy-start.1 = (bf16[96,1536]{1,0:T(8,128)(2,1)S(1)}, bf16[96,1536]{1,0:T(8,128)(2,1)}, u32[]{:S(2)}) copy-start(bf16[96,1536]{1,0:T(8,128)(2,1)} %param.20) | copy-start | bytes 884740
  368.7 1.7 copy-start.22
  368.7 2.4 copy-start.21
  368.7 3.0 copy-start.18
Sparse Core Ops, SparseCore 0:
  10.8 51.1 all-gather.1
  225.4 133.5 all-reduce.4

commit v3 on v2

v3 whole, which is shorter than its diff:
```python
import jax
import jax.numpy as jnp
from jax import lax
from jax.experimental import pallas as pl
from jax.experimental.pallas import tpu as pltpu
from jax.sharding import PartitionSpec as P

QUERY_HEADS = 12
KEY_VALUE_HEADS = 2
HEAD_SIZE = 128
TOPK = 4
EXPERTS = 8
GROUP = QUERY_HEADS // KEY_VALUE_HEADS
SCALE = HEAD_SIZE**-0.5
LOG2E = 1.4426950408889634
BLOCK = 512

EPSILON = 1e-06
ROPE_BASE = 1000000.0
MASK_FILL = -1e30
F32 = jnp.float32
BF16 = jnp.bfloat16

PARTNER = [(i, i ^ 1) for i in range(8)]
MESH = pl.DeviceIdType.MESH
ANY = pl.BlockSpec(memory_space=pl.ANY)
VMEM = pl.BlockSpec(memory_space=pltpu.VMEM)
MIB = 2**20


def dot(a, b, dims):
    return lax.dot_general(a, b, (dims, ((), ())), preferred_element_type=F32)


def mm(a, b):
    return dot(a, b, ((1,), (0,)))


def mm_nt(a, b):
    return dot(a, b, ((1,), (1,)))


def mm_tn(a, b):
    return dot(a, b, ((0,), (0,)))


def sds(shape, dtype):
    return jax.ShapeDtypeStruct(tuple(shape), dtype)


def remote_params(collective_id, mib):
    return pltpu.CompilerParams(
        collective_id=collective_id, has_side_effects=True, vmem_limit_bytes=mib * MIB
    )


def semaphores(count):
    return pltpu.SemaphoreType.DMA((count,))


def inverse_rms(rows):
    return lax.rsqrt(jnp.mean(rows * rows, axis=-1, keepdims=True) + EPSILON)


def rms_back(rows, gain, grad):
    inverse = inverse_rms(rows)
    scaled = rows * inverse
    weighted = grad * gain
    inner = jnp.mean(weighted * scaled, axis=-1, keepdims=True)
    return inverse * (weighted - scaled * inner), jnp.sum(grad * scaled, axis=0, keepdims=True)


def as_column(row, lanes):
    return jnp.broadcast_to(row, (lanes, row.shape[1])).T


def angles_for(positions):
    half_width = HEAD_SIZE // 2
    freqs = ROPE_BASE ** (-2.0 * jnp.arange(half_width, dtype=F32) / HEAD_SIZE)
    return positions.astype(F32)[:, None] * freqs[None, :]


def spin(z, cosine, sine):
    return z * cosine + pltpu.roll(z, HEAD_SIZE // 2, 1) * sine


def gather_dense(shard, core):
    half = shard.shape[1] // 2
    mine = lax.dynamic_slice_in_dim(shard, core * half, half, 1)
    got = lax.all_gather(mine, "dp", axis=0, tiled=True)
    other = lax.ppermute(got, "expert", PARTNER)
    first = jnp.where(core == 0, got, other)
    second = jnp.where(core == 0, other, got)
    return jnp.concatenate([first, second], axis=1)


class Sends:
    def __init__(self, send_sems, recv_sems):
        self.send_sems, self.recv_sems, self.made = send_sems, recv_sems, []

    def start(self, src, dst, to):
        at = len(self.made)
        copy = pltpu.make_async_remote_copy(
            src_ref=src,
            dst_ref=dst,
            send_sem=self.send_sems.at[at],
            recv_sem=self.recv_sems.at[at],
            device_id=to,
            device_id_type=MESH,
        )
        copy.start()
        self.made.append(copy)
        return copy

    def finish(self):
        for copy in self.made:
            copy.wait_send()


class Keeps:
    def __init__(self, sems):
        self.sems, self.made = sems, []

    def start(self, src, dst):
        copy = pltpu.make_async_copy(src, dst, self.sems.at[len(self.made)])
        copy.start()
        self.made.append(copy)
        return copy


class Place:
    def __init__(self):
        self.part = lax.axis_index("expert")
        self.core = self.part % 2
        self.chip = self.part // 2
        at = lambda d: lax.rem(self.chip + d, 4) * 2 + self.core
        self.right, self.left, self.far = at(1), at(3), at(2)
        to = lambda i: {"expert": i}
        self.partner = to(2 * self.chip + (1 - self.core))
        self.x_to = [to(self.right), to(self.left), to(self.far)]
        self.others = [to(lax.rem(self.part + d, 8)) for d in range(1, 8)]
        place = lax.axis_index("dp")
        self.y, self.z = place // 4, place % 4
        ring = lambda v: [lax.rem(v + d, 4) for d in (1, 3, 2)]
        self.y_ring, self.z_ring = ring(self.y), ring(self.z)
        self.y_to = [{"dp": v * 4 + self.z} for v in self.y_ring[:2]]
        self.z_to = [{"dp": self.y * 4 + v} for v in self.z_ring[:2]]

    def ring(self, along_y):
        if along_y:
            return self.y, self.y_ring, self.y_to
        return self.z, self.z_ring, self.z_to


def greet(others):
    barrier = pltpu.get_barrier_semaphore()
    for other in others:
        pl.semaphore_signal(barrier, inc=1, device_id=other, device_id_type=MESH)


def await_greetings(others):
    pl.semaphore_wait(pltpu.get_barrier_semaphore(), len(others))


def add_to(ref, *others):
    got = ref[...].astype(F32)
    for other in others:
        got += other[...].astype(F32)
    ref[...] = got.astype(ref.dtype)


def run_out(*steps):
    steps = list(steps)
    while steps:
        for s in list(steps):
            if next(s, "done") == "done":
                steps.remove(s)


def x_sum(place, sends, blocks_ref, out_ref, mine, theirs, total, from_left, from_right, sems):
    rows = out_ref.shape[0]
    half = rows // 2
    low, high = pl.ds(0, half), pl.ds(half, half)
    to_right, to_left = place.x_to[:2]
    flip = 1 - 2 * place.core
    keeps = Keeps(sems)
    swaps, loads = [], []
    for k, dest in enumerate((place.far, place.right, place.left, place.part)):
        swaps.append(sends.start(blocks_ref.at[dest + flip], theirs.at[k], place.partner))
        loads.append(keeps.start(blocks_ref.at[dest], mine.at[k]))

    def add_up(k):
        loads[k].wait()
        swaps[k].wait_recv()
        total[k] = (mine[k].astype(F32) + theirs[k].astype(F32)).astype(BF16)

    yield
    add_up(0)
    far_low = sends.start(total.at[0, low], from_left.at[0], to_right)
    far_high = sends.start(total.at[0, high], from_right.at[0], to_left)
    add_up(1)
    right_high = sends.start(total.at[1, high], from_left.at[2], to_right)
    add_up(2)
    left_low = sends.start(total.at[2, low], from_right.at[2], to_left)
    yield
    far_low.wait_recv()
    add_to(total.at[1, low], from_left.at[0])
    right_low = sends.start(total.at[1, low], from_left.at[1], to_right)
    far_high.wait_recv()
    add_to(total.at[2, high], from_right.at[0])
    left_high = sends.start(total.at[2, high], from_right.at[1], to_left)
    yield
    loads[3].wait()
    swaps[3].wait_recv()
    out_ref[...] = mine[3].astype(F32) + theirs[3].astype(F32)
    right_high.wait_recv()
    left_low.wait_recv()
    right_low.wait_recv()
    left_high.wait_recv()
    add_to(out_ref.at[low], from_left.at[1], from_right.at[2])
    add_to(out_ref.at[high], from_left.at[2], from_right.at[1])
    yield


def x_buffers(rows, columns):
    return [
        pltpu.VMEM((4, rows, columns), BF16),
        pltpu.VMEM((4, rows, columns), BF16),
        pltpu.VMEM((3, rows, columns), BF16),
        pltpu.VMEM((3, rows // 2, columns), BF16),
        pltpu.VMEM((3, rows // 2, columns), BF16),
        semaphores(4),
    ]


class Strip:
    def __init__(self, y_first, total, bufs, own=None, other=None):
        self.y_first, self.total, self.own, self.other = y_first, total, own, other
        self.theirs, self.big, self.far, self.mid, self.midfar, self.near = bufs

    def block(self, ref, w):
        return ref.at[w] if self.y_first else ref.at[:, w]


def strip_buffers(rows, columns, shared=True):
    return [
        pltpu.VMEM((4, 4, rows, columns) if shared else (1, 1, rows, columns), BF16),
        pltpu.VMEM((2, 2, 2, rows, columns), BF16),
        pltpu.VMEM((2, 2, rows, columns), BF16),
        pltpu.VMEM((2, 2, rows // 2, columns), BF16),
        pltpu.VMEM((2, rows // 2, columns), BF16),
        pltpu.VMEM((4, rows, columns), BF16),
    ]


def dp_sum(place, sends, strips, sems):
    y, z = place.y, place.z
    keeps = Keeps(sems)
    swaps, loads = {}, {}
    for k in range(4):
        for i, s in enumerate(strips):
            me, (right, left, far), _ = place.ring(s.y_first)
            w = (far, right, left, me)[k]
            if s.other is not None:
                swaps[k, i] = sends.start(s.other(w), s.block(s.theirs, w), place.partner)
            if s.own is not None:
                loads[k, i] = keeps.start(s.own(w), s.block(s.total, w))
    yield

    def joined(k, i, s, w):
        if s.own is not None:
            loads[k, i].wait()
        if s.other is not None:
            swaps[k, i].wait_recv()
            add_to(s.block(s.total, w), s.block(s.theirs, w))

    def big(s, w, h):
        span = pl.ds(2 * h, 2)
        return s.total.at[w, span] if s.y_first else s.total.at[span, w]

    def small(s, w, h):
        half = s.total.shape[2] // 2
        at = pl.ds(h * half, half)
        return s.total.at[y, w, at] if s.y_first else s.total.at[w, z, at]

    for first, view in ((True, big), (False, small)):
        whole = lambda s: s.big if first else s.mid
        farther = lambda s: s.far if first else s.midfar
        ready = joined if first else lambda *_: None
        ring = lambda s: place.ring(s.y_first == first)
        going = []
        for i, s in enumerate(strips):
            _, (right, left, far), to = ring(s)
            ready(0, i, s, far)
            going.append(
                [sends.start(view(s, far, h), farther(s).at[h], to[h]) for h in range(2)]
            )
        for i, s in enumerate(strips):
            _, (right, left, far), to = ring(s)
            ready(1, i, s, right)
            ready(2, i, s, left)
            going[i].append(sends.start(view(s, right, 1), whole(s).at[0, 1], to[0]))
            going[i].append(sends.start(view(s, left, 0), whole(s).at[1, 0], to[1]))
        yield
        for i, s in enumerate(strips):
            _, (right, left, far), to = ring(s)
            for h, w in enumerate((right, left)):
                going[i][h].wait_recv()
                add_to(view(s, w, h), farther(s).at[h])
                going[i].append(sends.start(view(s, w, h), whole(s).at[h, h], to[h]))
        yield
        for i, s in enumerate(strips):
            me, _, _ = ring(s)
            ready(3, i, s, me)
            for copy in going[i][2:]:
                copy.wait_recv()
            for h in range(2):
                add_to(view(s, me, h), whole(s).at[0, h], whole(s).at[1, h])

    shares, back = [], []
    for s in strips:
        shares.append(
            [sends.start(s.total.at[y, z], s.near.at[i], place.x_to[i]) for i in range(3)]
        )
    yield
    for s, share in zip(strips, shares):
        for copy in share:
            copy.wait_recv()
        got = s.total[y, z].astype(F32)
        for i in range(3):
            got += s.near[i].astype(F32)
        s.result = s.theirs.at[y, z] if s.other is not None else s.theirs.at[0, 0]
        s.result[...] = got.astype(BF16)
        back.append(sends.start(s.result, s.near.at[3], place.partner))
    yield
    for copy in back:
        copy.wait_recv()
    yield


def gather_first_kernel(
    wq_ref, wk_ref, wv_ref, small_ref, rows_ref, note_ref,
    out_ref, small_out, rows_out, notes_out, strips_ref, local_sems, send_sems, recv_sems,
):
    place = Place()
    y, z, core, part = place.y, place.z, place.core, place.part
    neighbours = [*place.others, *place.y_to, *place.z_to]
    greet(neighbours)
    rows = wq_ref.shape[0]
    wide, narrow = wq_ref.shape[1] // 4, wk_ref.shape[1] // 2
    strip = wide + narrow
    for s in range(4):
        strips_ref[:, s * strip : s * strip + wide] = wq_ref[:, s * wide : (s + 1) * wide]
        other = (wk_ref, wv_ref)[s % 2]
        begin = s // 2 * narrow
        strips_ref[:, s * strip + wide : (s + 1) * strip] = other[:, begin : begin + narrow]
    await_greetings(neighbours)
    sends, keeps = Sends(send_sems, recv_sems), Keeps(local_sems)

    def columns(p):
        return pl.ds(pl.multiple_of((2 * core + p) * strip, 128), strip)

    class Piece:
        def __init__(self, src, out, cols, y_first):
            self.src, self.out, self.cols, self.y_first = src, out, cols, y_first

        def ring(self, first):
            return place.ring(self.y_first == first)

        def view(self, first, where, piece=None):
            if first:
                at = pl.ds(0, rows) if piece is None else pl.ds(piece * rows // 2, rows // 2)
                if self.y_first:
                    return self.out.at[where, z, at, self.cols]
                return self.out.at[y, where, at, self.cols]
            span = pl.ds(0, 4) if piece is None else pl.ds(2 * piece, 2)
            if self.y_first:
                return self.out.at[span, where, :, self.cols]
            return self.out.at[where, span, :, self.cols]

    pieces = [
        Piece(strips_ref.at[:, columns(0)], out_ref, columns(0), False),
        Piece(strips_ref.at[:, columns(1)], out_ref, columns(1), True),
        Piece(small_ref, small_out, pl.ds(0, small_ref.shape[1]), False),
    ]
    across = []

    def send_across(s, view):
        if s.out is out_ref:
            across.append(sends.start(view, view, place.partner))

    half = rows_ref.shape[0] // 2
    for first in (True, False):
        stage = []
        for s in pieces:
            me, _, to = s.ring(first)
            src = s.src if first else s.view(first, me)
            stage.append([sends.start(src, s.view(first, me), to[i]) for i in range(2)])
        if first:
            for s in pieces:
                keeps.start(s.src, s.out.at[y, z, :, s.cols])
            x_came = [sends.start(rows_ref, rows_out.at[part], to) for to in place.x_to[:2]]
            across.append(sends.start(rows_ref, rows_out.at[part], place.partner))
            across += [sends.start(note_ref, notes_out.at[part], to) for to in place.others]
            keeps.start(rows_ref, rows_out.at[part])
            keeps.start(note_ref, notes_out.at[part])
        else:
            for s in pieces:
                send_across(s, s.view(first, s.ring(first)[0]))
            far_rows = []
            for i, origin in enumerate((place.left, place.right)):
                x_came[i].wait_recv()
                view = rows_out.at[origin, pl.ds(i * half, half)]
                far_rows.append(sends.start(view, view, place.x_to[i]))
                view = rows_out.at[origin]
                across.append(sends.start(view, view, place.partner))
        onward = []
        for s, came in zip(pieces, stage):
            _, (right, left, _), to = s.ring(first)
            pair = []
            for i, origin in enumerate((left, right)):
                came[i].wait_recv()
                view = s.view(first, origin, i)
                pair.append(sends.start(view, view, to[i]))
                if not first:
                    send_across(s, s.view(first, origin))
            onward.append(pair)
        for s, pair in zip(pieces, onward):
            far = s.ring(first)[1][2]
            for i in range(2):
                pair[i].wait_recv()
                if not first:
                    send_across(s, s.view(first, far, i))
        if first:
            for copy in keeps.made[:3]:
                copy.wait()
    for i in range(2):
        far_rows[i].wait_recv()
        view = rows_out.at[place.far, pl.ds(i * half, half)]
        across.append(sends.start(view, view, place.partner))
    for copy in across:
        copy.wait_recv()
    for copy in keeps.made[3:]:
        copy.wait()
    sends.finish()


def gather_first(wq, wk, wv, small, rows, note, collective_id):
    height, total = wq.shape[0], wq.shape[1] + wk.shape[1] + wv.shape[1]
    return pl.pallas_call(
        gather_first_kernel,
        out_shape=[
            sds((4, 4, height, total), BF16),
            sds((4, 4, *small.shape), BF16),
            sds((8, *rows.shape), BF16),
            sds((8, *note.shape), note.dtype),
        ],
        in_specs=[VMEM] * 6,
        out_specs=[ANY] * 4,
        scratch_shapes=[
            pltpu.VMEM((height, total), BF16), semaphores(5), semaphores(50), semaphores(50)
        ],
        compiler_params=remote_params(collective_id, 16),
    )(wq, wk, wv, small, rows, note)


def qkv_kernel(
    tokens_ref, w_ref, gain_ref, cos_ref, sin_ref, normed_ref, query_ref, kv_ref,
    own_kv, local_sems, send_sems, recv_sems,
):
    place = Place()
    neighbours = [place.partner, *place.x_to[:2]]
    greet(neighbours)
    sends, keeps = Sends(send_sems, recv_sems), Keeps(local_sems)
    cosine, sine = cos_ref[...], sin_ref[...]
    inputs = tokens_ref[...].astype(F32)
    normed_ref[...] = (inputs * inverse_rms(inputs) * gain_ref[...]).astype(BF16)
    strip = w_ref.shape[1] // 4
    wide = strip - HEAD_SIZE
    for s in range(4):
        got = mm(normed_ref[...], w_ref[:, s * strip + wide : (s + 1) * strip])
        if s % 2 == 0:
            got = spin(got, cosine, sine)
        own_kv[:, s * HEAD_SIZE : (s + 1) * HEAD_SIZE] = got.astype(BF16)

    def queries(s):
        got = mm(normed_ref[...], w_ref[:, s * strip : s * strip + wide])
        for h in range(0, wide, HEAD_SIZE):
            head = spin(got[:, h : h + HEAD_SIZE], cosine, sine)
            query_ref[:, s * wide + h : s * wide + h + HEAD_SIZE] = head.astype(BF16)

    await_greetings(neighbours)
    half = own_kv.shape[0] // 2
    slot = kv_ref.at[place.part]
    came = [sends.start(own_kv, slot, way) for way in place.x_to[:2]]
    across = [sends.start(own_kv, slot, place.partner)]
    keeps.start(own_kv, slot)
    queries(0)
    queries(1)
    onward = []
    for i, origin in enumerate((place.left, place.right)):
        came[i].wait_recv()
        view = kv_ref.at[origin, pl.ds(i * half, half)]
        onward.append(sends.start(view, view, place.x_to[i]))
        view = kv_ref.at[origin]
        across.append(sends.start(view, view, place.partner))
    queries(2)
    queries(3)
    for i in range(2):
        onward[i].wait_recv()
        view = kv_ref.at[place.far, pl.ds(i * half, half)]
        across.append(sends.start(view, view, place.partner))
    for copy in across:
        copy.wait_recv()
    keeps.made[0].wait()
    sends.finish()


def qkv(tokens, w, gain, cosine, sine, collective_id):
    rows, width = tokens.shape
    kv_width = w.shape[1] - width
    return pl.pallas_call(
        qkv_kernel,
        out_shape=[
            sds((rows, width), BF16), sds((rows, width), BF16), sds((8, rows, kv_width), BF16)
        ],
        in_specs=[VMEM] * 5,
        out_specs=[VMEM, VMEM, ANY],
        scratch_shapes=[
            pltpu.VMEM((rows, kv_width), BF16), semaphores(1), semaphores(9), semaphores(9)
        ],
        compiler_params=remote_params(collective_id, 40),
    )(tokens, w, gain, cosine, sine)


def fill_bias(bias, start_ref, first_row):
    length, rows = bias.shape
    places = lax.broadcasted_iota(jnp.int32, (length, rows), 0)
    mine = first_row + lax.broadcasted_iota(jnp.int32, (length, rows), 1)
    keep = (places >= start_ref[...]) & (places <= mine)
    bias[...] = jnp.where(keep, 0.0, MASK_FILL)


def attend_kernel(start_ref, q_ref, kv_ref, ctx_ref, lse_ref, bias, v_t, scores):
    head = pl.program_id(0)
    length = bias.shape[0]

    @pl.when(head == 0)
    def _():
        fill_bias(bias, start_ref, start_ref.shape[1] * lax.axis_index("expert"))

    @pl.when(head % GROUP == 0)
    def _():
        v_t[...] = kv_ref[:, HEAD_SIZE:].astype(F32).T.astype(BF16)

    query = q_ref[...]
    top = None
    for at in range(0, length, BLOCK):
        span = pl.ds(at, BLOCK)
        s = mm_nt(kv_ref[span, :HEAD_SIZE], query) + bias[span]
        scores[span] = s
        here = jnp.max(s, axis=0, keepdims=True)
        top = here if top is None else jnp.maximum(top, here)
    total = jnp.zeros_like(top)
    context = jnp.zeros((HEAD_SIZE, query.shape[0]), F32)
    for at in range(0, length, BLOCK):
        span = pl.ds(at, BLOCK)
        p = jnp.exp2((scores[span] - top) * (SCALE * LOG2E))
        total += jnp.sum(p, axis=0, keepdims=True)
        context += mm(v_t[:, span], p.astype(BF16))
    ctx_ref[...] = (context / total).T.astype(BF16)
    lse_ref[0] = top * (SCALE * LOG2E) + jnp.log2(total)


def attend(start, query, kv):
    rows, width = query.shape
    length = kv.shape[0]
    by_head = pl.BlockSpec((rows, HEAD_SIZE), lambda h: (0, h))
    return pl.pallas_call(
        attend_kernel,
        grid=(QUERY_HEADS,),
        out_shape=[sds((rows, width), BF16), sds((QUERY_HEADS, 1, rows), F32)],
        in_specs=[
            pl.BlockSpec((1, rows), lambda h: (0, 0)),
            by_head,
            pl.BlockSpec((length, 2 * HEAD_SIZE), lambda h: (0, h // GROUP)),
        ],
        out_specs=[by_head, pl.BlockSpec((1, 1, rows), lambda h: (h, 0, 0))],
        scratch_shapes=[
            pltpu.VMEM((length, rows), F32),
            pltpu.VMEM((HEAD_SIZE, length), BF16),
            pltpu.VMEM((length, rows), F32),
        ],
        compiler_params=pltpu.CompilerParams(vmem_limit_bytes=40 * MIB),
        cost_estimate=pl.CostEstimate(
            flops=4 * rows * length * width, bytes_accessed=4 * length * width, transcendentals=0
        ),
    )(start, query, kv)


LOW, HIGH = 0, 1


def gelu_parts(a):
    k = (2.0 / jnp.pi) ** 0.5
    square = a * a
    t = jnp.tanh(k * a * (1.0 + 0.044715 * square))
    slope = 0.5 * (1.0 + t) + 0.5 * a * (1.0 - t * t) * k * (1.0 + 3 * 0.044715 * square)
    return 0.5 * a * (1.0 + t), slope


def experts_kernel(
    ctx_ref, tokens_ref, small_ref, gain_ref, member_ref, slot_ref,
    up_all, wo_hbm, wg_hbm, wu_hbm, wd_hbm,
    middle_ref, gates_ref, gg_all, sums_ref, own_ref, back_out, w_grads,
    wo_ref, wg_ref, wu_ref, wd_ref, rows_all, returns, arrived, pair_grad, hidden, grad_pre,
    theirs, far_left, far_right, from_left, from_right, tile, tile_d, back_rows, gates_all, gg_src,
    local_sems, tile_sems, back_sems, send_sems, recv_sems,
):
    place = Place()
    part, core = place.part, place.core
    right, left, far = place.right, place.left, place.far
    to_right, to_left = place.x_to[:2]
    greet(place.others)
    sends, keeps, stores = (
        Sends(send_sems, recv_sems), Keeps(local_sems), Keeps(back_sems)
    )
    rows, width = ctx_ref.shape
    half = rows // 2
    halves = (pl.ds(0, half), pl.ds(half, half))
    ff = wg_ref.shape[1]
    capacity = arrived.shape[0] // 8

    for src, dst in ((wo_hbm, wo_ref), (wg_hbm, wg_ref), (wu_hbm, wu_ref), (wd_hbm, wd_ref)):
        keeps.start(src, dst)
    chips = [lax.rem(place.chip + d, 4) for d in (0, 3, 1, 2)]
    for u in range(4):
        keeps.start(up_all.at[pl.ds(2 * chips[u], 2)], returns.at[u])

    keeps.made[0].wait()
    middle = tokens_ref[...].astype(F32) + mm(ctx_ref[...], wo_ref[...])
    middle_ref[...] = middle
    normed = (middle * inverse_rms(middle) * gain_ref[...]).astype(BF16)
    rows_all[part] = normed
    member = member_ref[...]
    logits = jnp.where(member > 0.0, mm(normed, small_ref[...]), MASK_FILL)
    weight = jnp.exp(logits - jnp.max(logits, axis=-1, keepdims=True)) * member
    gates = weight / jnp.sum(weight, axis=-1, keepdims=True)
    gates_ref[...] = gates.T[:EXPERTS]

    await_greetings(place.others)
    mine = rows_all.at[part]
    go_right = sends.start(mine, mine, to_right)
    go_left = sends.start(mine, mine, to_left)
    swap_own = sends.start(mine, mine, place.partner)
    note_sends = [sends.start(gates_ref, gates_all.at[part], to) for to in place.others]
    gates_all[part] = gates_ref[...]

    def pick_of(source):
        slots = lax.broadcasted_iota(jnp.int32, (capacity, rows), 0)
        return slots == slot_ref[source]

    for u in range(4):
        keeps.made[4 + u].wait()
        for c in range(2):
            pick = pick_of(2 * chips[u] + c).astype(BF16)
            got = mm(pick, returns[u, c])
            pair_grad[pl.ds((2 * u + c) * capacity, capacity)] = got.astype(BF16)
    for load in keeps.made[1:4]:
        load.wait()

    swaps, gg_sends = [], []

    def unit(u):
        at = chips[u]
        picks = [pick_of(2 * at + c) for c in range(2)]
        picks_b = [pick.astype(BF16) for pick in picks]
        spans = [pl.ds((2 * u + c) * capacity, capacity) for c in range(2)]
        both = pl.ds(2 * u * capacity, 2 * capacity)
        gate = []
        for c in range(2):
            arrived[spans[c]] = mm(picks_b[c], rows_all[2 * at + c]).astype(BF16)
            row = gates_all[2 * at + c, pl.ds(part, 1)]
            gate.append(jnp.sum(jnp.where(picks[c], row, 0.0), axis=-1, keepdims=True))
        gate = jnp.concatenate(gate, axis=0)
        x = arrived[both]
        a, b = mm(x, wg_ref[...]), mm(x, wu_ref[...])
        act, slope = gelu_parts(a)
        h = (act * b).astype(BF16)
        hidden[both] = h
        out = mm(h, wd_ref[...]).astype(BF16).astype(F32)
        up = pair_grad[both].astype(F32)
        gg = jnp.sum(up * out, axis=-1, keepdims=True)
        weighted = (gate * out).astype(BF16)
        pg = (gate * up).astype(BF16)
        pair_grad[both] = pg
        for c in range(2):
            if u > 0:
                stores.made[2 * (u - 1) + c].wait()
            back_rows[c] = mm_tn(picks_b[c], weighted[c * capacity : (c + 1) * capacity]).astype(
                BF16
            )
            stores.start(back_rows.at[c], back_out.at[2 * at + c])
            gg_c = gg[c * capacity : (c + 1) * capacity]
            row = jnp.sum(jnp.where(picks[c], gg_c, 0.0), axis=0, keepdims=True)
            gg_src[u, c] = jnp.broadcast_to(row, (8, rows))
        grad_h = mm_nt(pg, wd_ref[...])
        grad_a = (grad_h * b * slope).astype(BF16)
        grad_b = (grad_h * act).astype(BF16)
        grad_pre[both, :ff] = grad_a
        grad_pre[both, ff:] = grad_b
        grad_rows = (mm_nt(grad_a, wg_ref[...]) + mm_nt(grad_b, wu_ref[...])).astype(BF16)
        for c in range(2):
            returns[u, c] = mm_tn(
                picks_b[c], grad_rows[c * capacity : (c + 1) * capacity]
            ).astype(BF16)
        swaps.append(sends.start(returns.at[u, 1 - core], theirs.at[u], place.partner))
        if u == 0:
            gg_all[part] = gg_src[0, core]
            gg_sends.append(sends.start(gg_src.at[0, 1 - core], gg_all.at[part], place.partner))
        else:
            for c in (core, 1 - core):
                gg_sends.append(
                    sends.start(gg_src.at[u, c], gg_all.at[part], {"expert": 2 * at + c})
                )

    def joined(u):
        swaps[u].wait_recv()
        add_to(theirs.at[u], returns.at[u, core])

    swap_own.wait_recv()
    for copy in note_sends:
        copy.wait_recv()
    unit(0)
    go_right.wait_recv()
    first = rows_all.at[left, halves[LOW]]
    far_low = sends.start(first, first, to_right)
    swap_left = sends.start(rows_all.at[left], rows_all.at[left], place.partner)
    go_left.wait_recv()
    second = rows_all.at[right, halves[HIGH]]
    far_high = sends.start(second, second, to_left)
    swap_right = sends.start(rows_all.at[right], rows_all.at[right], place.partner)
    swap_left.wait_recv()
    unit(1)
    swap_right.wait_recv()
    unit(2)
    swap_far = []
    for h, copy in enumerate((far_low, far_high)):
        copy.wait_recv()
        piece = rows_all.at[far, halves[h]]
        swap_far.append(sends.start(piece, piece, place.partner))
    joined(1)
    joined(2)
    back_right = sends.start(theirs.at[2, halves[HIGH]], from_left, to_right)
    back_left = sends.start(theirs.at[1, halves[LOW]], from_right, to_left)
    for copy in swap_far:
        copy.wait_recv()
    unit(3)
    joined(3)
    back_far_low = sends.start(theirs.at[3, halves[LOW]], far_left, to_right)
    back_far_high = sends.start(theirs.at[3, halves[HIGH]], far_right, to_left)

    tall = 4 * w_grads.shape[2] * 2 // 3
    high = tall // 4
    w_stores = Keeps(tile_sems)
    for i in range(ff // tall):
        got = mm_tn(hidden[:, i * tall : (i + 1) * tall], pair_grad[...]).astype(BF16)
        tile_d[i] = got.reshape(tile_d.shape[1:])
        w_stores.start(tile_d.at[i], w_grads.at[pl.ds(2 * i, 2), :, pl.ds(high, high // 2)])
    for i in range(width // tall):
        if i >= 2:
            w_stores.made[ff // tall + i - 2].wait()
        got = mm_tn(arrived[:, i * tall : (i + 1) * tall], grad_pre[...]).astype(BF16)
        tile[i % 2] = got.reshape(tile.shape[1:])
        w_stores.start(tile.at[i % 2], w_grads.at[i, :, pl.ds(0, high)])

    swaps[0].wait_recv()
    back_right.wait_recv()
    back_left.wait_recv()
    own_ref[...] = theirs[0].astype(F32) + returns[0, core].astype(F32)
    add_to(own_ref.at[halves[HIGH]], from_left)
    add_to(own_ref.at[halves[LOW]], from_right)
    back_far_low.wait_recv()
    sums_ref[0] = (theirs[2, halves[LOW]].astype(F32) + far_left[...].astype(F32)).astype(BF16)
    back_far_high.wait_recv()
    sums_ref[1] = (theirs[1, halves[HIGH]].astype(F32) + far_right[...].astype(F32)).astype(BF16)
    for copy in gg_sends:
        copy.wait_recv()
    for copy in [*stores.made[6:], *w_stores.made[: ff // tall], *w_stores.made[-2:]]:
        copy.wait()
    sends.finish()


def experts(ctx, tokens, small, gain, member, slots, up_all, wo, wg, wu, wd, collective_id):
    rows, width = ctx.shape
    ff = wg.shape[1]
    capacity = rows * 9 // 16
    high = width // 16
    vmem = pltpu.VMEM
    return pl.pallas_call(
        experts_kernel,
        out_shape=[
            sds((rows, width), F32),
            sds((EXPERTS, rows), F32),
            sds((8, 8, rows), F32),
            sds((2, rows // 2, width), BF16),
            sds((rows, width), F32),
            sds((8, rows, width), BF16),
            sds((4, 4, high * 3 // 2, width), BF16),
        ],
        in_specs=[VMEM] * 6 + [ANY] * 5,
        out_specs=[VMEM] * 5 + [ANY] * 2,
        scratch_shapes=[
            vmem((width, width), BF16),
            vmem((width, ff), BF16),
            vmem((width, ff), BF16),
            vmem((ff, width), BF16),
            vmem((8, rows, width), BF16),
            vmem((4, 2, rows, width), BF16),
            vmem((8 * capacity, width), BF16),
            vmem((8 * capacity, width), BF16),
            vmem((8 * capacity, ff), BF16),
            vmem((8 * capacity, 2 * ff), BF16),
            vmem((4, rows, width), BF16),
            *[vmem((rows // 2, width), BF16)] * 4,
            vmem((2, 4, high, width), BF16),
            vmem((2, 2, 4, high // 2, width), BF16),
            vmem((2, rows, width), BF16),
            vmem((8, EXPERTS, rows), F32),
            vmem((4, 2, 8, rows), F32),
            semaphores(8),
            semaphores(6),
            semaphores(8),
            semaphores(40),
            semaphores(40),
        ],
        compiler_params=remote_params(collective_id, 63),
    )(ctx, tokens, small, gain, member, slots, up_all, wo, wg, wu, wd)


def after_kernel(
    middle_ref, gates_ref, gg_all, sums_ref, own_ref, d_out_ref, ctx_ref, small_ref, gain_ref,
    wo_ref, grad_middle_ref, grad_ctx_ref, small_grad_ref, grad_wo_ref,
    from_left, from_right, send_sems, recv_sems,
):
    place = Place()
    greet(place.x_to[:2])
    await_greetings(place.x_to[:2])
    sends = Sends(send_sems, recv_sems)
    came = [
        sends.start(sums_ref.at[i], dst, place.x_to[i])
        for i, dst in enumerate((from_left, from_right))
    ]
    rows, width = middle_ref.shape
    half = rows // 2
    grad_gates = jnp.concatenate([gg_all[e, :1] for e in range(EXPERTS)], axis=0)
    gates_t = gates_ref[...]
    products = gates_t * grad_gates
    grad_logits = products - gates_t * jnp.sum(products, axis=0, keepdims=True)
    grad_logits = jnp.concatenate(
        [grad_logits, jnp.zeros((128 - EXPERTS, rows), F32)], axis=0
    ).T.astype(BF16)
    total = own_ref[...] + mm_nt(grad_logits, small_ref[...])
    middle, gain = middle_ref[...], gain_ref[...]
    inverse = inverse_rms(middle)
    scaled = middle * inverse
    small_grad = mm_tn((scaled * gain).astype(BF16), grad_logits)
    for copy in came:
        copy.wait_recv()
    total += jnp.concatenate([from_left[...], from_right[...]], axis=0).astype(F32)
    grad_gain = jnp.sum(total * scaled, axis=0, keepdims=True)
    lanes = lax.broadcasted_iota(jnp.int32, (width, 128), 1)
    small_grad += jnp.where(lanes == EXPERTS, as_column(grad_gain, 128), 0.0)
    small_grad_ref[...] = small_grad.astype(BF16)
    weighted = total * gain
    inner = jnp.mean(weighted * scaled, axis=-1, keepdims=True)
    grad_middle = d_out_ref[...].astype(F32) + inverse * (weighted - scaled * inner)
    grad_middle_ref[...] = grad_middle
    grad_attn = grad_middle.astype(BF16)
    grad_ctx_ref[...] = mm_nt(grad_attn, wo_ref[...]).astype(BF16)
    tall = 256
    for at in range(0, width, tall):
        grad_wo_ref[pl.ds(at, tall)] = mm_tn(ctx_ref[:, at : at + tall], grad_attn).astype(BF16)
    sends.finish()


def after(middle, gates, gg, sums, own, d_out, ctx, small, gain, wo, collective_id):
    rows, width = middle.shape
    return pl.pallas_call(
        after_kernel,
        out_shape=[
            sds((rows, width), F32),
            sds((rows, width), BF16),
            sds((width, 128), BF16),
            sds((width, width), BF16),
        ],
        in_specs=[VMEM] * 10,
        out_specs=[VMEM] * 4,
        scratch_shapes=[
            pltpu.VMEM((rows // 2, width), BF16),
            pltpu.VMEM((rows // 2, width), BF16),
            semaphores(2),
            semaphores(2),
        ],
        compiler_params=remote_params(collective_id, 56),
    )(middle, gates, gg, sums, own, d_out, ctx, small, gain, wo)


def attend_back_kernel(
    start_ref, q_ref, kv_ref, g_ref, lse_ref, cos_ref, sin_ref, middle_ref, wo_grads, blocks_ref,
    gq_ref, gkv_ref, wo_out, mixed_ref,
    bias, k_t, gkv, probs, grad_probs, combined, *refs,
):
    place = Place()
    neighbours = [place.partner, *place.x_to, *place.y_to, *place.z_to]
    greet(neighbours)
    totals, bufs, x_bufs = refs[:2], refs[2:14], refs[14:20]
    local_sems, send_sems, recv_sems = refs[20:]
    length, rows = bias.shape
    fill_bias(bias, start_ref, rows * place.part)
    await_greetings(neighbours)
    sends = Sends(send_sems, recv_sems)
    quarter = wo_grads.shape[3] // 4

    def columns(c, p):
        return pl.ds(pl.multiple_of((2 * c + p) * quarter, 128), quarter)

    def source(c, p):
        cols = columns(c, p)
        if p == 0:
            return lambda w: wo_grads.at[w, :, :, cols]
        return lambda w: wo_grads.at[:, w, :, cols]

    strips = [
        Strip(
            p == 0, totals[p], bufs[6 * p : 6 * p + 6],
            source(place.core, p), source(1 - place.core, p),
        )
        for p in range(2)
    ]
    dense = dp_sum(place, sends, strips, local_sems)
    rest = x_sum(place, sends, blocks_ref, combined, *x_bufs)
    next(dense)
    next(rest)

    for group in range(KEY_VALUE_HEADS):
        keys = slice(2 * group * HEAD_SIZE, (2 * group + 1) * HEAD_SIZE)
        values = slice((2 * group + 1) * HEAD_SIZE, (2 * group + 2) * HEAD_SIZE)
        k_t[...] = kv_ref[:, keys].astype(F32).T.astype(BF16)
        gkv[...] = jnp.zeros_like(gkv)

        def one_head(i, carry, base):
            head = base + i
            cols = pl.ds(pl.multiple_of(head * HEAD_SIZE, HEAD_SIZE), HEAD_SIZE)
            query, grad = q_ref[:, cols], g_ref[:, cols]
            lse = lse_ref[head]
            inner = jnp.zeros_like(lse)
            for at in range(0, length, BLOCK):
                span = pl.ds(at, BLOCK)
                s = mm_nt(kv_ref[span, keys], query) + bias[span]
                p = jnp.exp2(s * (SCALE * LOG2E) - lse)
                gp = mm_nt(kv_ref[span, values], grad)
                inner += jnp.sum(p * gp, axis=0, keepdims=True)
                probs[span] = p
                grad_probs[span] = gp
                gkv[span, HEAD_SIZE:] += mm(p.astype(BF16), grad)
            gq = jnp.zeros((HEAD_SIZE, rows), F32)
            for at in range(0, length, BLOCK):
                span = pl.ds(at, BLOCK)
                gs = (probs[span] * (grad_probs[span] - inner)).astype(BF16)
                gkv[span, :HEAD_SIZE] += mm(gs, query)
                gq += mm(k_t[:, span], gs)
            gq_ref[:, cols] = spin(gq.T * SCALE, cos_ref[...], -sin_ref[...]).astype(BF16)
            return carry

        for base in range(group * GROUP, (group + 1) * GROUP, 2):
            lax.fori_loop(0, 2, lambda i, carry, base=base: one_head(i, carry, base), 0)
            next(dense, None)
            next(rest, None)
        gkv_ref[:, keys] = (gkv[:, :HEAD_SIZE] * SCALE).astype(BF16)
        gkv_ref[:, values] = gkv[:, HEAD_SIZE:].astype(BF16)
    run_out(dense, rest)
    mixed_ref[...] = (middle_ref[...] + combined[...]).astype(BF16)
    for p, s in enumerate(strips):
        wo_out[:, columns(place.core, p)] = s.result[...].astype(F32)
        wo_out[:, columns(1 - place.core, p)] = s.near[3].astype(F32)
    sends.finish()


def attend_back(
    start, query, kv, grad, lse, cosine, sine, middle, grad_wo, back_out, collective_id
):
    rows, width = query.shape
    length = kv.shape[0]
    height = grad_wo.shape[2]
    quarter = width // 4
    return pl.pallas_call(
        attend_back_kernel,
        out_shape=[
            sds((rows, width), BF16),
            sds(kv.shape, BF16),
            sds((height, width), F32),
            sds((rows, width), BF16),
        ],
        in_specs=[VMEM] * 8 + [ANY] * 2,
        out_specs=[VMEM] * 4,
        scratch_shapes=[
            pltpu.VMEM((length, rows), F32),
            pltpu.VMEM((HEAD_SIZE, length), BF16),
            pltpu.VMEM((length, 2 * HEAD_SIZE), F32),
            pltpu.VMEM((length, rows), F32),
            pltpu.VMEM((length, rows), F32),
            pltpu.VMEM((rows, width), F32),
            *[pltpu.VMEM((4, 4, height, quarter), BF16)] * 2,
            *strip_buffers(height, quarter),
            *strip_buffers(height, quarter),
            *x_buffers(rows, width),
            semaphores(8),
            semaphores(60),
            semaphores(60),
        ],
        compiler_params=remote_params(collective_id, 60),
    )(start, query, kv, grad, lse, cosine, sine, middle, grad_wo, back_out)


def last_kernel(
    kv_terms, gq_ref, normed_ref, tokens_ref, gain_ref, cos_ref, sin_ref, grad_middle_ref,
    small_ref, w_hbm,
    grad_tokens_ref, wq_out, wk_out, wv_out, small_out,
    grads, small_total, w_ref, normed_t, lin_kv, kv_sum, *refs,
):
    place = Place()
    core = place.core
    neighbours = [place.partner, *place.x_to, *place.y_to, *place.z_to]
    greet(neighbours)
    bufs, x_bufs = refs[:18], refs[18:24]
    w_sem, local_sems, send_sems, recv_sems = refs[24:]
    load = pltpu.make_async_copy(w_hbm, w_ref, w_sem)
    load.start()
    await_greetings(neighbours)
    sends = Sends(send_sems, recv_sems)
    kv_steps = x_sum(place, sends, kv_terms, kv_sum, *x_bufs)
    next(kv_steps)
    strip = grads.shape[-1]
    wide = strip - HEAD_SIZE
    rows, width = normed_ref.shape
    height = grads.shape[3]

    def put(s, cols, right_side):
        got = mm(normed_t[...], right_side).astype(BF16)
        grads[s, :, :, :, cols] = got.reshape(4, 4, height, right_side.shape[1])

    normed_t[...] = normed_ref[...].astype(F32).T.astype(BF16)
    for s in range(4):
        put(s, pl.ds(0, wide), gq_ref[:, s * wide : (s + 1) * wide])
        next(kv_steps, None)
    run_out(kv_steps)
    cosine, sine = cos_ref[...], sin_ref[...]
    for s in range(4):
        got = kv_sum[:, s * HEAD_SIZE : (s + 1) * HEAD_SIZE]
        if s % 2 == 0:
            got = spin(got, cosine, -sine)
        got = got.astype(BF16)
        lin_kv[:, s * HEAD_SIZE : (s + 1) * HEAD_SIZE] = got
        put(s, pl.ds(wide, HEAD_SIZE), got)

    def source(s, y_first):
        if y_first:
            return lambda w: grads.at[s, w]
        return lambda w: grads.at[s, :, w]

    strips = [
        Strip(
            p == 0, grads.at[2 * core + p], bufs[6 * p : 6 * p + 6],
            None, source(2 * (1 - core) + p, p == 0),
        )
        for p in range(2)
    ]
    wide_steps = dp_sum(place, sends, strips, local_sems)
    next(wide_steps)
    next(wide_steps)

    load.wait()
    grad_normed = None
    for s in range(4):
        at = s * strip
        term = mm_nt(gq_ref[:, s * wide : (s + 1) * wide], w_ref[:, at : at + wide])
        term += mm_nt(
            lin_kv[:, s * HEAD_SIZE : (s + 1) * HEAD_SIZE], w_ref[:, at + wide : at + strip]
        )
        grad_normed = term if grad_normed is None else grad_normed + term
    grad_inputs, grad_gain = rms_back(tokens_ref[...].astype(F32), gain_ref[...], grad_normed)
    grad_tokens_ref[...] = grad_middle_ref[...] + grad_inputs
    lanes = lax.broadcasted_iota(jnp.int32, (width, 128), 1)
    small = jnp.where(
        lanes == EXPERTS + 1, as_column(grad_gain, 128), small_ref[...].astype(F32)
    )
    small_total[...] = small.astype(BF16).reshape(small_total.shape)
    small_strip = Strip(True, small_total, bufs[12:18])
    small_steps = dp_sum(place, sends, [small_strip], local_sems)
    next(small_steps)
    run_out(small_steps, wide_steps)
    small_out[...] = small_strip.result[...].astype(F32) + small_strip.near[3].astype(F32)
    for p, (s, other) in enumerate(zip(strips, (wk_out, wv_out))):
        for c, got in ((core, s.result[...]), (1 - core, s.near[3])):
            got = got.astype(F32)
            at = pl.multiple_of((2 * c + p) * wide, 128)
            wq_out[:, pl.ds(at, wide)] = got[:, :wide]
            at = pl.multiple_of(c * HEAD_SIZE, 128)
            other[:, pl.ds(at, HEAD_SIZE)] = got[:, wide:]
    sends.finish()


def last(
    kv_terms, grad_query, normed, tokens, gain, cosine, sine, grad_middle, small, w, collective_id
):
    rows, width = normed.shape
    total = w.shape[1]
    height, strip = width // 16, total // 4
    kv_width = total - width
    vmem = pltpu.VMEM
    return pl.pallas_call(
        last_kernel,
        out_shape=[
            sds((rows, width), F32),
            sds((height, width), F32),
            sds((height, kv_width // 2), F32),
            sds((height, kv_width // 2), F32),
            sds((height, 128), F32),
        ],
        in_specs=[ANY] + [VMEM] * 8 + [ANY],
        out_specs=[VMEM] * 5,
        scratch_shapes=[
            vmem((4, 4, 4, height, strip), BF16),
            vmem((4, 4, height, 128), BF16),
            vmem((width, total), BF16),
            vmem((width, rows), BF16),
            vmem((rows, kv_width), BF16),
            vmem((rows, kv_width), F32),
            *strip_buffers(height, strip),
            *strip_buffers(height, strip),
            *strip_buffers(height, 128, shared=False),
            *x_buffers(rows, kv_width),
            pltpu.SemaphoreType.DMA,
            semaphores(8),
            semaphores(80),
            semaphores(80),
        ],
        compiler_params=remote_params(collective_id, 60),
    )(kv_terms, grad_query, normed, tokens, gain, cosine, sine, grad_middle, small, w)


def widen_kernel(late_ref, sums_ref, g_out, u_out, d_out):
    high, ff = g_out.shape
    g_out[...] = sums_ref[0, :high, :ff].astype(F32)
    u_out[...] = sums_ref[0, :high, ff:].astype(F32)
    d_out[...] = sums_ref[0, high:].astype(F32)


def widen(sums, late):
    owners, high, width = sums.shape
    ff = width // 2
    gu, d = high * 2 // 3, high // 3
    spec = lambda a, b: pl.BlockSpec((a, b), lambda i: (i, 0))
    return pl.pallas_call(
        widen_kernel,
        grid=(owners,),
        out_shape=[
            sds((owners * gu, ff), F32), sds((owners * gu, ff), F32), sds((owners * d, width), F32)
        ],
        in_specs=[ANY, pl.BlockSpec((1, high, width), lambda i: (i, 0, 0))],
        out_specs=[spec(gu, ff), spec(gu, ff), spec(d, width)],
        cost_estimate=pl.CostEstimate(flops=0, bytes_accessed=21 * MIB, transcendentals=0),
    )(late, sums)


def on_device(
    tokens,
    d_out,
    gain_in,
    w_query,
    key_projection_weight,
    value_projection_weight,
    w_out,
    gain_mid,
    w_router,
    w_gate,
    w_up,
    w_down,
    routes,
    segments,
):
    rows, width = tokens.shape
    length = segments.shape[1]
    part = lax.axis_index("expert")
    seg_row = segments[0]
    offset = part * rows
    my_seg = lax.dynamic_slice_in_dim(seg_row, offset, rows, 0)
    start = jnp.sum((seg_row[None, :] < my_seg[:, None]).astype(jnp.int32), axis=1)
    angles = angles_for(offset + jnp.arange(rows, dtype=jnp.int32) - start)
    cosine, sine = jnp.cos(angles), jnp.sin(angles)
    cosine = jnp.concatenate([cosine, cosine], axis=1)
    sine = jnp.concatenate([-sine, sine], axis=1)
    start = start[None, :]

    small = jnp.concatenate([w_router, gain_mid[:, None], gain_in[:, None]], axis=1)
    small = jnp.pad(small, ((0, 0), (0, 128 - small.shape[1])))
    note = jnp.pad(routes.T, ((0, 8 - TOPK), (0, 0)))
    w_strips, small, upstream_all, notes = gather_first(
        w_query, key_projection_weight, value_projection_weight, small, d_out, note, 1
    )
    w_strips = w_strips.reshape(width, -1)
    small = small.reshape(width, -1)
    gain_mid_row = small[:, EXPERTS].astype(F32)[None, :]
    gain_in_row = small[:, EXPERTS + 1].astype(F32)[None, :]
    wo = gather_dense(w_out, part % 2)

    normed, query, kv_all = qkv(tokens, w_strips, gain_in_row, cosine, sine, 2)
    kv_all = kv_all.reshape(length, -1)
    context, lse = attend(start, query, kv_all)

    member = jnp.any(routes[:, :, None] == jnp.arange(128, dtype=jnp.int32), axis=1).astype(F32)
    chosen = jnp.any(notes[:, :TOPK] == part, axis=1)
    slots = jnp.where(chosen, jnp.cumsum(chosen.astype(jnp.int32), axis=1) - 1, -1)[:, None, :]
    middle, gates, gg, sums, own, back_out, w_grads = experts(
        context, tokens, small, gain_mid_row, member, slots, upstream_all,
        wo, w_gate[0], w_up[0], w_down[0], 3,
    )
    w_sums = lax.psum(w_grads.reshape(-1, *w_grads.shape[2:]), "dp")

    grad_middle, grad_ctx, small_grads, grad_wo = after(
        middle, gates, gg, sums, own, d_out, context, small, gain_mid_row, wo, 4
    )
    grad_wo = grad_wo.reshape(4, 4, width // 16, width)
    grad_query, kv_terms, g_wo, mixed = attend_back(
        start, query, kv_all, grad_ctx, lse, cosine, sine, middle, grad_wo, back_out, 5
    )
    grad_tokens, g_wq, g_wk, g_wv, small_sum = last(
        kv_terms.reshape(8, rows, -1), grad_query, normed, tokens, gain_in_row, cosine, sine,
        grad_middle, small_grads, w_strips, 6,
    )
    return (
        mixed,
        grad_tokens,
        small_sum[:, EXPERTS + 1],
        g_wq,
        g_wk,
        g_wv,
        g_wo,
        small_sum[:, EXPERTS],
        small_sum[:, :EXPERTS],
        *(g[None] for g in widen(w_sums, small_sum)),
    )


def solution(mesh):
    whole = P(("dp", "expert"), None)
    over_dp, by_dp, over_expert = P("dp"), P("dp", None), P("expert", None, None)
    return jax.shard_map(
        on_device,
        mesh=mesh,
        in_specs=(whole, whole, over_dp, by_dp, by_dp, by_dp, by_dp, over_dp, by_dp)
        + (over_expert,) * 3
        + (whole, by_dp),
        out_specs=(whole, whole, over_dp, by_dp, by_dp, by_dp, by_dp, over_dp, by_dp)
        + (over_expert,) * 3,
        check_vma=False,
    )
```

time: 387 us -> 425 us (1.098)
  waiting for transfers between devices: 0.06 us -> 48.5 us
  matrix products: 7.62 us -> 0 us
  other arithmetic: 16 us -> 10.4 us
  local copies, waits for them, and re-layouts: 18.9 us -> 23.9 us
    all_gather x1, waiting for transfers between devices: 0.02 us -> 48.5 us  [gather_dense(): got = lax.all_gather(mine, 'dp', axis=0, tiled=True)]
    dot_general x2 -> x0, matrix products: 7.62 us -> none  [dot(): return lax.dot_general(a, b, (dims, ((), ())), preferred_element_type=F32)]
    unnamed x65 -> x63, local copies, waits for them, and re-layouts: 13.5 us -> 20 us
    pallas_call x8, Pallas kernels: 322 us -> 318 us  [the longest x1 77.4 us: last(): pl.pallas_call(last_kernel, out_shape=[sds((rows, width), F32), sds((heig...]
  transfers between devices with their start and end apart: 3 -> 3, of which waited for: 0 -> 1; matrix products, arithmetic and copies ran while one was open for 7% -> 2% of each run, Pallas kernels for 58% -> 55%
where the time goes in v3:
time: 425 us; the launch traced here: 417 us
  Pallas kernels  318 us (75%)
  waiting for transfers between devices  48.5 us (11%)
  local copies, waits for them, and re-layouts  23.9 us (6%)
  between operations  14.6 us (3%)
  other arithmetic  10.4 us (2%)
    pallas_call x1, Pallas kernels, last(): pl.pallas_call(last_kernel, out_shape=[sds((rows, width), F32), sds((heig...  77.4 us
    pallas_call x1, Pallas kernels, experts(): pl.pallas_call(experts_kernel, out_shape=[sds((rows, width), F32), sds((E...  76.2 us
    pallas_call x1, Pallas kernels, attend_back(): pl.pallas_call(attend_back_kernel, out_shape=[sds((rows, width), BF16), s...  60 us
    all_gather x1, waiting for transfers between devices, gather_dense(): got = lax.all_gather(mine, 'dp', axis=0, tiled=True)  48.5 us
    pallas_call x1, Pallas kernels, gather_first(): pl.pallas_call(gather_first_kernel, out_shape=[sds((4, 4, height, total),...  35.7 us
    pallas_call x1, Pallas kernels, after(): pl.pallas_call(after_kernel, out_shape=[sds((rows, width), F32), sds((row...  22.6 us
    unnamed x63, local copies, waits for them, and re-layouts  20 us
    pallas_call x1, Pallas kernels, attend(): pl.pallas_call(attend_kernel, grid=(QUERY_HEADS,), out_shape=[sds((rows,...  18.4 us
  transfers between devices with their start and end apart: 3, of which 1 were waited for; matrix products, arithmetic and copies ran while one was open for 2% of the time, Pallas kernels for 55%

profile of v3, /device:TPU:1, one launch (start us, length us, event | category | flops | bytes accessed | tf_op | source)
XLA Modules:
  0.0 417.1 jit_solution(11948259529388128964)
XLA Ops:
  7.2 0.0 all-gather.2.cloned.1.call-start
  7.3 0.9 copy-done
  8.1 0.7 constant_dynamic-slice_fusion
  8.8 0.0 all-gather.2.cloned.1.call-update
  8.8 0.0 all-reduce.4.cloned.1.call-start
  8.9 0.7 pad.9.note_ref
  9.6 0.7 pad_maximum_fusion.3
  10.3 0.1 copy.44
  10.4 48.5 %all-gather.2.cloned.1.call-done = bf16[1536,768]{1,0:T(8,128)(2,1)} async-done(((bf16[96,768]{1,0:T(8,128)(2,1)}), bf16[1536,768]{1,0:T(8,128)(2,1)}) %all-gather.2.cloned.1.call-update) | async-done | bytes 2359312 | tf_op jit(solution)/shard_map/all_gather | solution.py:90
  58.9 1.6 collective-permute-start
  60.6 0.9 fusion
  61.5 0.7 convert_element_type.54.member_ref
  62.2 1.1 copy-done.8
  63.3 1.0 copy-done.14
  64.3 0.8 copy-done.16
  65.1 0.8 copy-done.17
  65.9 35.7 %shard_map.229 = (bf16[4,4,96,2048]{3,2,1,0:T(8,128)(2,1)S(1)}, bf16[4,4,96,128]{3,2,1,0:T(8,128)(2,1)S(1)}, bf16[8,256,1536]{2,1,0:T(8,128)(2,1)S(1)}, s32[8,8,256]{2,1,0:T(8,128)S(1)}) custom-call(bf16[96,1536]{1,0:T(8,128)(2,1)S(1)} %copy-done.14, bf16[96,256]{1,0:T(8,128)(2,1)S(1)} %copy-done.16, bf16[96,256]{1,0:T(8,128)(2,1)S(1)} %copy-done.17, ...), custom_call_target="tpu_custom_call" | custom-call | tf_op jit(solution)/shard_map/pallas_call | solution.py:450
  101.6 2.6 copy-done.2
  104.2 2.7 copy-done.6
  106.9 0.6 reduce-window.6
  107.5 0.2 slice_reduce_fusion.2
  107.8 0.1 add_add_fusion
  107.9 0.5 convert_reduce_fusion.1
  108.4 0.6 reshape.131.gain_ref
  109.1 0.4 convert_reduce_fusion
  109.4 0.5 fusion.1
  110.0 0.1 pad_maximum_fusion.1
  110.2 2.9 copy-done.3
  113.0 15.1 %shard_map.230 = (bf16[256,1536]{1,0:T(8,128)(2,1)S(1)}, bf16[256,1536]{1,0:T(8,128)(2,1)S(1)}, bf16[8,256,512]{2,1,0:T(8,128)(2,1)S(1)}) custom-call(bf16[256,1536]{1,0:T(8,128)(2,1)S(1)} %copy-done.4, bf16[1536,2048]{1,0:T(8,128)(2,1)S(1)} %bitcast.24, f32[1,1536]{1,0:T(1,128)S(1)} %reshape.130.gain_ref, f32[256,128]{1,0:T(8,128)S(1)} %get-tuple-element.133.cos_ref, ...), custom_call_target="tpu_custom_call" | custom-call | tf_op jit(solution)/shard_map/pallas_call | solution.py:522
  128.2 0.7 copy_select_fusion.slot_ref
  128.9 18.4 %shard_map.231 = (bf16[256,1536]{1,0:T(8,128)(2,1)S(1)}, f32[12,1,256]{2,1,0:T(1,128)S(1)}) custom-call(s32[1,256]{1,0:T(1,128)S(1)} %bitcast.30, bf16[256,1536]{1,0:T(8,128)(2,1)S(1)} %get-tuple-element.46.q_ref, bf16[2048,512]{1,0:T(8,128)(2,1)S(1)} %bitcast.28), custom_call_target="tpu_custom_call" | custom-call | flops 3221225472 | bytes 12582912 | tf_op jit(solution)/shard_map/pallas_call | solution.py:579
  147.4 2.5 broadcast_select_fusion.1
  149.9 2.6 pad_maximum_fusion.wo_hbm.wo_ref
  152.5 76.2 %shard_map.232 = (f32[256,1536]{1,0:T(8,128)}, f32[8,256]{1,0:T(8,128)}, f32[8,8,256]{2,1,0:T(8,128)}, bf16[2,128,1536]{2,1,0:T(8,128)(2,1)}, f32[256,1536]{1,0:...) custom-call(bf16[256,1536]{1,0:T(8,128)(2,1)} %copy-done.7, bf16[256,1536]{1,0:T(8,128)(2,1)} %tokens_ref.5, ...), custom_call_target="tpu_custom_call" | custom-call | tf_op jit(solution)/shard_map/pallas_call | solution.py:800
  228.7 0.0 all-reduce.4.cloned.1.call-update
  228.7 22.6 %shard_map.233 = (f32[256,1536]{1,0:T(8,128)}, bf16[256,1536]{1,0:T(8,128)(2,1)}, bf16[1536,128]{1,0:T(8,128)(2,1)}, bf16[1536,1536]{1,0:T(8,128)(2,1)}) custom-call(f32[256,1536]{1,0:T(8,128)} %get-tuple-element.51.middle_ref, f32[8,256]{1,0:T(8,128)} %get-tuple-element.52.gates_ref, f32[8,8,256]{2,1,0:T(8,128)} %get-tuple-element.53.gg_all, ...), custom_call_target="tpu_custom_call" | custom-call | tf_op jit(solution)/shard_map/pallas_call | solution.py:889
  251.3 60.0 %shard_map.234 = (bf16[256,1536]{1,0:T(8,128)(2,1)}, bf16[2048,512]{1,0:T(8,128)(2,1)}, f32[96,1536]{1,0:T(8,128)}, bf16[256,1536]{1,0:T(8,128)(2,1)}) custom-call(s32[1,256]{1,0:T(1,128)} %bitcast.31, bf16[256,1536]{1,0:T(8,128)(2,1)} %copy-done.12, bf16[2048,512]{1,0:T(8,128)(2,1)} %bitcast.29, bf16[256,1536]{1,0:T(8,128)(2,1)} %get-tuple-element.56.g_ref, ...), custom_call_target="tpu_custom_call" | custom-call | tf_op jit(solution)/shard_map/pallas_call | solution.py:997
  311.4 77.4 %shard_map.235 = (f32[256,1536]{1,0:T(8,128)}, f32[96,1536]{1,0:T(8,128)}, f32[96,256]{1,0:T(8,128)}, f32[96,256]{1,0:T(8,128)}, f32[96,128]{1,0:T(8,128)}) custom-call(bf16[8,256,512]{2,1,0:T(8,128)(2,1)} %bitcast.37, bf16[256,1536]{1,0:T(8,128)(2,1)} %get-tuple-element.62.gq_ref, bf16[256,1536]{1,0:T(8,128)(2,1)} %copy-done.13, ...), custom_call_target="tpu_custom_call" | custom-call | tf_op jit(solution)/shard_map/pallas_call | solution.py:1122
  388.8 1.5 copy.47
  390.2 1.6 slice_reduce_fusion
  391.8 12.5 %shard_map.236 = (f32[1536,768]{1,0:T(8,128)}, f32[1536,768]{1,0:T(8,128)}, f32[768,1536]{1,0:T(8,128)}) custom-call(f32[96,128]{1,0:T(8,128)} %get-tuple-element.67.late_ref, bf16[16,144,1536]{2,1,0:T(8,128)(2,1)} %all-reduce.4.cloned.1.call-done.sums_ref), custom_call_target="tpu_custom_call" | custom-call | bytes 22020096 | tf_op jit(solution)/shard_map/pallas_call | solution.py:1165
  404.3 0.9 copy.56
  405.2 0.8 copy-done.21
  406.0 1.1 copy.57
  407.1 0.8 copy.58
  407.9 0.6 copy.59
  408.6 0.6 copy.60
  409.2 0.8 copy.61
  (59 shorter events, 0.3 us)
Async XLA Ops:
  7.2 1.0 copy-start
  7.2 101.8 %copy-start.27 = (s32[1,2048]{1,0:T(1,128)S(1)}, s32[1,2048]{1,0:T(1,128)}, u32[]{:S(2)}) copy-start(s32[1,2048]{1,0:T(1,128)} %param.27) | copy-start | bytes 24580
  7.2 102.9 %copy-start.4 = (bf16[256,1536]{1,0:T(8,128)(2,1)S(1)}, bf16[256,1536]{1,0:T(8,128)(2,1)}, u32[]{:S(2)}) copy-start(bf16[256,1536]{1,0:T(8,128)(2,1)} %tokens_ref.5) | copy-start | bytes 2359300
  7.2 51.7 %all-gather.2.cloned.1.call-start = ((), (), s32[]{:S(2)}) async-start(), calls=%async_computation | async-start | bytes 2506752 | tf_op jit(solution)/shard_map/all_gather | solution.py:90
  8.8 383.0 %all-reduce.4.cloned.1.call-start = ((), (), s32[]{:S(2)}) async-start(), calls=%async_computation.1 | async-start | bytes 14155776 | tf_op jit(solution)/shard_map/psum | solution.py:1229
  58.9 88.4 %collective-permute-start = (bf16[1536,768]{1,0:T(8,128)(2,1)}, bf16[1536,768]{1,0:T(8,128)(2,1)}, u32[]{:S(2)}, u32[]{:S(2)}) collective-permute-start(bf16[1536,768]{1,0:T(8,128)(2,1)} %all-gather.2.cloned.1.call-done), channel_id=1, source_target_pairs={{0,1},{1,0},{2,3},{3,2},{4,5},{5,4},{6,7},{7,6},{8,9},{9,8},{10,11... | collective-permute-start | bytes 7077896 | tf_op jit(solution)/shard_map/ppermute | solution.py:91
  62.2 1.1 copy-start.8
  63.3 1.0 copy-start.14
  64.3 0.8 copy-start.16
  65.1 0.8 copy-start.17
  101.6 2.6 copy-start.2
  104.2 2.7 copy-start.6
  106.9 21.2 %copy-start.5 = (bf16[4,4,96,128]{3,2,1,0:T(8,128)(2,1)}, bf16[4,4,96,128]{3,2,1,0:T(8,128)(2,1)S(1)}, u32[]{:S(2)}) copy-start(bf16[4,4,96,128]{3,2,1,0:T(8,128)(2,1)S(1)} %get-tuple-element.45) | copy-start | bytes 1179652
  109.0 19.1 %copy-start.15 = (f32[1,1536]{1,0:T(1,128)}, f32[1,1536]{1,0:T(1,128)S(1)}, u32[]{:S(2)}) copy-start(f32[1,1536]{1,0:T(1,128)S(1)} %reshape.130.gain_ref) | copy-start | bytes 18436
  109.4 19.5 %copy-start.19 = (s32[256]{0:T(256)}, s32[256]{0:T(256)S(1)}, u32[]{:S(2)}) copy-start(s32[256]{0:T(256)S(1)} %convert_reduce_fusion) | copy-start | bytes 3076
  110.1 18.0 %copy-start.9 = (f32[256,128]{1,0:T(8,128)}, f32[256,128]{1,0:T(8,128)S(1)}, u32[]{:S(2)}) copy-start(f32[256,128]{1,0:T(8,128)S(1)} %get-tuple-element.133.cos_ref) | copy-start | bytes 393220
  110.1 18.0 %copy-start.10 = (f32[256,128]{1,0:T(8,128)}, f32[256,128]{1,0:T(8,128)S(1)}, u32[]{:S(2)}) copy-start(f32[256,128]{1,0:T(8,128)S(1)} %get-tuple-element.134.sin_ref) | copy-start | bytes 393220
  110.2 2.9 copy-start.3
  128.1 19.2 %copy-start.11 = (bf16[8,256,512]{2,1,0:T(8,128)(2,1)}, bf16[8,256,512]{2,1,0:T(8,128)(2,1)S(1)}, u32[]{:S(2)}) copy-start(bf16[8,256,512]{2,1,0:T(8,128)(2,1)S(1)} %get-tuple-element.47) | copy-start | bytes 6291460
  128.2 19.2 %copy-start.12 = (bf16[256,1536]{1,0:T(8,128)(2,1)}, bf16[256,1536]{1,0:T(8,128)(2,1)S(1)}, u32[]{:S(2)}) copy-start(bf16[256,1536]{1,0:T(8,128)(2,1)S(1)} %get-tuple-element.46.q_ref) | copy-start | bytes 2359300
  128.2 19.2 %copy-start.13 = (bf16[256,1536]{1,0:T(8,128)(2,1)}, bf16[256,1536]{1,0:T(8,128)(2,1)S(1)}, u32[]{:S(2)}) copy-start(bf16[256,1536]{1,0:T(8,128)(2,1)S(1)} %get-tuple-element.63.normed_ref) | copy-start | bytes 2359300
  128.9 18.5 %copy-start.20 = (bf16[1536,768]{1,0:T(8,128)(2,1)S(1)}, bf16[1536,768]{1,0:T(8,128)(2,1)}, u32[]{:S(2)}) copy-start(bf16[1536,768]{1,0:T(8,128)(2,1)} %all-gather.2.cloned.1.call-done) | copy-start | bytes 7077892
  147.3 2.6 copy-start.7
  147.4 2.6 copy-start.18
  391.8 12.5 %copy-start.22 = (bf16[256,1536]{1,0:T(8,128)(2,1)S(1)}, bf16[256,1536]{1,0:T(8,128)(2,1)}, u32[]{:S(2)}) copy-start(bf16[256,1536]{1,0:T(8,128)(2,1)} %get-tuple-element.147) | copy-start | bytes 2359300
  404.3 1.7 copy-start.21
  404.3 2.8 copy-start.24
  404.3 5.8 %copy-start.1 = (bf16[96,1536]{1,0:T(8,128)(2,1)S(1)}, bf16[96,1536]{1,0:T(8,128)(2,1)}, u32[]{:S(2)}) copy-start(bf16[96,1536]{1,0:T(8,128)(2,1)} %param.20) | copy-start | bytes 884740
  406.0 2.0 copy-start.26
  406.0 2.6 copy-start.25
  406.0 3.3 copy-start.23
Sparse Core Ops, SparseCore 0:
  10.8 48.0 all-gather.1
  228.8 151.8 all-reduce.3
